TPU v7x, 32 devices: a whole 2x2x4 slice. The times are simulated.
32 devices in a mesh: cam: 4 (over y, x), tile: 8 (over z, core).
Axes of the slice: x: 2, y: 2, z: 4, core: 2. Of those that a mesh axis runs over, the one named last changes fastest.
Arguments:
- positions: float32 [3, 32768], P(None, ('cam', 'tile')), may hold values from -1 to 1
- log_scales: float32 [3, 32768], P(None, ('cam', 'tile')), may hold values from -4.5 to -2.5
- rotations: float32 [4, 32768], P(None, ('cam', 'tile')), may hold values from 0.3 to 1
- opacities: float32 [32768], P(('cam', 'tile')), may hold values from -6 to -3
- colors: float32 [48, 32768], P(None, ('cam', 'tile')), may hold values from -3 to 3
- cameras: float32 [2, 4, 6], replicated, may hold values from -0.05 to 0.05
- targets: float32 [2, 4, 8, 3, 256], P(None, 'cam', 'tile'), may hold values from 0 to 1
- tile_ids: int32 [2, 4, 8], P(None, 'cam', 'tile'), may hold values from 15488 to 17280, as said below
- tile_counts: int32 [2, 4, 8], P(None, 'cam', 'tile'), may hold values from 128 to 256, as said below
- tile_lists: int32 [2, 4, 8, 256], P(None, 'cam', 'tile'), may hold values from 0 to 1023, as said below
- fetch_ids: int32 [2, 4, 8, 4, 8, 32], P(None, 'cam', 'tile'), may hold values from 0 to 1023, as said below
Outputs:
- grad_positions: float32 [3, 32768], P(None, ('cam', 'tile'))
- grad_log_scales: float32 [3, 32768], P(None, ('cam', 'tile'))
- grad_rotations: float32 [4, 32768], P(None, ('cam', 'tile'))
- grad_opacities: float32 [32768], P(('cam', 'tile'))
- grad_colors: float32 [48, 32768], P(None, ('cam', 'tile'))
Inputs may be any that keep to these rules, and one draw needn't show every extreme that they name: Within one row fetch_ids[p, c, t, a, b, :] the entries are distinct local columns of the owner at cam a, tile b, all within the block of 1024 // 8 columns that belongs to the device's row of tiles; not every slot is named by a list. `tile_lists`: entries are slots of the rendering device, distinct within a tile, in increasing order of the third coordinate of their Gaussians' positions. `tile_counts`: each device has a tile with 256 live entries in each pass. `tile_ids`: each device renders one image tile in a pass; in each pass and camera group the devices' rows are distinct and together form a window of 8 rows.
All inputs are finite; a program needn't handle non-finite values.
Results may differ from a plain program's by a relative error of at most 0.0003.
Values sent between devices are 32-bit elements; how exact they have to be, the bound alone decides.
No kernel may reach another device: no remote copies, remote signals or barrier semaphores. Data moves between devices by JAX's collectives and lax.ppermute only.
A program may use at most 192 MiB of HBM per device.

v0:
```python
import functools

import jax
import jax.numpy as jnp
from jax import lax
from jax.experimental import pallas as pl
from jax.experimental.pallas import tpu as pltpu
from jax.sharding import PartitionSpec as P

FOCAL = 4096.0
CENTER_X = 2048.0
CENTER_Y = 1024.0
SH_ZERO = 0.28209479177387814
SH_ONE = 0.4886025119029199
SH_TWO = [
    1.0925484305920792,
    -1.0925484305920792,
    0.31539156525252005,
    -1.0925484305920792,
    0.5462742152960396,
]
SH_THREE = [
    -0.5900435899266435,
    2.890611442640554,
    -0.4570457994644658,
    0.3731763325901154,
    -0.4570457994644658,
    1.445305721320277,
    -0.5900435899266435,
]
LANES = 128
HALF = LANES // 2
FIELDS = 9
SENT = 8
RAW = 59
TERMS = 15
F32 = jnp.float32
BF16 = jnp.bfloat16


def dot(left, right, contract):
    return lax.dot_general(left, right, ((contract[0], contract[1]), ((), ())), preferred_element_type=F32)


def split(x):
    high = x.astype(BF16)
    return high, (x - high.astype(F32)).astype(BF16)


def lane_pick(source, index):
    return jnp.take_along_axis(source, index, axis=1, mode="promise_in_bounds")


def row_pick(source, index):
    return jnp.take_along_axis(source, index, axis=0, mode="promise_in_bounds")


def spin_of(quat):
    norm = jnp.sqrt(quat[0] * quat[0] + quat[1] * quat[1] + quat[2] * quat[2] + quat[3] * quat[3])
    back = 1.0 / norm
    w, x, y, z = [q * back for q in quat]
    spin = [
        [1.0 - 2.0 * (y * y + z * z), 2.0 * (x * y - w * z), 2.0 * (x * z + w * y)],
        [2.0 * (x * y + w * z), 1.0 - 2.0 * (x * x + z * z), 2.0 * (y * z - w * x)],
        [2.0 * (x * z - w * y), 2.0 * (y * z + w * x), 1.0 - 2.0 * (x * x + y * y)],
    ]
    return spin, (w, x, y, z), back


def world_cov(spin, squares):
    scaled = [[spin[i][k] * squares[k] for k in range(3)] for i in range(3)]
    cov = [[None] * 3 for _ in range(3)]
    for i in range(3):
        for j in range(i, 3):
            cov[i][j] = scaled[i][0] * spin[j][0] + scaled[i][1] * spin[j][1] + scaled[i][2] * spin[j][2]
            cov[j][i] = cov[i][j]
    return cov


def dot3(a, b):
    return a[0] * b[0] + a[1] * b[1] + a[2] * b[2]


def screen_of(point, cov, rotate, offset):
    m = [dot3(rotate[i], point) + offset[i] for i in range(3)]
    inverse = 1.0 / m[2]
    main = FOCAL * inverse
    at_x, at_y = m[0] * inverse, m[1] * inverse
    side_x, side_y = -main * at_x, -main * at_y
    t_x = [main * rotate[0][i] + side_x * rotate[2][i] for i in range(3)]
    t_y = [main * rotate[1][i] + side_y * rotate[2][i] for i in range(3)]
    w_x = [dot3(cov[i], t_x) for i in range(3)]
    w_y = [dot3(cov[i], t_y) for i in range(3)]
    s_xx = dot3(t_x, w_x) + 0.3
    s_xy = dot3(t_y, w_x)
    s_yy = dot3(t_y, w_y) + 0.3
    back = 1.0 / (s_xx * s_yy - s_xy * s_xy)
    conic = (s_yy * back, -s_xy * back, s_xx * back)
    return m, inverse, main, at_x, at_y, t_x, t_y, w_x, w_y, conic


def direction_of(point, center):
    toward = [point[j] - center[j] for j in range(3)]
    back = lax.rsqrt(dot3(toward, toward))
    return [t * back for t in toward], back


def basis_of(x, y, z):
    xx, yy, zz = x * x, y * y, z * z
    xy, yz, xz = x * y, y * z, x * z
    less = xx - yy
    four = 4.0 * zz - xx - yy
    return [
        None,
        -SH_ONE * y,
        SH_ONE * z,
        -SH_ONE * x,
        SH_TWO[0] * xy,
        SH_TWO[1] * yz,
        SH_TWO[2] * (2.0 * zz - xx - yy),
        SH_TWO[3] * xz,
        SH_TWO[4] * less,
        SH_THREE[0] * y * (3.0 * xx - yy),
        SH_THREE[1] * xy * z,
        SH_THREE[2] * y * four,
        SH_THREE[3] * z * (2.0 * zz - 3.0 * xx - 3.0 * yy),
        SH_THREE[4] * x * four,
        SH_THREE[5] * z * less,
        SH_THREE[6] * x * (xx - 3.0 * yy),
    ]


def basis_pull(x, y, z, g):
    xx, yy, zz = x * x, y * y, z * z
    xy, yz, xz = x * y, y * z, x * z
    less = xx - yy
    four = 4.0 * zz - xx - yy
    g4, g5, g6, g7, g8 = [SH_TWO[i] * g[4 + i] for i in range(5)]
    h = [SH_THREE[i] * g[9 + i] for i in range(7)]
    g_x = (
        -SH_ONE * g[3] + g4 * y - 2.0 * g6 * x + g7 * z + 2.0 * g8 * x
        + 6.0 * h[0] * xy + h[1] * yz - 2.0 * h[2] * xy - 6.0 * h[3] * xz
        + h[4] * (four - 2.0 * xx) + 2.0 * h[5] * xz + 3.0 * h[6] * less
    )
    g_y = (
        -SH_ONE * g[1] + g4 * x + g5 * z - 2.0 * g6 * y - 2.0 * g8 * y
        + 3.0 * h[0] * less + h[1] * xz + h[2] * (four - 2.0 * yy) - 6.0 * h[3] * yz
        - 2.0 * h[4] * xy - 2.0 * h[5] * yz - 6.0 * h[6] * xy
    )
    g_z = (
        SH_ONE * g[2] + g5 * y + 4.0 * g6 * z + g7 * x
        + h[1] * xy + 8.0 * h[2] * yz + h[3] * (6.0 * zz - 3.0 * xx - 3.0 * yy)
        + 8.0 * h[4] * xz + h[5] * less
    )
    return [g_x, g_y, g_z]


def camera_rows(cam_ref, table, passes, cams):
    views = passes * cams
    for p in range(passes):
        cam = cam_ref[p]
        cos, sin = jnp.cos(cam), jnp.sin(cam)
        ca, cb, cg = [cos[:, k : k + 1] for k in range(3)]
        sa, sb, sg = [sin[:, k : k + 1] for k in range(3)]
        rotate = [
            [cg * cb, cg * sb * sa - sg * ca, cg * sb * ca + sg * sa],
            [sg * cb, sg * sb * sa + cg * ca, sg * sb * ca - cg * sa],
            [-sb, cb * sa, cb * ca],
        ]
        offset = [cam[:, 3:4], cam[:, 4:5], 6.0 + cam[:, 5:6]]
        center = [-(rotate[0][j] * offset[0] + rotate[1][j] * offset[1] + rotate[2][j] * offset[2]) for j in range(3)]
        for k, term in enumerate(rotate[0] + rotate[1] + rotate[2] + offset + center):
            table[k * views + p * cams : k * views + (p + 1) * cams, :] = jnp.broadcast_to(term, (cams, LANES))


def camera_of(table, view, views, shape):
    terms = [jnp.broadcast_to(table[k * views + view : k * views + view + 1, :], shape) for k in range(TERMS)]
    return [terms[0:3], terms[3:6], terms[6:9]], terms[9:12], terms[12:15]


def project_kernel(passes, cams, rows, pos, scales, rots, opac, cols, cam, rec, raw, table):
    views = passes * cams
    shape = (rows, LANES)
    camera_rows(cam, table, passes, cams)
    base = 0
    for ref in (pos, scales, rots):
        count = ref.shape[0]
        for i in range(rows):
            raw[pl.ds(base * rows + i, count, stride=rows), :] = ref[:, i * LANES : (i + 1) * LANES]
        base += count
    raw[base * rows : (base + 1) * rows, :] = opac[...]
    base += 1
    for i in range(rows):
        raw[pl.ds(base * rows + i, cols.shape[0], stride=rows), :] = cols[:, i * LANES : (i + 1) * LANES]

    def at(k):
        return raw[k * rows : (k + 1) * rows, :]

    point = [at(k) for k in range(3)]
    squares = [jnp.exp(2.0 * at(3 + k)) for k in range(3)]
    spin, _, _ = spin_of([at(6 + k) for k in range(4)])
    cov = world_cov(spin, squares)
    opacity = 1.0 / (1.0 + jnp.exp(-at(10)))
    for view in range(views):
        rotate, offset, center = camera_of(table, view, views, shape)
        _, _, _, at_x, at_y, _, _, _, _, conic = screen_of(point, cov, rotate, offset)
        direction, _ = direction_of(point, center)
        basis = basis_of(*direction)
        fields = [FOCAL * at_x + CENTER_X, FOCAL * at_y + CENTER_Y, conic[0], conic[1], conic[2], opacity]
        for channel in range(3):
            total = 0.5 + SH_ZERO * at(11 + channel)
            for k in range(1, 16):
                total = total + basis[k] * at(11 + 3 * k + channel)
            fields.append(total)
        for f, value in enumerate(fields):
            rec[(view * FIELDS + f) * rows : (view * FIELDS + f + 1) * rows, :] = value


def lane_pass(shape, cap):
    lane = lax.broadcasted_iota(jnp.int32, shape, 1) % HALF
    return lane // cap, lane % cap


def pick_kernel(passes, cams, tiles, rows, cap, aligned, ids, rec, out):
    group = 8
    shape = (group, LANES)
    lane = lax.broadcasted_iota(jnp.int32, shape, 1)
    lane_p, _ = lane_pass(shape, cap)

    def packets(first, c):
        asked = ids[pl.ds(first, group), :]
        low, high = asked % LANES, asked // LANES
        if aligned:
            blocks = [
                jnp.broadcast_to(high[:, p * cap : p * cap + 1], shape) for p in range(passes)
            ]

        def pick(f):
            found = jnp.zeros(shape, F32)
            for p in range(passes):
                start = ((p * cams + c) * FIELDS + f) * rows
                if aligned:
                    own = lane_pick(row_pick(rec[start : start + rows, :], blocks[p]), low)
                else:
                    own = jnp.zeros(shape, F32)
                    for b in range(rows):
                        line = jnp.broadcast_to(rec[start + b : start + b + 1, :], shape)
                        own = jnp.where(high == b, lane_pick(line, low), own)
                found = jnp.where(lane_p == p, own, found)
            return found

        for f in range(SENT):
            value = pick(f)
            if f == 0:
                value = jnp.where(lane < HALF, value, pick(FIELDS - 1))
            out[pl.ds(first * SENT + f, group, stride=SENT), :] = value

    for c in range(cams):
        if tiles == group:
            packets(c * tiles, c)
        else:

            def step(k, carry, c=c):
                packets(pl.multiple_of(c * tiles + k * group, group), c)
                return carry

            lax.fori_loop(0, tiles // group, step, 0)


def inverse_kernel(passes, cams, tiles, rows, cap, ids, inverse):
    shape = (LANES, LANES)
    column = lax.broadcasted_iota(jnp.int32, shape, 0)
    _, lane_j = lane_pass(shape, cap)
    place = (lane_j + 1).astype(F32)
    wide = (passes * rows, LANES)
    lane_p, _ = lane_pass(wide, cap)
    lane = lax.broadcasted_iota(jnp.int32, wide, 1)
    key = lax.broadcasted_iota(jnp.int32, wide, 0)
    lane_key = jnp.where(lane < passes * cap, lane_p * rows, -(1 << 20))

    def one(c, t, found):
        asked = ids[pl.ds(c * tiles + t, 1), :]
        low = jnp.broadcast_to(asked % LANES, shape)
        high = jnp.broadcast_to(asked // LANES, wide)
        match = jnp.where(low == column, place, 0.0).astype(BF16)
        owner = jnp.where(high + lane_key == key, 1.0, 0.0).astype(BF16)
        hit = dot(owner, match, ((1,), (1,)))
        return jnp.where(hit > 0.5, hit.astype(jnp.int32) + t * cap, found)

    for c in range(cams):
        found = jnp.zeros(wide, jnp.int32)
        if tiles <= 8:
            for t in range(tiles):
                found = one(c, t, found)
        else:
            found = lax.fori_loop(0, tiles, lambda t, f, c=c: one(c, t, f), found)
        for p in range(passes):
            start = (p * cams + c) * rows
            inverse[start : start + rows, :] = found[p * rows : (p + 1) * rows, :]


def render_kernel(passes, owners, cap, entries, pixels, got, lists, counts, places, wanted, out, alphas, logs, weights):
    halves = entries // LANES
    shape = (SENT, LANES)
    wide = 16
    lane = lax.broadcasted_iota(jnp.int32, shape, 1)
    sub = lax.broadcasted_iota(jnp.int32, shape, 0)

    slot_owner, slot_lane = [], []
    for p in range(passes):
        for h in range(halves):
            slot = jnp.broadcast_to(lists[p, 0, :, h * LANES : (h + 1) * LANES], shape)
            slot_owner.append(slot // cap)
            slot_lane.append(slot % cap + p * cap)
    total = passes * halves

    def gather(o, found):
        packet = got[pl.ds(pl.multiple_of(o * SENT, SENT), SENT), :]
        return tuple(
            jnp.where(slot_owner[i] == o, lane_pick(packet, slot_lane[i]), found[i]) for i in range(total)
        )

    def gather_last(g, found):
        lines = got[pl.ds(g * SENT * SENT, SENT, stride=SENT), :]
        return tuple(
            jnp.where(slot_owner[i] == g * SENT + sub, lane_pick(lines, slot_lane[i] + HALF), found[i])
            for i in range(total)
        )

    empty = tuple(jnp.zeros(shape, F32) for _ in range(total))
    if owners <= 32:
        fields, last = empty, empty
        for o in range(owners):
            fields = gather(o, fields)
        for g in range(owners // SENT):
            last = gather_last(g, last)
    else:
        fields = lax.fori_loop(0, owners, gather, empty)
        last = lax.fori_loop(0, owners // SENT, gather_last, empty)
    last = [jnp.sum(x, axis=0, keepdims=True) for x in last]

    pair = (LANES, LANES)
    lane_p, lane_j = lane_pass(pair, cap)
    turned_p, turned_j = lax.broadcasted_iota(jnp.int32, pair, 0) % HALF // cap, lax.broadcasted_iota(jnp.int32, pair, 0) % cap
    entry = (lax.broadcasted_iota(jnp.int32, pair, 1) + 1).astype(F32)
    owner_row = lax.broadcasted_iota(jnp.int32, (owners, LANES), 0)
    source = jnp.zeros((owners, LANES), jnp.int32)
    for p in range(passes):
        for h in range(halves):
            i = p * halves + h
            slot = lists[p, 0, :, h * LANES : (h + 1) * LANES]
            mine = jnp.where(jnp.broadcast_to(slot // cap, (owners, LANES)) == owner_row, 1.0, 0.0).astype(BF16)
            here = jnp.where(
                (jnp.broadcast_to(slot % cap, pair) == turned_j) & (turned_p == p), entry, 0.0
            ).astype(BF16)
            hit = dot(mine, here, ((1,), (1,)))
            source = jnp.where(hit > 0.5, hit.astype(jnp.int32) + h * LANES, source)

    before = jnp.where(
        lax.broadcasted_iota(jnp.int32, (entries, entries), 0) < lax.broadcasted_iota(jnp.int32, (entries, entries), 1),
        1.0,
        0.0,
    ).astype(BF16)
    after = jnp.where(
        lax.broadcasted_iota(jnp.int32, (entries, entries), 0) > lax.broadcasted_iota(jnp.int32, (entries, entries), 1),
        1.0,
        0.0,
    ).astype(BF16)
    entry_row = lax.broadcasted_iota(jnp.int32, (1, entries), 1)
    pixel = lax.broadcasted_iota(jnp.int32, (SENT, pixels), 1)
    local_x = (pixel % wide).astype(F32) - 7.5
    local_y = (pixel // wide).astype(F32) - 7.5
    kind = lax.broadcasted_iota(jnp.int32, (SENT, pixels), 0)
    moment = jnp.where(
        kind == 0,
        1.0,
        jnp.where(
            kind == 1,
            local_x,
            jnp.where(
                kind == 2,
                local_y,
                jnp.where(kind == 3, local_x * local_x, jnp.where(kind == 4, local_x * local_y, local_y * local_y)),
            ),
        ),
    ).astype(BF16)
    column_x = lax.broadcasted_iota(jnp.int32, (wide, entries), 0).astype(F32) - 7.5

    grads = []
    for p in range(passes):
        line = [
            jnp.concatenate([fields[p * halves + h][f : f + 1, :] for h in range(halves)], axis=1) for f in range(SENT)
        ]
        blue = jnp.concatenate([last[p * halves + h] for h in range(halves)], axis=1)
        place = places[p, 0, 0]
        u = line[0] - (place % 256 * 16 + 8).astype(F32)
        v = line[1] - (place // 256 * 16 + 8).astype(F32)
        c_a, c_b, c_c, base = line[2], line[3], line[4], line[5]
        color = jnp.concatenate([line[6], line[7], blue], axis=0)
        live = jnp.where(entry_row < counts[p, 0, 0], base, 0.0)

        d_x = column_x - u
        q_xx = (-0.5 * c_a) * d_x * d_x
        q_x = c_b * d_x
        for y in range(pixels // wide):
            d_y = (y - 7.5) - v
            power = q_xx - (q_x * d_y + 0.5 * c_c * d_y * d_y)
            alpha = live * jnp.exp(power)
            alphas[p, y * wide : (y + 1) * wide, :] = alpha
            logs[y * wide : (y + 1) * wide, :] = jnp.log(1.0 - alpha)
        high, low = split(logs[...])
        through = jnp.exp(dot(high, before, ((1,), (0,))) + dot(low, before, ((1,), (0,))))
        alpha = alphas[p]
        weight = alpha * through
        weights[p] = weight
        w_high, w_low = split(weight)
        c_high, c_low = split(color)
        shown = (
            dot(c_high, w_high, ((1,), (1,))) + dot(c_low, w_high, ((1,), (1,))) + dot(c_high, w_low, ((1,), (1,)))
        )
        residual = shown - wanted[p, 0, 0]
        r_high, r_low = split(residual)
        left = jnp.concatenate([r_high, r_high, r_low], axis=0)
        right = jnp.concatenate([c_high, c_low, c_high], axis=0)
        slope = dot(left, right, ((0,), (0,)))
        pulled = weight * slope
        high, low = split(pulled)
        rest = dot(high, after, ((1,), (0,))) + dot(low, after, ((1,), (0,)))
        power_grad = pulled - alpha / (1.0 - alpha) * rest
        high, low = split(power_grad)
        moments = dot(moment, high, ((1,), (0,))) + dot(moment, low, ((1,), (0,)))
        color_grad = (
            dot(r_high, w_high, ((1,), (0,))) + dot(r_low, w_high, ((1,), (0,))) + dot(r_high, w_low, ((1,), (0,)))
        )
        m_1, m_x, m_y, m_xx, m_xy, m_yy = [moments[k : k + 1, :] for k in range(6)]
        s_x = m_x - u * m_1
        s_y = m_y - v * m_1
        s_xx = m_xx - u * (m_x + s_x)
        s_yy = m_yy - v * (m_y + s_y)
        s_xy = m_xy - u * m_y - v * s_x
        grads.append(
            [
                c_a * s_x + c_b * s_y,
                c_b * s_x + c_c * s_y,
                -0.5 * s_xx,
                -s_xy,
                -0.5 * s_yy,
                m_1 / base,
                color_grad[0:1, :],
                color_grad[1:2, :],
                color_grad[2:3, :],
            ]
        )

    def packets(first, origin):
        origin = origin - 1
        which = jnp.where(origin < 0, -1, origin // LANES)
        index = jnp.maximum(origin, 0) % LANES
        own_p, _ = lane_pass(shape, cap)

        def pick(f):
            found = jnp.zeros(shape, F32)
            for p in range(passes):
                for h in range(halves):
                    line = jnp.broadcast_to(grads[p][f][:, h * LANES : (h + 1) * LANES], shape)
                    found = jnp.where((which == h) & (own_p == p), lane_pick(line, index), found)
            return found

        for f in range(SENT):
            value = pick(f)
            if f == 0:
                value = jnp.where(lane < HALF, value, pick(FIELDS - 1))
            out[pl.ds(first * SENT + f, SENT, stride=SENT), :] = value

    for g in range(owners // SENT):
        packets(g * SENT, source[g * SENT : (g + 1) * SENT, :])


def pull_kernel(passes, cams, tiles, rows, cap, aligned, got, inverse, raw, table, pos, scales, rots, opac, cols, total):
    views = passes * cams
    shape = (rows, LANES)

    def at(k):
        return raw[k * rows : (k + 1) * rows, :]

    point = [at(k) for k in range(3)]
    squares = [jnp.exp(2.0 * at(3 + k)) for k in range(3)]
    spin, quat, quat_back = spin_of([at(6 + k) for k in range(4)])
    cov = world_cov(spin, squares)

    g_point = [jnp.zeros(shape, F32) for _ in range(3)]
    g_cov = [[jnp.zeros(shape, F32) for _ in range(3)] for _ in range(3)]
    g_opacity = jnp.zeros(shape, F32)
    for view in range(views):
        p, c = view // cams, view % cams
        slot = inverse[view * rows : (view + 1) * rows, :] - 1
        valid = slot >= 0
        slot = jnp.maximum(slot, 0)
        slot_t, slot_lane = slot // cap, slot % cap + p * cap
        if aligned:
            row_t = jnp.broadcast_to(jnp.max(slot_t, axis=1, keepdims=True), shape)

        def fetch(f, row, shift):
            if aligned:
                lines = got[pl.ds(c * tiles * SENT + row, tiles, stride=SENT), :]
                return jnp.where(valid, lane_pick(row_pick(lines, row_t), slot_lane + shift), 0.0)

            def one(t, found):
                line = jnp.broadcast_to(got[pl.ds((c * tiles + t) * SENT + row, 1), :], shape)
                return jnp.where(valid & (slot_t == t), lane_pick(line, slot_lane + shift), found)

            return lax.fori_loop(0, tiles, one, jnp.zeros(shape, F32))

        g = [fetch(f, f, 0) for f in range(SENT)] + [fetch(FIELDS - 1, 0, HALF)]
        rotate, offset, center = camera_of(table, view, views, shape)
        m, inv, main, at_x, at_y, t_x, t_y, w_x, w_y, conic = screen_of(point, cov, rotate, offset)
        c_a, c_b, c_c = conic
        half = 0.5 * g[3]
        p00, p01 = g[2] * c_a + half * c_b, g[2] * c_b + half * c_c
        p10, p11 = half * c_a + g[4] * c_b, half * c_b + g[4] * c_c
        g_xx = -(c_a * p00 + c_b * p10)
        g_xy = -(c_a * p01 + c_b * p11)
        g_yy = -(c_b * p01 + c_c * p11)
        left = [g_xx * t_x[i] + g_xy * t_y[i] for i in range(3)]
        right = [g_yy * t_y[i] + g_xy * t_x[i] for i in range(3)]
        for i in range(3):
            for j in range(i, 3):
                g_cov[i][j] = g_cov[i][j] + (t_x[i] * left[j] + t_y[i] * right[j])
        g_tx = [2.0 * (g_xx * w_x[i] + g_xy * w_y[i]) for i in range(3)]
        g_ty = [2.0 * (g_yy * w_y[i] + g_xy * w_x[i]) for i in range(3)]
        g_main = dot3(rotate[0], g_tx) + dot3(rotate[1], g_ty)
        g_sx, g_sy = dot3(rotate[2], g_tx), dot3(rotate[2], g_ty)
        g_m0 = main * (g[0] - inv * g_sx)
        g_m1 = main * (g[1] - inv * g_sy)
        g_m2 = -main * (
            at_x * g[0] + at_y * g[1] + inv * g_main - 2.0 * inv * (at_x * g_sx + at_y * g_sy)
        )
        direction, length_back = direction_of(point, center)
        basis = basis_of(*direction)
        g_basis = [None]
        for k in range(1, 16):
            g_basis.append(
                at(11 + 3 * k) * g[6] + at(12 + 3 * k) * g[7] + at(13 + 3 * k) * g[8]
            )
        g_dir = basis_pull(*direction, g_basis)
        along = dot3(direction, g_dir)
        for j in range(3):
            g_point[j] = g_point[j] + (
                rotate[0][j] * g_m0 + rotate[1][j] * g_m1 + rotate[2][j] * g_m2
                + (g_dir[j] - direction[j] * along) * length_back
            )
        g_opacity = g_opacity + g[5]
        for k in range(16):
            for channel in range(3):
                term = SH_ZERO * g[6 + channel] if k == 0 else basis[k] * g[6 + channel]
                start = (11 + 3 * k + channel) * rows
                if view == 0:
                    total[start : start + rows, :] = term
                else:
                    total[start : start + rows, :] += term
    for i in range(3):
        for j in range(i):
            g_cov[i][j] = g_cov[j][i]

    g_scales = []
    g_spin = [[None] * 3 for _ in range(3)]
    for k in range(3):
        column = [spin[j][k] for j in range(3)]
        turned = [dot3(g_cov[i], column) for i in range(3)]
        g_scales.append(2.0 * squares[k] * dot3(column, turned))
        for i in range(3):
            g_spin[i][k] = 2.0 * squares[k] * turned[i]
    w, x, y, z = quat
    d = g_spin
    g_quat = [
        2.0 * (z * (d[1][0] - d[0][1]) + y * (d[0][2] - d[2][0]) + x * (d[2][1] - d[1][2])),
        2.0 * (y * (d[0][1] + d[1][0]) + z * (d[0][2] + d[2][0]) + w * (d[2][1] - d[1][2]) - 2.0 * x * (d[1][1] + d[2][2])),
        2.0 * (x * (d[0][1] + d[1][0]) + z * (d[1][2] + d[2][1]) + w * (d[0][2] - d[2][0]) - 2.0 * y * (d[0][0] + d[2][2])),
        2.0 * (x * (d[0][2] + d[2][0]) + y * (d[1][2] + d[2][1]) + w * (d[1][0] - d[0][1]) - 2.0 * z * (d[0][0] + d[1][1])),
    ]
    along = w * g_quat[0] + x * g_quat[1] + y * g_quat[2] + z * g_quat[3]
    g_rots = [(g_quat[k] - quat[k] * along) * quat_back for k in range(4)]
    opacity = 1.0 / (1.0 + jnp.exp(-at(10)))
    opac[...] = g_opacity * opacity * (1.0 - opacity)
    for k, value in enumerate(g_point + g_scales + g_rots):
        total[k * rows : (k + 1) * rows, :] = value
    base = 0
    for ref in (pos, scales, rots, cols):
        count = ref.shape[0]
        if ref is cols:
            base = 11
        for i in range(rows):
            ref[:, i * LANES : (i + 1) * LANES] = total[pl.ds(base * rows + i, count, stride=rows), :]
        base += count


def vmem(count):
    return [pl.BlockSpec(memory_space=pltpu.VMEM)] * count


def call(kernel, outs, operands, in_specs=None, scratch=(), flops=1_000_000):
    return pl.pallas_call(
        kernel,
        out_shape=outs,
        in_specs=in_specs or vmem(len(operands)),
        out_specs=jax.tree.map(lambda _: pl.BlockSpec(memory_space=pltpu.VMEM), outs),
        scratch_shapes=list(scratch),
        compiler_params=pltpu.CompilerParams(vmem_limit_bytes=32 << 20),
        cost_estimate=pl.CostEstimate(flops=flops, bytes_accessed=1 << 20, transcendentals=0),
    )(*operands)


def body(
    cams,
    tiles,
    positions,
    log_scales,
    rotations,
    opacities,
    colors,
    cameras,
    targets,
    tile_ids,
    tile_counts,
    tile_lists,
    fetch_ids,
):
    axes = ("cam", "tile")
    passes, cap = fetch_ids.shape[0], fetch_ids.shape[-1]
    entries, pixels = tile_lists.shape[-1], targets.shape[-1]
    columns = positions.shape[-1]
    rows = columns // LANES
    owners = cams * tiles
    views = passes * cams
    aligned = tiles == rows == 8

    def shaped(*shape):
        return jax.ShapeDtypeStruct(shape, F32)

    def exchange(x):
        return lax.all_to_all(x, axes, split_axis=0, concat_axis=0, tiled=True)

    wanted_ids = jnp.transpose(fetch_ids[:, 0, 0], (1, 2, 0, 3)).reshape(owners, passes * cap)
    wanted_ids = jnp.pad(wanted_ids, ((0, 0), (0, HALF - passes * cap)))
    arrived = exchange(jnp.concatenate([wanted_ids, wanted_ids], axis=1))

    records, raw, table = call(
        functools.partial(project_kernel, passes, cams, rows),
        [shaped(views * FIELDS * rows, LANES), shaped(RAW * rows, LANES), shaped(TERMS * views, LANES)],
        [positions, log_scales, rotations, opacities.reshape(rows, LANES), colors, cameras],
    )
    packets = call(
        functools.partial(pick_kernel, passes, cams, tiles, rows, cap, aligned),
        shaped(owners * SENT, LANES),
        [arrived, records],
    )
    fetched = exchange(packets)
    inverse = call(
        functools.partial(inverse_kernel, passes, cams, tiles, rows, cap),
        jax.ShapeDtypeStruct((views * rows, LANES), jnp.int32),
        [arrived],
    )
    smem = pl.BlockSpec(memory_space=pltpu.SMEM)
    whole = vmem(1)[0]
    slot_grads = call(
        functools.partial(render_kernel, passes, owners, cap, entries, pixels),
        shaped(owners * SENT, LANES),
        [fetched, tile_lists, tile_counts, tile_ids, targets],
        in_specs=[whole, whole, smem, smem, whole],
        scratch=[
            pltpu.VMEM((passes, pixels, entries), F32),
            pltpu.VMEM((pixels, entries), F32),
            pltpu.VMEM((passes, pixels, entries), F32),
        ],
    )
    coming = exchange(slot_grads)
    g_pos, g_scales, g_rots, g_opac, g_cols = call(
        functools.partial(pull_kernel, passes, cams, tiles, rows, cap, aligned),
        [shaped(3, columns), shaped(3, columns), shaped(4, columns), shaped(rows, LANES), shaped(48, columns)],
        [coming, inverse, raw, table],
        scratch=[pltpu.VMEM((RAW * rows, LANES), F32)],
    )
    return (g_pos, g_scales, g_rots, g_opac.reshape(columns), g_cols)


def solution(mesh):
    return jax.shard_map(
        functools.partial(body, mesh.shape["cam"], mesh.shape["tile"]),
        mesh=mesh,
        in_specs=(
            P(None, ("cam", "tile")),
            P(None, ("cam", "tile")),
            P(None, ("cam", "tile")),
            P(("cam", "tile")),
            P(None, ("cam", "tile")),
            P(),
            P(None, "cam", "tile", None, None),
            P(None, "cam", "tile"),
            P(None, "cam", "tile"),
            P(None, "cam", "tile", None),
            P(None, "cam", "tile", None, None, None),
        ),
        out_specs=(
            P(None, ("cam", "tile")),
            P(None, ("cam", "tile")),
            P(None, ("cam", "tile")),
            P(("cam", "tile")),
            P(None, ("cam", "tile")),
        ),
        check_vma=False,
    )
```

profile of v0, /device:TPU:0, one launch (start us, length us, event | category | flops | bytes accessed | tf_op | source)
XLA Modules:
  0.0 44.5 jit_solution(6817185815549717799)
XLA Ops:
  0.6 0.8 %copy.20 = s32[4,8,2,32]{3,2,1,0:T(2,128)S(1)} copy(s32[4,8,2,32]{3,1,0,2:T(8,128)} %bitcast.16) | data formatting | bytes 16384 | tf_op jit(solution)/shard_map/transpose | solution.py:643
  1.4 0.1 reshape.25
  1.5 0.0 copy-start.3
  1.5 0.0 copy-start.4
  1.5 0.0 copy-start.5
  1.5 0.7 %pad_add_fusion = s32[32,128]{1,0:T(8,128)} fusion(s32[32,64]{1,0:T(8,128)S(1)} %reshape.25), kind=kLoop, calls=%fused_computation | loop fusion | flops 4096 | bytes 24576 | tf_op jit(solution)/shard_map/concatenate | solution.py:645
  2.2 0.0 copy-start.1
  2.2 0.0 copy-start.2
  2.2 7.3 %all-to-all-start = ((s32[32,1,128]{2,1,0:T(1,128)}), s32[32,1,128]{2,1,0:T(1,128)S(1)}, u32[]{:S(2)}, u32[]{:S(2)}) async-start(s32[32,1,128]{2,1,0:T(1,128)} %bitcast.2), calls=%async_computation | async-start | bytes 32768 | tf_op jit(solution)/shard_map/all_to_all | solution.py:641
  9.5 0.0 copy-done.3
  9.5 0.0 copy-done.4
  9.5 0.0 copy-done.5
  9.5 0.0 copy-done.1
  9.5 0.0 copy-done.2
  9.6 0.0 copy-start
  9.6 0.9 %copy-done = f32[48,1024]{1,0:T(8,128)S(1)} copy-done((f32[48,1024]{1,0:T(8,128)S(1)}, f32[48,1024]{1,0:T(8,128)}, u32[]{:S(2)}) %copy-start) | copy-done | bytes 196632
  10.5 0.6 %shard_map.146 = (f32[576,128]{1,0:T(8,128)S(1)}, f32[472,128]{1,0:T(8,128)S(1)}, f32[120,128]{1,0:T(8,128)S(1)}) custom-call(f32[3,1024]{1,0:T(4,128)S(1)} %copy-done.1, f32[3,1024]{1,0:T(4,128)S(1)} %copy-done.2, f32[4,1024]{1,0:T(4,128)S(1)} %copy-done.3, f32[8,128]{1,0:T(8,128)S(1)} %bitcast.15, f32[48,1024]{1,0:T(8,128)S(1)} %copy-done, ...), custom_call_target="tpu_custom_call" | custom-call | flops 1000000 | bytes 1048576 | tf_op jit(solution)/shard_map/pallas_call | solution.py:602
  11.0 5.5 %all-to-all-done = s32[32,1,128]{2,1,0:T(1,128)S(1)} async-done(((s32[32,1,128]{2,1,0:T(1,128)}), s32[32,1,128]{2,1,0:T(1,128)S(1)}, u32[]{:S(2)}, u32[]{:S(2)}) %all-to-all-start) | async-done | bytes 16416 | tf_op jit(solution)/shard_map/all_to_all | solution.py:641
  16.6 0.9 %shard_map.147 = f32[256,128]{1,0:T(8,128)} custom-call(s32[32,128]{1,0:T(8,128)S(1)} %bitcast.13, f32[576,128]{1,0:T(8,128)S(1)} %get-tuple-element.13.rec), custom_call_target="tpu_custom_call" | custom-call | flops 1000000 | bytes 1048576 | tf_op jit(solution)/shard_map/pallas_call | solution.py:602
  17.5 0.0 copy-start.7
  17.5 2.7 %all-to-all-start.1 = ((f32[32,8,128]{2,1,0:T(8,128)}), f32[32,8,128]{2,1,0:T(8,128)S(1)}, u32[]{:S(2)}, u32[]{:S(2)}) async-start(f32[32,8,128]{2,1,0:T(8,128)} %bitcast.5), calls=%async_computation.1 | async-start | bytes 262144 | tf_op jit(solution)/shard_map/all_to_all | solution.py:641
  20.2 0.0 copy-done.7
  20.2 0.0 copy-start.8
  20.2 0.6 %copy-done.8 = s32[2,1,1]{0,2,1:T(1,128)S(1)} copy-done((s32[2,1,1]{0,2,1:T(1,128)S(1)}, s32[2,1,1]{0,2,1:T(1,128)}, u32[]{:S(2)}) %copy-start.8) | copy-done | bytes 32
  20.9 0.0 copy-start.9
  20.9 0.1 copy.21.counts
  21.0 0.6 %copy-done.9 = s32[2,1,1]{0,2,1:T(1,128)S(1)} copy-done((s32[2,1,1]{0,2,1:T(1,128)S(1)}, s32[2,1,1]{0,2,1:T(1,128)}, u32[]{:S(2)}) %copy-start.9) | copy-done | bytes 32
  21.5 0.0 copy-start.6
  21.5 0.1 copy.22.places
  21.6 6.8 %all-to-all-done.1 = f32[32,8,128]{2,1,0:T(8,128)S(1)} async-done(((f32[32,8,128]{2,1,0:T(8,128)}), f32[32,8,128]{2,1,0:T(8,128)S(1)}, u32[]{:S(2)}, u32[]{:S(2)}) %all-to-all-start.1) | async-done | bytes 131104 | tf_op jit(solution)/shard_map/all_to_all | solution.py:641
  28.4 0.0 copy-done.6
  28.4 3.7 %shard_map.148 = f32[256,128]{1,0:T(8,128)} custom-call(f32[256,128]{1,0:T(8,128)S(1)} %bitcast.12, s32[2,1,1,256]{3,2,1,0:T(1,128)S(1)} %copy-done.6, s32[2,1,1]{2,1,0:T(1,128)S(1)} %copy.21.counts, s32[2,1,1]{2,1,0:T(1,128)S(1)} %copy.22.places, f32[2,1,1,3,256]{4,3,2,1,0:T(4,128)S(1)} %copy.23.wanted), custom_call_target="tpu_custom_call" | custom-call | flops 1000000 | bytes 1048576 | tf_op jit(solution)/shard_map/pallas_call | solution.py:602
  32.0 2.6 %all-to-all-start.2 = ((f32[32,8,128]{2,1,0:T(8,128)}), f32[32,8,128]{2,1,0:T(8,128)S(1)}, u32[]{:S(2)}, u32[]{:S(2)}) async-start(f32[32,8,128]{2,1,0:T(8,128)} %bitcast.7), calls=%async_computation.2 | async-start | bytes 262144 | tf_op jit(solution)/shard_map/all_to_all | solution.py:641
  34.6 0.7 %shard_map.149.inverse = s32[64,128]{1,0:T(8,128)S(1)} custom-call(s32[32,128]{1,0:T(8,128)S(1)} %bitcast.14), custom_call_target="tpu_custom_call" | custom-call | flops 1000000 | bytes 1048576 | tf_op jit(solution)/shard_map/pallas_call | solution.py:602
  35.3 7.5 %all-to-all-done.2 = f32[32,8,128]{2,1,0:T(8,128)S(1)} async-done(((f32[32,8,128]{2,1,0:T(8,128)}), f32[32,8,128]{2,1,0:T(8,128)S(1)}, u32[]{:S(2)}, u32[]{:S(2)}) %all-to-all-start.2) | async-done | bytes 131104 | tf_op jit(solution)/shard_map/all_to_all | solution.py:641
  42.8 1.7 %shard_map.150 = (f32[3,1024]{1,0:T(4,128)}, f32[3,1024]{1,0:T(4,128)}, f32[4,1024]{1,0:T(4,128)}, f32[8,128]{1,0:T(8,128)}, f32[48,1024]{1,0:T(8,128)}) custom-call(f32[256,128]{1,0:T(8,128)S(1)} %bitcast.11, s32[64,128]{1,0:T(8,128)S(1)} %shard_map.149.inverse, f32[472,128]{1,0:T(8,128)S(1)} %get-tuple-element.14.raw, f32[120,128]{1,0:T(8,128)S(1)} %get-tuple-element.15.table), custom_call_target="tpu_custom_call" | custom-call | flops 1000000 | bytes 1048576 | tf_op jit(solution)/shard_map/pallas_call | solution.py:602
  (1 shorter events, 0.0 us)
Async XLA Ops:
  1.5 8.0 %copy-start.3 = (f32[4,1024]{1,0:T(4,128)S(1)}, f32[4,1024]{1,0:T(4,128)}, u32[]{:S(2)}) copy-start(f32[4,1024]{1,0:T(4,128)} %rots.1) | copy-start | bytes 49156
  1.5 8.0 %copy-start.4 = (f32[1024]{0:T(1024)S(1)}, f32[1024]{0:T(1024)}, u32[]{:S(2)}) copy-start(f32[1024]{0:T(1024)} %param.14) | copy-start | bytes 12292
  1.5 8.0 %copy-start.5 = (f32[2,4,6]{2,1,0:T(4,128)S(1)}, f32[2,4,6]{2,1,0:T(4,128)}, u32[]{:S(2)}) copy-start(f32[2,4,6]{2,1,0:T(4,128)} %cam.1) | copy-start | bytes 580
  2.2 7.3 %copy-start.1 = (f32[3,1024]{1,0:T(4,128)S(1)}, f32[3,1024]{1,0:T(4,128)}, u32[]{:S(2)}) copy-start(f32[3,1024]{1,0:T(4,128)} %pos.1) | copy-start | bytes 36868
  2.2 7.3 %copy-start.2 = (f32[3,1024]{1,0:T(4,128)S(1)}, f32[3,1024]{1,0:T(4,128)}, u32[]{:S(2)}) copy-start(f32[3,1024]{1,0:T(4,128)} %scales.1) | copy-start | bytes 36868
  2.2 14.4 %all-to-all-start = ((s32[32,1,128]{2,1,0:T(1,128)}), s32[32,1,128]{2,1,0:T(1,128)S(1)}, u32[]{:S(2)}, u32[]{:S(2)}) async-start(s32[32,1,128]{2,1,0:T(1,128)} %bitcast.2), calls=%async_computation | async-start | bytes 32768 | tf_op jit(solution)/shard_map/all_to_all | solution.py:641
  9.6 0.9 %copy-start = (f32[48,1024]{1,0:T(8,128)S(1)}, f32[48,1024]{1,0:T(8,128)}, u32[]{:S(2)}) copy-start(f32[48,1024]{1,0:T(8,128)} %cols.1) | copy-start | bytes 589828
  17.5 2.7 %copy-start.7 = (f32[2,1,1,3,256]{4,2,3,1,0:T(1,128)S(1)}, f32[2,1,1,3,256]{4,2,3,1,0:T(1,128)}, u32[]{:S(2)}) copy-start(f32[2,1,1,3,256]{4,2,3,1,0:T(1,128)} %param.17) | copy-start | bytes 18436
  17.5 10.9 %all-to-all-start.1 = ((f32[32,8,128]{2,1,0:T(8,128)}), f32[32,8,128]{2,1,0:T(8,128)S(1)}, u32[]{:S(2)}, u32[]{:S(2)}) async-start(f32[32,8,128]{2,1,0:T(8,128)} %bitcast.5), calls=%async_computation.1 | async-start | bytes 262144 | tf_op jit(solution)/shard_map/all_to_all | solution.py:641
  20.2 0.7 %copy-start.8 = (s32[2,1,1]{0,2,1:T(1,128)S(1)}, s32[2,1,1]{0,2,1:T(1,128)}, u32[]{:S(2)}) copy-start(s32[2,1,1]{0,2,1:T(1,128)} %param.19) | copy-start | bytes 28
  20.9 0.7 %copy-start.9 = (s32[2,1,1]{0,2,1:T(1,128)S(1)}, s32[2,1,1]{0,2,1:T(1,128)}, u32[]{:S(2)}) copy-start(s32[2,1,1]{0,2,1:T(1,128)} %param.18) | copy-start | bytes 28
  21.5 6.9 %copy-start.6 = (s32[2,1,1,256]{3,2,1,0:T(1,128)S(1)}, s32[2,1,1,256]{3,2,1,0:T(1,128)}, u32[]{:S(2)}) copy-start(s32[2,1,1,256]{3,2,1,0:T(1,128)} %lists.1) | copy-start | bytes 6148
  32.0 10.8 %all-to-all-start.2 = ((f32[32,8,128]{2,1,0:T(8,128)}), f32[32,8,128]{2,1,0:T(8,128)S(1)}, u32[]{:S(2)}, u32[]{:S(2)}) async-start(f32[32,8,128]{2,1,0:T(8,128)} %bitcast.7), calls=%async_computation.2 | async-start | bytes 262144 | tf_op jit(solution)/shard_map/all_to_all | solution.py:641
where the time goes:
time: 44.9 us; the launch traced here: 44.5 us
  waiting for transfers between devices  19.8 us (44%)
  starting transfers between devices  12.6 us (28%)
  Pallas kernels  7.49 us (17%)
  local copies, waits for them, and re-layouts  3.21 us (7%)
  between operations  0.75 us (2%)
  other arithmetic  0.68 us (2%)
    all_to_all x3, waiting for transfers between devices, exchange(): return lax.all_to_all(x, axes, split_axis=0, concat_axis=0, tiled=True)  19.8 us
    all_to_all x3, starting transfers between devices, exchange(): return lax.all_to_all(x, axes, split_axis=0, concat_axis=0, tiled=True)  12.6 us
    pallas_call x5, Pallas kernels, call(): pl.pallas_call(kernel, out_shape=outs, in_specs=in_specs or vmem(len(oper...  7.49 us
    unnamed x23, local copies, waits for them, and re-layouts  2.34 us
  transfers between devices with their start and end apart: 3, of which 3 were waited for; matrix products, arithmetic and copies ran while one was open for 0% of the time, Pallas kernels for 3%

commit v1 on v0

--- a/solution.py
+++ b/solution.py
@@ -31,7 +31,8 @@
 LANES = 128
 HALF = LANES // 2
 FIELDS = 9
-SENT = 8
+SENT = 5
+GROUP = 8
 RAW = 59
 TERMS = 15
 F32 = jnp.float32
@@ -221,19 +222,25 @@
     return lane // cap, lane % cap
 
 
-def pick_kernel(passes, cams, tiles, rows, cap, aligned, ids, rec, out):
-    group = 8
-    shape = (group, LANES)
+def ids_kernel(passes, cams, cap, ids, out):
+    for c in range(cams):
+        parts = [ids[p, 0, 0, c] for p in range(passes)]
+        tiles = parts[0].shape[0]
+        if passes * cap < HALF:
+            parts.append(jnp.zeros((tiles, HALF - passes * cap), jnp.int32))
+        out[c * tiles : (c + 1) * tiles, :] = jnp.concatenate(parts + parts, axis=1)
+
+
+def pick_kernel(passes, cams, tiles, rows, cap, aligned, ids, rec, out, inverse):
+    shape = (GROUP, LANES)
     lane = lax.broadcasted_iota(jnp.int32, shape, 1)
     lane_p, _ = lane_pass(shape, cap)
 
     def packets(first, c):
-        asked = ids[pl.ds(first, group), :]
+        asked = ids[pl.ds(first, GROUP), :]
         low, high = asked % LANES, asked // LANES
         if aligned:
-            blocks = [
-                jnp.broadcast_to(high[:, p * cap : p * cap + 1], shape) for p in range(passes)
-            ]
+            blocks = [jnp.broadcast_to(high[:, p * cap : p * cap + 1], shape) for p in range(passes)]
 
         def pick(f):
             found = jnp.zeros(shape, F32)
@@ -246,41 +253,39 @@
                     for b in range(rows):
                         line = jnp.broadcast_to(rec[start + b : start + b + 1, :], shape)
                         own = jnp.where(high == b, lane_pick(line, low), own)
-                found = jnp.where(lane_p == p, own, found)
+                found = own if p == 0 else jnp.where(lane_p == p, own, found)
             return found
 
-        for f in range(SENT):
-            value = pick(f)
-            if f == 0:
-                value = jnp.where(lane < HALF, value, pick(FIELDS - 1))
-            out[pl.ds(first * SENT + f, group, stride=SENT), :] = value
+        for r in range(SENT):
+            value = pick(2 * r)
+            if 2 * r + 1 < FIELDS:
+                value = jnp.where(lane < HALF, value, pick(2 * r + 1))
+            out[pl.ds(first * SENT + r, GROUP, stride=SENT), :] = value
 
     for c in range(cams):
-        if tiles == group:
+        if tiles == GROUP:
             packets(c * tiles, c)
         else:
 
             def step(k, carry, c=c):
-                packets(pl.multiple_of(c * tiles + k * group, group), c)
+                packets(pl.multiple_of(c * tiles + k * GROUP, GROUP), c)
                 return carry
 
-            lax.fori_loop(0, tiles // group, step, 0)
-
-
-def inverse_kernel(passes, cams, tiles, rows, cap, ids, inverse):
-    shape = (LANES, LANES)
-    column = lax.broadcasted_iota(jnp.int32, shape, 0)
-    _, lane_j = lane_pass(shape, cap)
-    place = (lane_j + 1).astype(F32)
+            lax.fori_loop(0, tiles // GROUP, step, 0)
+
+    square = (LANES, LANES)
+    column = lax.broadcasted_iota(jnp.int32, square, 0)
+    _, lane_j = lane_pass(square, cap)
+    place = (lane_j + 1 + lax.broadcasted_iota(jnp.int32, square, 1) // HALF * cap).astype(F32)
     wide = (passes * rows, LANES)
-    lane_p, _ = lane_pass(wide, cap)
-    lane = lax.broadcasted_iota(jnp.int32, wide, 1)
+    wide_lane = lax.broadcasted_iota(jnp.int32, wide, 1)
     key = lax.broadcasted_iota(jnp.int32, wide, 0)
-    lane_key = jnp.where(lane < passes * cap, lane_p * rows, -(1 << 20))
-
-    def one(c, t, found):
-        asked = ids[pl.ds(c * tiles + t, 1), :]
-        low = jnp.broadcast_to(asked % LANES, shape)
+    lane_key = jnp.where(wide_lane % HALF < passes * cap, lane_pass(wide, cap)[0] * rows, -(1 << 20))
+    line_lane = lax.broadcasted_iota(jnp.int32, (1, LANES), 1)
+
+    def two(c, t, found):
+        asked = jnp.where(line_lane < HALF, ids[pl.ds(c * tiles + t, 1), :], ids[pl.ds(c * tiles + t + 1, 1), :])
+        low = jnp.broadcast_to(asked % LANES, square)
         high = jnp.broadcast_to(asked // LANES, wide)
         match = jnp.where(low == column, place, 0.0).astype(BF16)
         owner = jnp.where(high + lane_key == key, 1.0, 0.0).astype(BF16)
@@ -290,18 +295,18 @@
     for c in range(cams):
         found = jnp.zeros(wide, jnp.int32)
         if tiles <= 8:
-            for t in range(tiles):
-                found = one(c, t, found)
+            for t in range(0, tiles, 2):
+                found = two(c, t, found)
         else:
-            found = lax.fori_loop(0, tiles, lambda t, f, c=c: one(c, t, f), found)
+            found = lax.fori_loop(0, tiles // 2, lambda t, f, c=c: two(c, 2 * t, f), found)
         for p in range(passes):
             start = (p * cams + c) * rows
             inverse[start : start + rows, :] = found[p * rows : (p + 1) * rows, :]
 
 
-def render_kernel(passes, owners, cap, entries, pixels, got, lists, counts, places, wanted, out, alphas, logs, weights):
+def render_kernel(passes, owners, cap, entries, pixels, got, lists, counts, places, wanted, out, alphas, logs):
     halves = entries // LANES
-    shape = (SENT, LANES)
+    shape = (GROUP, LANES)
     wide = 16
     lane = lax.broadcasted_iota(jnp.int32, shape, 1)
     sub = lax.broadcasted_iota(jnp.int32, shape, 0)
@@ -314,30 +319,22 @@
             slot_lane.append(slot % cap + p * cap)
     total = passes * halves
 
-    def gather(o, found):
-        packet = got[pl.ds(pl.multiple_of(o * SENT, SENT), SENT), :]
-        return tuple(
-            jnp.where(slot_owner[i] == o, lane_pick(packet, slot_lane[i]), found[i]) for i in range(total)
-        )
-
-    def gather_last(g, found):
-        lines = got[pl.ds(g * SENT * SENT, SENT, stride=SENT), :]
-        return tuple(
-            jnp.where(slot_owner[i] == g * SENT + sub, lane_pick(lines, slot_lane[i] + HALF), found[i])
-            for i in range(total)
-        )
-
-    empty = tuple(jnp.zeros(shape, F32) for _ in range(total))
+    def gather(g, found):
+        mine = [slot_owner[i] == g * GROUP + sub for i in range(total)]
+        new = []
+        for f in range(FIELDS):
+            lines = got[pl.ds(g * (GROUP * SENT) + f // 2, GROUP, stride=SENT), :]
+            for i in range(total):
+                new.append(jnp.where(mine[i], lane_pick(lines, slot_lane[i] + f % 2 * HALF), found[f * total + i]))
+        return tuple(new)
+
+    fields = tuple(jnp.zeros(shape, F32) for _ in range(FIELDS * total))
     if owners <= 32:
-        fields, last = empty, empty
-        for o in range(owners):
-            fields = gather(o, fields)
-        for g in range(owners // SENT):
-            last = gather_last(g, last)
+        for g in range(owners // GROUP):
+            fields = gather(g, fields)
     else:
-        fields = lax.fori_loop(0, owners, gather, empty)
-        last = lax.fori_loop(0, owners // SENT, gather_last, empty)
-    last = [jnp.sum(x, axis=0, keepdims=True) for x in last]
+        fields = lax.fori_loop(0, owners // GROUP, gather, fields)
+    fields = [jnp.sum(x, axis=0, keepdims=True) for x in fields]
 
     pair = (LANES, LANES)
     lane_p, lane_j = lane_pass(pair, cap)
@@ -367,10 +364,10 @@
         0.0,
     ).astype(BF16)
     entry_row = lax.broadcasted_iota(jnp.int32, (1, entries), 1)
-    pixel = lax.broadcasted_iota(jnp.int32, (SENT, pixels), 1)
+    pixel = lax.broadcasted_iota(jnp.int32, (GROUP, pixels), 1)
     local_x = (pixel % wide).astype(F32) - 7.5
     local_y = (pixel // wide).astype(F32) - 7.5
-    kind = lax.broadcasted_iota(jnp.int32, (SENT, pixels), 0)
+    kind = lax.broadcasted_iota(jnp.int32, (GROUP, pixels), 0)
     moment = jnp.where(
         kind == 0,
         1.0,
@@ -389,15 +386,14 @@
     grads = []
     for p in range(passes):
         line = [
-            jnp.concatenate([fields[p * halves + h][f : f + 1, :] for h in range(halves)], axis=1) for f in range(SENT)
+            jnp.concatenate([fields[f * total + p * halves + h] for h in range(halves)], axis=1) for f in range(FIELDS)
         ]
-        blue = jnp.concatenate([last[p * halves + h] for h in range(halves)], axis=1)
-        place = places[p, 0, 0]
+        place = places[0, p]
         u = line[0] - (place % 256 * 16 + 8).astype(F32)
         v = line[1] - (place // 256 * 16 + 8).astype(F32)
         c_a, c_b, c_c, base = line[2], line[3], line[4], line[5]
-        color = jnp.concatenate([line[6], line[7], blue], axis=0)
-        live = jnp.where(entry_row < counts[p, 0, 0], base, 0.0)
+        color = jnp.concatenate(line[6:9], axis=0)
+        live = jnp.where(entry_row < counts[0, p], base, 0.0)
 
         d_x = column_x - u
         q_xx = (-0.5 * c_a) * d_x * d_x
@@ -412,13 +408,12 @@
         through = jnp.exp(dot(high, before, ((1,), (0,))) + dot(low, before, ((1,), (0,))))
         alpha = alphas[p]
         weight = alpha * through
-        weights[p] = weight
         w_high, w_low = split(weight)
         c_high, c_low = split(color)
         shown = (
             dot(c_high, w_high, ((1,), (1,))) + dot(c_low, w_high, ((1,), (1,))) + dot(c_high, w_low, ((1,), (1,)))
         )
-        residual = shown - wanted[p, 0, 0]
+        residual = shown - jnp.concatenate([wanted[p, k] for k in range(3)], axis=0)
         r_high, r_low = split(residual)
         left = jnp.concatenate([r_high, r_high, r_low], axis=0)
         right = jnp.concatenate([c_high, c_low, c_high], axis=0)
@@ -466,14 +461,14 @@
                     found = jnp.where((which == h) & (own_p == p), lane_pick(line, index), found)
             return found
 
-        for f in range(SENT):
-            value = pick(f)
-            if f == 0:
-                value = jnp.where(lane < HALF, value, pick(FIELDS - 1))
-            out[pl.ds(first * SENT + f, SENT, stride=SENT), :] = value
-
-    for g in range(owners // SENT):
-        packets(g * SENT, source[g * SENT : (g + 1) * SENT, :])
+        for r in range(SENT):
+            value = pick(2 * r)
+            if 2 * r + 1 < FIELDS:
+                value = jnp.where(lane < HALF, value, pick(2 * r + 1))
+            out[pl.ds(first * SENT + r, GROUP, stride=SENT), :] = value
+
+    for g in range(owners // GROUP):
+        packets(g * GROUP, source[g * GROUP : (g + 1) * GROUP, :])
 
 
 def pull_kernel(passes, cams, tiles, rows, cap, aligned, got, inverse, raw, table, pos, scales, rots, opac, cols, total):
@@ -500,7 +495,8 @@
         if aligned:
             row_t = jnp.broadcast_to(jnp.max(slot_t, axis=1, keepdims=True), shape)
 
-        def fetch(f, row, shift):
+        def fetch(f):
+            row, shift = f // 2, f % 2 * HALF
             if aligned:
                 lines = got[pl.ds(c * tiles * SENT + row, tiles, stride=SENT), :]
                 return jnp.where(valid, lane_pick(row_pick(lines, row_t), slot_lane + shift), 0.0)
@@ -511,7 +507,7 @@
 
             return lax.fori_loop(0, tiles, one, jnp.zeros(shape, F32))
 
-        g = [fetch(f, f, 0) for f in range(SENT)] + [fetch(FIELDS - 1, 0, HALF)]
+        g = [fetch(f) for f in range(FIELDS)]
         rotate, offset, center = camera_of(table, view, views, shape)
         m, inv, main, at_x, at_y, t_x, t_y, w_x, w_y, conic = screen_of(point, cov, rotate, offset)
         c_a, c_b, c_c = conic
@@ -638,39 +634,42 @@
         return jax.ShapeDtypeStruct(shape, F32)
 
     def exchange(x):
-        return lax.all_to_all(x, axes, split_axis=0, concat_axis=0, tiled=True)
-
-    wanted_ids = jnp.transpose(fetch_ids[:, 0, 0], (1, 2, 0, 3)).reshape(owners, passes * cap)
-    wanted_ids = jnp.pad(wanted_ids, ((0, 0), (0, HALF - passes * cap)))
-    arrived = exchange(jnp.concatenate([wanted_ids, wanted_ids], axis=1))
-
+        lines = x.reshape(owners, 1, -1)
+        return lax.all_to_all(lines, axes, split_axis=0, concat_axis=0, tiled=True).reshape(x.shape)
+
+    wanted_ids = call(
+        functools.partial(ids_kernel, passes, cams, cap),
+        jax.ShapeDtypeStruct((owners, LANES), jnp.int32),
+        [fetch_ids],
+    )
+    arrived = exchange(wanted_ids)
     records, raw, table = call(
         functools.partial(project_kernel, passes, cams, rows),
         [shaped(views * FIELDS * rows, LANES), shaped(RAW * rows, LANES), shaped(TERMS * views, LANES)],
         [positions, log_scales, rotations, opacities.reshape(rows, LANES), colors, cameras],
     )
-    packets = call(
+    packets, inverse = call(
         functools.partial(pick_kernel, passes, cams, tiles, rows, cap, aligned),
-        shaped(owners * SENT, LANES),
+        [shaped(owners * SENT, LANES), jax.ShapeDtypeStruct((views * rows, LANES), jnp.int32)],
         [arrived, records],
     )
     fetched = exchange(packets)
-    inverse = call(
-        functools.partial(inverse_kernel, passes, cams, tiles, rows, cap),
-        jax.ShapeDtypeStruct((views * rows, LANES), jnp.int32),
-        [arrived],
-    )
     smem = pl.BlockSpec(memory_space=pltpu.SMEM)
     whole = vmem(1)[0]
     slot_grads = call(
         functools.partial(render_kernel, passes, owners, cap, entries, pixels),
         shaped(owners * SENT, LANES),
-        [fetched, tile_lists, tile_counts, tile_ids, targets],
+        [
+            fetched,
+            tile_lists,
+            tile_counts.reshape(1, passes),
+            tile_ids.reshape(1, passes),
+            targets.reshape(passes, 3, 1, pixels),
+        ],
         in_specs=[whole, whole, smem, smem, whole],
         scratch=[
             pltpu.VMEM((passes, pixels, entries), F32),
             pltpu.VMEM((pixels, entries), F32),
-            pltpu.VMEM((passes, pixels, entries), F32),
         ],
     )
     coming = exchange(slot_grads)

time: 44.9 us -> 41.3 us (0.920)
  blocking collectives: 0 us -> 18.7 us
  waiting for transfers between devices: 19.8 us -> 5.52 us
  starting transfers between devices: 12.6 us -> 7.3 us
  Pallas kernels: 7.49 us -> 6.34 us
  local copies, waits for them, and re-layouts: 3.21 us -> 2.38 us
  other arithmetic: 0.68 us -> 0 us
    all_to_all x0 -> x2, blocking collectives: none -> 18.7 us  [exchange(): lax.all_to_all(lines, axes, split_axis=0, concat_axis=0, tiled=True)]
    all_to_all x3 -> x1, waiting for transfers between devices: 19.8 us -> 5.52 us  [exchange(): lax.all_to_all(lines, axes, split_axis=0, concat_axis=0, tiled=True)]
    all_to_all x3 -> x1, starting transfers between devices: 12.6 us -> 7.3 us  [exchange(): lax.all_to_all(lines, axes, split_axis=0, concat_axis=0, tiled=True)]
    pallas_call x5, Pallas kernels: 7.49 us -> 6.34 us  [call(): pl.pallas_call(kernel, out_shape=outs, in_specs=in_specs or vmem(len(oper...]
    transpose x1 -> x0, local copies, waits for them, and re-layouts: 0.79 us -> none  [body(): jnp.transpose(fetch_ids[:, 0, 0], (1, 2, 0, 3))]
    concatenate x1 -> x0, other arithmetic: 0.68 us -> none  [body(): arrived = exchange(jnp.concatenate([wanted_ids, wanted_ids], axis=1))]
    unnamed x23 -> x22, local copies, waits for them, and re-layouts: 2.34 us -> 2.38 us
  transfers between devices with their start and end apart: 3 -> 1, of which waited for: 3 -> 1; matrix products, arithmetic and copies ran while one was open for 0% -> 0% of each run, Pallas kernels for 3% -> 1%
where the time goes in v1:
time: 41.3 us; the launch traced here: 40.9 us
  blocking collectives  18.7 us (45%)
  starting transfers between devices  7.3 us (18%)
  Pallas kernels  6.34 us (15%)
  waiting for transfers between devices  5.52 us (13%)
  local copies, waits for them, and re-layouts  2.38 us (6%)
  between operations  0.72 us (2%)
    all_to_all x2, blocking collectives, exchange(): lax.all_to_all(lines, axes, split_axis=0, concat_axis=0, tiled=True)  18.7 us
    all_to_all x1, starting transfers between devices, exchange(): lax.all_to_all(lines, axes, split_axis=0, concat_axis=0, tiled=True)  7.3 us
    pallas_call x5, Pallas kernels, call(): pl.pallas_call(kernel, out_shape=outs, in_specs=in_specs or vmem(len(oper...  6.34 us
    all_to_all x1, waiting for transfers between devices, exchange(): lax.all_to_all(lines, axes, split_axis=0, concat_axis=0, tiled=True)  5.52 us
    unnamed x22, local copies, waits for them, and re-layouts  2.38 us
  transfers between devices with their start and end apart: 1, of which 1 were waited for; matrix products, arithmetic and copies ran while one was open for 0% of the time, Pallas kernels for 1%

profile of v1, /device:TPU:0, one launch (start us, length us, event | category | flops | bytes accessed | tf_op | source)
XLA Modules:
  0.0 40.9 jit_solution(11787579124700519927)
XLA Ops:
  0.6 0.0 copy-start.1
  0.6 0.7 %copy-done.1 = s32[2,1,1,4,8,32]{5,4,3,2,1,0:T(8,128)S(1)} copy-done((s32[2,1,1,4,8,32]{5,4,3,2,1,0:T(8,128)S(1)}, s32[2,1,1,4,8,32]{5,4,3,2,1,0:T(8,128)}, u32[]{:S(2)}) %copy-start.1) | copy-done | bytes 8216
  1.4 0.0 copy-start.4
  1.4 0.0 copy-start.6
  1.4 0.0 copy-start.7
  1.4 0.7 %shard_map.146 = s32[32,128]{1,0:T(8,128)} custom-call(s32[2,1,1,4,8,32]{5,4,3,2,1,0:T(8,128)S(1)} %copy-done.1), custom_call_target="tpu_custom_call" | custom-call | flops 1000000 | bytes 1048576 | tf_op jit(solution)/shard_map/pallas_call | solution.py:598
  2.1 0.0 copy-start.2
  2.1 0.0 copy-start.3
  2.1 7.3 %all-to-all-start = ((s32[32,1,128]{2,1,0:T(1,128)}), s32[32,1,128]{2,1,0:T(1,128)S(1)}, u32[]{:S(2)}, u32[]{:S(2)}) async-start(s32[32,1,128]{2,1,0:T(1,128)} %bitcast.1), calls=%async_computation | async-start | bytes 32768 | tf_op jit(solution)/shard_map/all_to_all | solution.py:638
  9.4 0.0 copy-done.4
  9.4 0.0 copy-done.6
  9.4 0.0 copy-done.7
  9.4 0.0 copy-done.2
  9.4 0.0 copy-done.3
  9.4 0.0 copy-start
  9.5 0.9 %copy-done = f32[48,1024]{1,0:T(8,128)S(1)} copy-done((f32[48,1024]{1,0:T(8,128)S(1)}, f32[48,1024]{1,0:T(8,128)}, u32[]{:S(2)}) %copy-start) | copy-done | bytes 196632
  10.4 0.6 %shard_map.147 = (f32[576,128]{1,0:T(8,128)S(1)}, f32[472,128]{1,0:T(8,128)S(1)}, f32[120,128]{1,0:T(8,128)S(1)}) custom-call(f32[3,1024]{1,0:T(4,128)S(1)} %copy-done.2, f32[3,1024]{1,0:T(4,128)S(1)} %copy-done.3, f32[4,1024]{1,0:T(4,128)S(1)} %copy-done.4, f32[8,128]{1,0:T(8,128)S(1)} %bitcast.19, f32[48,1024]{1,0:T(8,128)S(1)} %copy-done, ...), custom_call_target="tpu_custom_call" | custom-call | flops 1000000 | bytes 1048576 | tf_op jit(solution)/shard_map/pallas_call | solution.py:598
  10.9 5.5 %all-to-all-done = s32[32,1,128]{2,1,0:T(1,128)S(1)} async-done(((s32[32,1,128]{2,1,0:T(1,128)}), s32[32,1,128]{2,1,0:T(1,128)S(1)}, u32[]{:S(2)}, u32[]{:S(2)}) %all-to-all-start) | async-done | bytes 16416 | tf_op jit(solution)/shard_map/all_to_all | solution.py:638
  16.5 0.4 shard_map.148
  16.9 0.0 copy-start.8
  16.9 9.4 %all_to_all.15 = f32[32,1,640]{2,1,0:T(1,128)S(1)} all-to-all(f32[32,1,640]{2,1,0:T(1,128)S(1)} %bitcast.16), channel_id=1, replica_groups=mesh['cam'=4,'tile'=8] {'cam','tile'}, dimensions={0} | all-to-all | bytes 163840 | tf_op jit(solution)/shard_map/all_to_all | solution.py:638
  26.3 0.0 copy-start.5
  26.3 0.0 copy-start.9
  26.3 0.0 copy-start.10
  26.3 0.0 copy-done.8
  26.3 0.7 %copy-done.5 = f32[2,1,1,3,256]{4,2,3,1,0:T(1,128)S(1)} copy-done((f32[2,1,1,3,256]{4,2,3,1,0:T(1,128)S(1)}, f32[2,1,1,3,256]{4,2,3,1,0:T(1,128)}, u32[]{:S(2)}) %copy-start.5) | copy-done | bytes 6168
  26.9 0.0 copy-done.9
  27.0 0.0 copy-done.10
  27.0 3.0 %shard_map.149 = f32[160,128]{1,0:T(8,128)S(1)} custom-call(f32[160,128]{1,0:T(8,128)S(1)} %bitcast.14, s32[2,1,1,256]{3,2,1,0:T(1,128)S(1)} %copy-done.8, s32[1,2]{1,0:T(1,128)S(1)} %bitcast.20, s32[1,2]{1,0:T(1,128)S(1)} %bitcast.21, f32[2,3,1,256]{3,2,1,0:T(1,128)S(1)} %bitcast.18), custom_call_target="tpu_custom_call" | custom-call | flops 1000000 | bytes 1048576 | tf_op jit(solution)/shard_map/pallas_call | solution.py:598
  30.0 9.3 %all_to_all.16 = f32[32,1,640]{2,1,0:T(1,128)S(1)} all-to-all(f32[32,1,640]{2,1,0:T(1,128)S(1)} %bitcast.15), channel_id=1, replica_groups=mesh['cam'=4,'tile'=8] {'cam','tile'}, dimensions={0} | all-to-all | bytes 163840 | tf_op jit(solution)/shard_map/all_to_all | solution.py:638
  39.2 1.7 %shard_map.150 = (f32[3,1024]{1,0:T(4,128)}, f32[3,1024]{1,0:T(4,128)}, f32[4,1024]{1,0:T(4,128)}, f32[8,128]{1,0:T(8,128)}, f32[48,1024]{1,0:T(8,128)}) custom-call(f32[160,128]{1,0:T(8,128)S(1)} %bitcast.13, s32[64,128]{1,0:T(8,128)S(1)} %get-tuple-element.17.inverse, f32[472,128]{1,0:T(8,128)S(1)} %get-tuple-element.18.raw, ...), custom_call_target="tpu_custom_call" | custom-call | flops 1000000 | bytes 1048576 | tf_op jit(solution)/shard_map/pallas_call | solution.py:598
Async XLA Ops:
  0.6 0.8 %copy-start.1 = (s32[2,1,1,4,8,32]{5,4,3,2,1,0:T(8,128)S(1)}, s32[2,1,1,4,8,32]{5,4,3,2,1,0:T(8,128)}, u32[]{:S(2)}) copy-start(s32[2,1,1,4,8,32]{5,4,3,2,1,0:T(8,128)} %ids.1) | copy-start | bytes 24580
  1.4 8.0 %copy-start.4 = (f32[4,1024]{1,0:T(4,128)S(1)}, f32[4,1024]{1,0:T(4,128)}, u32[]{:S(2)}) copy-start(f32[4,1024]{1,0:T(4,128)} %rots.1) | copy-start | bytes 49156
  1.4 8.0 %copy-start.6 = (f32[1024]{0:T(1024)S(1)}, f32[1024]{0:T(1024)}, u32[]{:S(2)}) copy-start(f32[1024]{0:T(1024)} %param.14) | copy-start | bytes 12292
  1.4 8.0 %copy-start.7 = (f32[2,4,6]{2,1,0:T(4,128)S(1)}, f32[2,4,6]{2,1,0:T(4,128)}, u32[]{:S(2)}) copy-start(f32[2,4,6]{2,1,0:T(4,128)} %cam.1) | copy-start | bytes 580
  2.1 7.3 %copy-start.2 = (f32[3,1024]{1,0:T(4,128)S(1)}, f32[3,1024]{1,0:T(4,128)}, u32[]{:S(2)}) copy-start(f32[3,1024]{1,0:T(4,128)} %pos.1) | copy-start | bytes 36868
  2.1 7.3 %copy-start.3 = (f32[3,1024]{1,0:T(4,128)S(1)}, f32[3,1024]{1,0:T(4,128)}, u32[]{:S(2)}) copy-start(f32[3,1024]{1,0:T(4,128)} %scales.1) | copy-start | bytes 36868
  2.1 14.4 %all-to-all-start = ((s32[32,1,128]{2,1,0:T(1,128)}), s32[32,1,128]{2,1,0:T(1,128)S(1)}, u32[]{:S(2)}, u32[]{:S(2)}) async-start(s32[32,1,128]{2,1,0:T(1,128)} %bitcast.1), calls=%async_computation | async-start | bytes 32768 | tf_op jit(solution)/shard_map/all_to_all | solution.py:638
  9.4 0.9 %copy-start = (f32[48,1024]{1,0:T(8,128)S(1)}, f32[48,1024]{1,0:T(8,128)}, u32[]{:S(2)}) copy-start(f32[48,1024]{1,0:T(8,128)} %cols.1) | copy-start | bytes 589828
  16.9 9.4 %copy-start.8 = (s32[2,1,1,256]{3,2,1,0:T(1,128)S(1)}, s32[2,1,1,256]{3,2,1,0:T(1,128)}, u32[]{:S(2)}) copy-start(s32[2,1,1,256]{3,2,1,0:T(1,128)} %lists.1) | copy-start | bytes 6148
  26.3 0.7 %copy-start.5 = (f32[2,1,1,3,256]{4,2,3,1,0:T(1,128)S(1)}, f32[2,1,1,3,256]{4,2,3,1,0:T(1,128)}, u32[]{:S(2)}) copy-start(f32[2,1,1,3,256]{4,2,3,1,0:T(1,128)} %param.17) | copy-start | bytes 18436
  26.3 0.7 %copy-start.9 = (s32[2,1,1]{0,2,1:T(1,128)S(1)}, s32[2,1,1]{0,2,1:T(1,128)}, u32[]{:S(2)}) copy-start(s32[2,1,1]{0,2,1:T(1,128)} %param.19) | copy-start | bytes 28
  26.3 0.7 %copy-start.10 = (s32[2,1,1]{0,2,1:T(1,128)S(1)}, s32[2,1,1]{0,2,1:T(1,128)}, u32[]{:S(2)}) copy-start(s32[2,1,1]{0,2,1:T(1,128)} %param.18) | copy-start | bytes 28

commit v2 on v1

--- a/solution.py
+++ b/solution.py
@@ -34,6 +34,8 @@
 SENT = 5
 GROUP = 8
 RAW = 59
+KEPT = 38
+SCENE = 6
 TERMS = 15
 F32 = jnp.float32
 BF16 = jnp.bfloat16
@@ -179,9 +181,20 @@
     return [terms[0:3], terms[3:6], terms[6:9]], terms[9:12], terms[12:15]
 
 
-def project_kernel(passes, cams, rows, pos, scales, rots, opac, cols, cam, rec, raw, table):
+def project_kernel(
+    passes, cams, rows, owners, cap, far_pos, far_scales, far_rots, far_opac, far_cols, far_cam, far_lists, far_wanted,
+    far_counts, far_places, rec, raw, table, kept, scene, source, chosen,
+    pos, scales, rots, opac, cols, cam, lists, wanted, counts, places, done,
+):
     views = passes * cams
     shape = (rows, LANES)
+    fars = (far_cam, far_pos, far_scales, far_rots, far_opac, far_lists, far_wanted, far_counts, far_places, far_cols)
+    nears = (cam, pos, scales, rots, opac, lists, wanted, counts, places, cols)
+    copies = [pltpu.make_async_copy(a, b, done.at[k]) for k, (a, b) in enumerate(zip(fars, nears))]
+    for copy in copies:
+        copy.start()
+    for copy in copies[:-1]:
+        copy.wait()
     camera_rows(cam, table, passes, cams)
     base = 0
     for ref in (pos, scales, rots):
@@ -190,12 +203,12 @@
             raw[pl.ds(base * rows + i, count, stride=rows), :] = ref[:, i * LANES : (i + 1) * LANES]
         base += count
     raw[base * rows : (base + 1) * rows, :] = opac[...]
-    base += 1
-    for i in range(rows):
-        raw[pl.ds(base * rows + i, cols.shape[0], stride=rows), :] = cols[:, i * LANES : (i + 1) * LANES]
 
     def at(k):
         return raw[k * rows : (k + 1) * rows, :]
+
+    def put(ref, k, value):
+        ref[k * rows : (k + 1) * rows, :] = value
 
     point = [at(k) for k in range(3)]
     squares = [jnp.exp(2.0 * at(3 + k)) for k in range(3)]
@@ -204,17 +217,55 @@
     opacity = 1.0 / (1.0 + jnp.exp(-at(10)))
     for view in range(views):
         rotate, offset, center = camera_of(table, view, views, shape)
-        _, _, _, at_x, at_y, _, _, _, _, conic = screen_of(point, cov, rotate, offset)
-        direction, _ = direction_of(point, center)
+        _, inv, main, at_x, at_y, t_x, t_y, w_x, w_y, conic = screen_of(point, cov, rotate, offset)
+        direction, back = direction_of(point, center)
         basis = basis_of(*direction)
         fields = [FOCAL * at_x + CENTER_X, FOCAL * at_y + CENTER_Y, conic[0], conic[1], conic[2], opacity]
-        for channel in range(3):
-            total = 0.5 + SH_ZERO * at(11 + channel)
-            for k in range(1, 16):
-                total = total + basis[k] * at(11 + 3 * k + channel)
-            fields.append(total)
         for f, value in enumerate(fields):
-            rec[(view * FIELDS + f) * rows : (view * FIELDS + f + 1) * rows, :] = value
+            put(rec, view * FIELDS + f, value)
+        for k, value in enumerate([inv, main, at_x, at_y, *t_x, *t_y, *w_x, *w_y, *conic, *direction, back, *basis[1:]]):
+            put(kept, view * KEPT + k, value)
+
+    entries, pixels = lists.shape[-1], wanted.shape[-1]
+    entry_row = lax.broadcasted_iota(jnp.int32, (1, entries), 1)
+    for p in range(passes):
+        for k in range(3):
+            scene[p * SCENE + k : p * SCENE + k + 1, :] = wanted[p, k]
+        count = jnp.broadcast_to(counts[:, p : p + 1], (1, entries))
+        scene[p * SCENE + 3 : p * SCENE + 4, :] = jnp.where(entry_row < count, 1.0, 0.0)
+        place = jnp.broadcast_to(places[:, p : p + 1], (1, entries))
+        for k, value in enumerate((place % 256 * 16 + 8, place // 256 * 16 + 8)):
+            scene[p * SCENE + 4 + k : p * SCENE + 5 + k, :] = value.astype(F32)
+        chosen[p : p + 1, :] = lists[p, 0]
+    pair = (LANES, LANES)
+    turned = lax.broadcasted_iota(jnp.int32, pair, 0)
+    turned_p, turned_j = turned % HALF // cap, turned % cap
+    entry = (lax.broadcasted_iota(jnp.int32, pair, 1) + 1).astype(F32)
+    owner_row = lax.broadcasted_iota(jnp.int32, (owners, LANES), 0)
+    found = jnp.zeros((owners, LANES), jnp.int32)
+    for p in range(passes):
+        for h in range(entries // LANES):
+            slot = lists[p, 0, :, h * LANES : (h + 1) * LANES]
+            mine = jnp.where(jnp.broadcast_to(slot // cap, (owners, LANES)) == owner_row, 1.0, 0.0).astype(BF16)
+            here = jnp.where(
+                (jnp.broadcast_to(slot % cap, pair) == turned_j) & (turned_p == p), entry, 0.0
+            ).astype(BF16)
+            hit = dot(mine, here, ((1,), (1,)))
+            found = jnp.where(hit > 0.5, hit.astype(jnp.int32) + h * LANES, found)
+    source[...] = found
+
+    copies[-1].wait()
+    for i in range(rows):
+        raw[pl.ds(11 * rows + i, cols.shape[0], stride=rows), :] = cols[:, i * LANES : (i + 1) * LANES]
+    for channel in range(3):
+        totals = [0.5 + SH_ZERO * at(11 + channel)] * views
+        for k in range(1, 16):
+            color = at(11 + 3 * k + channel)
+            for view in range(views):
+                start = (view * KEPT + KEPT - 16 + k) * rows
+                totals[view] = totals[view] + kept[start : start + rows, :] * color
+        for view in range(views):
+            put(rec, view * FIELDS + 6 + channel, totals[view])
 
 
 def lane_pass(shape, cap):
@@ -222,13 +273,19 @@
     return lane // cap, lane % cap
 
 
-def ids_kernel(passes, cams, cap, ids, out):
+def ids_kernel(passes, cams, cap, ids, out, landed, lines, done):
+    copy = pltpu.make_async_copy(ids, landed, done)
+    copy.start()
+    copy.wait()
     for c in range(cams):
-        parts = [ids[p, 0, 0, c] for p in range(passes)]
+        parts = [landed[p, 0, 0, c] for p in range(passes)]
         tiles = parts[0].shape[0]
         if passes * cap < HALF:
             parts.append(jnp.zeros((tiles, HALF - passes * cap), jnp.int32))
-        out[c * tiles : (c + 1) * tiles, :] = jnp.concatenate(parts + parts, axis=1)
+        lines[c * tiles : (c + 1) * tiles, :] = jnp.concatenate(parts + parts, axis=1)
+    copy = pltpu.make_async_copy(lines, out, done)
+    copy.start()
+    copy.wait()
 
 
 def pick_kernel(passes, cams, tiles, rows, cap, aligned, ids, rec, out, inverse):
@@ -304,7 +361,8 @@
             inverse[start : start + rows, :] = found[p * rows : (p + 1) * rows, :]
 
 
-def render_kernel(passes, owners, cap, entries, pixels, got, lists, counts, places, wanted, out, alphas, logs):
+def render_kernel(passes, owners, cap, entries, pixels, got, lists, scene, source, out, *scratch):
+    alphas, ratios, sums, high, low = [scratch[k * passes : (k + 1) * passes] for k in range(5)]
     halves = entries // LANES
     shape = (GROUP, LANES)
     wide = 16
@@ -314,7 +372,7 @@
     slot_owner, slot_lane = [], []
     for p in range(passes):
         for h in range(halves):
-            slot = jnp.broadcast_to(lists[p, 0, :, h * LANES : (h + 1) * LANES], shape)
+            slot = jnp.broadcast_to(lists[p : p + 1, h * LANES : (h + 1) * LANES], shape)
             slot_owner.append(slot // cap)
             slot_lane.append(slot % cap + p * cap)
     total = passes * halves
@@ -336,103 +394,80 @@
         fields = lax.fori_loop(0, owners // GROUP, gather, fields)
     fields = [jnp.sum(x, axis=0, keepdims=True) for x in fields]
 
-    pair = (LANES, LANES)
-    lane_p, lane_j = lane_pass(pair, cap)
-    turned_p, turned_j = lax.broadcasted_iota(jnp.int32, pair, 0) % HALF // cap, lax.broadcasted_iota(jnp.int32, pair, 0) % cap
-    entry = (lax.broadcasted_iota(jnp.int32, pair, 1) + 1).astype(F32)
-    owner_row = lax.broadcasted_iota(jnp.int32, (owners, LANES), 0)
-    source = jnp.zeros((owners, LANES), jnp.int32)
-    for p in range(passes):
-        for h in range(halves):
-            i = p * halves + h
-            slot = lists[p, 0, :, h * LANES : (h + 1) * LANES]
-            mine = jnp.where(jnp.broadcast_to(slot // cap, (owners, LANES)) == owner_row, 1.0, 0.0).astype(BF16)
-            here = jnp.where(
-                (jnp.broadcast_to(slot % cap, pair) == turned_j) & (turned_p == p), entry, 0.0
-            ).astype(BF16)
-            hit = dot(mine, here, ((1,), (1,)))
-            source = jnp.where(hit > 0.5, hit.astype(jnp.int32) + h * LANES, source)
-
-    before = jnp.where(
-        lax.broadcasted_iota(jnp.int32, (entries, entries), 0) < lax.broadcasted_iota(jnp.int32, (entries, entries), 1),
-        1.0,
-        0.0,
-    ).astype(BF16)
-    after = jnp.where(
-        lax.broadcasted_iota(jnp.int32, (entries, entries), 0) > lax.broadcasted_iota(jnp.int32, (entries, entries), 1),
-        1.0,
-        0.0,
-    ).astype(BF16)
-    entry_row = lax.broadcasted_iota(jnp.int32, (1, entries), 1)
-    pixel = lax.broadcasted_iota(jnp.int32, (GROUP, pixels), 1)
-    local_x = (pixel % wide).astype(F32) - 7.5
-    local_y = (pixel // wide).astype(F32) - 7.5
-    kind = lax.broadcasted_iota(jnp.int32, (GROUP, pixels), 0)
-    moment = jnp.where(
-        kind == 0,
-        1.0,
-        jnp.where(
-            kind == 1,
-            local_x,
-            jnp.where(
-                kind == 2,
-                local_y,
-                jnp.where(kind == 3, local_x * local_x, jnp.where(kind == 4, local_x * local_y, local_y * local_y)),
-            ),
-        ),
-    ).astype(BF16)
+    square = (entries, entries)
+    row_at, column_at = lax.broadcasted_iota(jnp.int32, square, 0), lax.broadcasted_iota(jnp.int32, square, 1)
+    before = jnp.where(row_at < column_at, 1.0, 0.0).astype(BF16)
+    after = jnp.where(row_at > column_at, 1.0, 0.0).astype(BF16)
     column_x = lax.broadcasted_iota(jnp.int32, (wide, entries), 0).astype(F32) - 7.5
-
-    grads = []
+    steps = [slice(y * wide, (y + 1) * wide) for y in range(pixels // wide)]
+
+    lines, spans = [], []
     for p in range(passes):
         line = [
             jnp.concatenate([fields[f * total + p * halves + h] for h in range(halves)], axis=1) for f in range(FIELDS)
         ]
-        place = places[0, p]
-        u = line[0] - (place % 256 * 16 + 8).astype(F32)
-        v = line[1] - (place // 256 * 16 + 8).astype(F32)
-        c_a, c_b, c_c, base = line[2], line[3], line[4], line[5]
-        color = jnp.concatenate(line[6:9], axis=0)
-        live = jnp.where(entry_row < counts[0, p], base, 0.0)
-
-        d_x = column_x - u
+        line[0] = line[0] - scene[p * SCENE + 4 : p * SCENE + 5, :]
+        line[1] = line[1] - scene[p * SCENE + 5 : p * SCENE + 6, :]
+        lines.append(line)
+        spans.append(column_x - line[0])
+
+    def offset_y(p, y):
+        return (y - 7.5) - lines[p][1]
+
+    for p in range(passes):
+        _, _, c_a, c_b, c_c, base = lines[p][:6]
+        live = base * scene[p * SCENE + 3 : p * SCENE + 4, :]
+        d_x = spans[p]
         q_xx = (-0.5 * c_a) * d_x * d_x
-        q_x = c_b * d_x
-        for y in range(pixels // wide):
-            d_y = (y - 7.5) - v
-            power = q_xx - (q_x * d_y + 0.5 * c_c * d_y * d_y)
-            alpha = live * jnp.exp(power)
-            alphas[p, y * wide : (y + 1) * wide, :] = alpha
-            logs[y * wide : (y + 1) * wide, :] = jnp.log(1.0 - alpha)
-        high, low = split(logs[...])
-        through = jnp.exp(dot(high, before, ((1,), (0,))) + dot(low, before, ((1,), (0,))))
-        alpha = alphas[p]
-        weight = alpha * through
-        w_high, w_low = split(weight)
-        c_high, c_low = split(color)
-        shown = (
-            dot(c_high, w_high, ((1,), (1,))) + dot(c_low, w_high, ((1,), (1,))) + dot(c_high, w_low, ((1,), (1,)))
-        )
-        residual = shown - jnp.concatenate([wanted[p, k] for k in range(3)], axis=0)
-        r_high, r_low = split(residual)
-        left = jnp.concatenate([r_high, r_high, r_low], axis=0)
-        right = jnp.concatenate([c_high, c_low, c_high], axis=0)
-        slope = dot(left, right, ((0,), (0,)))
-        pulled = weight * slope
-        high, low = split(pulled)
-        rest = dot(high, after, ((1,), (0,))) + dot(low, after, ((1,), (0,)))
-        power_grad = pulled - alpha / (1.0 - alpha) * rest
-        high, low = split(power_grad)
-        moments = dot(moment, high, ((1,), (0,))) + dot(moment, low, ((1,), (0,)))
-        color_grad = (
-            dot(r_high, w_high, ((1,), (0,))) + dot(r_low, w_high, ((1,), (0,))) + dot(r_high, w_low, ((1,), (0,)))
-        )
-        m_1, m_x, m_y, m_xx, m_xy, m_yy = [moments[k : k + 1, :] for k in range(6)]
-        s_x = m_x - u * m_1
-        s_y = m_y - v * m_1
-        s_xx = m_xx - u * (m_x + s_x)
-        s_yy = m_yy - v * (m_y + s_y)
-        s_xy = m_xy - u * m_y - v * s_x
+        q_x = -c_b * d_x
+        for y, at in enumerate(steps):
+            d_y = offset_y(p, y)
+            alpha = live * jnp.exp(q_xx + (q_x * d_y - 0.5 * c_c * d_y * d_y))
+            clear = jnp.log(1.0 - alpha)
+            alphas[p][at, :] = alpha
+            ratios[p][at, :] = alpha * jnp.exp(-clear)
+            high[p][at, :], low[p][at, :] = split(clear)
+    for p in range(passes):
+        sums[p][...] = dot(high[p][...], before, ((1,), (0,))) + dot(low[p][...], before, ((1,), (0,)))
+    for p in range(passes):
+        for at in steps:
+            weight = alphas[p][at, :] * jnp.exp(sums[p][at, :])
+            alphas[p][at, :] = weight
+            high[p][at, :], low[p][at, :] = split(weight)
+    residuals, pair_rows = [], []
+    for p in range(passes):
+        c_high, c_low = split(jnp.concatenate(lines[p][6:9], axis=0))
+        both = dot(jnp.concatenate([c_high, c_low], axis=0), high[p][...], ((1,), (1,)))
+        shown = both[0:3, :] + both[3:6, :] + dot(c_high, low[p][...], ((1,), (1,)))
+        residuals.append(split(shown - scene[p * SCENE : p * SCENE + 3, :]))
+        pair_rows.append(jnp.concatenate([c_high, c_low, c_high], axis=0))
+    color_grads = []
+    for p in range(passes):
+        r_high, r_low = residuals[p]
+        sums[p][...] = dot(jnp.concatenate([r_high, r_high, r_low], axis=0), pair_rows[p], ((0,), (0,)))
+        both = dot(jnp.concatenate([r_high, r_low], axis=0), high[p][...], ((1,), (0,)))
+        color_grads.append(both[0:3, :] + both[3:6, :] + dot(r_high, low[p][...], ((1,), (0,))))
+    for p in range(passes):
+        for at in steps:
+            pulled = alphas[p][at, :] * sums[p][at, :]
+            alphas[p][at, :] = pulled
+            high[p][at, :], low[p][at, :] = split(pulled)
+    for p in range(passes):
+        sums[p][...] = dot(high[p][...], after, ((1,), (0,))) + dot(low[p][...], after, ((1,), (0,)))
+    grads = []
+    for p in range(passes):
+        m_1 = m_y = m_yy = jnp.zeros((wide, entries), F32)
+        for y, at in enumerate(steps):
+            grad = alphas[p][at, :] - ratios[p][at, :] * sums[p][at, :]
+            d_y = offset_y(p, y)
+            grad_y = grad * d_y
+            m_1, m_y, m_yy = m_1 + grad, m_y + grad_y, m_yy + grad_y * d_y
+        d_x = spans[p]
+        m_x = m_1 * d_x
+        s_1, s_x, s_y, s_xx, s_xy, s_yy = [
+            jnp.sum(m, axis=0, keepdims=True) for m in (m_1, m_x, m_y, m_x * d_x, m_y * d_x, m_yy)
+        ]
+        _, _, c_a, c_b, c_c, base = lines[p][:6]
         grads.append(
             [
                 c_a * s_x + c_b * s_y,
@@ -440,10 +475,10 @@
                 -0.5 * s_xx,
                 -s_xy,
                 -0.5 * s_yy,
-                m_1 / base,
-                color_grad[0:1, :],
-                color_grad[1:2, :],
-                color_grad[2:3, :],
+                s_1 / base,
+                color_grads[p][0:1, :],
+                color_grads[p][1:2, :],
+                color_grads[p][2:3, :],
             ]
         )
 
@@ -471,22 +506,17 @@
         packets(g * GROUP, source[g * GROUP : (g + 1) * GROUP, :])
 
 
-def pull_kernel(passes, cams, tiles, rows, cap, aligned, got, inverse, raw, table, pos, scales, rots, opac, cols, total):
+def pull_kernel(
+    passes, cams, tiles, rows, cap, aligned, got, inverse, raw, table, kept,
+    pos, scales, rots, opac, cols, total, leaving, done,
+):
     views = passes * cams
     shape = (rows, LANES)
 
     def at(k):
         return raw[k * rows : (k + 1) * rows, :]
 
-    point = [at(k) for k in range(3)]
-    squares = [jnp.exp(2.0 * at(3 + k)) for k in range(3)]
-    spin, quat, quat_back = spin_of([at(6 + k) for k in range(4)])
-    cov = world_cov(spin, squares)
-
-    g_point = [jnp.zeros(shape, F32) for _ in range(3)]
-    g_cov = [[jnp.zeros(shape, F32) for _ in range(3)] for _ in range(3)]
-    g_opacity = jnp.zeros(shape, F32)
-    for view in range(views):
+    def fetcher(view):
         p, c = view // cams, view % cams
         slot = inverse[view * rows : (view + 1) * rows, :] - 1
         valid = slot >= 0
@@ -507,9 +537,40 @@
 
             return lax.fori_loop(0, tiles, one, jnp.zeros(shape, F32))
 
-        g = [fetch(f) for f in range(FIELDS)]
-        rotate, offset, center = camera_of(table, view, views, shape)
-        m, inv, main, at_x, at_y, t_x, t_y, w_x, w_y, conic = screen_of(point, cov, rotate, offset)
+        return fetch
+
+    def held(view, k):
+        start = (view * KEPT + k) * rows
+        return kept[start : start + rows, :]
+
+    fetchers = [fetcher(view) for view in range(views)]
+    shades = [[fetchers[view](6 + channel) for view in range(views)] for channel in range(3)]
+    for k in range(16):
+        basis = [held(view, KEPT - 16 + k) for view in range(views)] if k else None
+        for channel in range(3):
+            terms = shades[channel] if k == 0 else [basis[view] * shades[channel][view] for view in range(views)]
+            while len(terms) > 1:
+                terms = [sum(terms[n : n + 2][1:], terms[n]) for n in range(0, len(terms), 2)]
+            start = (11 + 3 * k + channel) * rows
+            total[start : start + rows, :] = terms[0] if k else SH_ZERO * terms[0]
+    for i in range(rows):
+        leaving[:, i * LANES : (i + 1) * LANES] = total[pl.ds(11 * rows + i, cols.shape[0], stride=rows), :]
+    copy = pltpu.make_async_copy(leaving, cols, done)
+    copy.start()
+
+    point = [at(k) for k in range(3)]
+    squares = [jnp.exp(2.0 * at(3 + k)) for k in range(3)]
+    spin, quat, quat_back = spin_of([at(6 + k) for k in range(4)])
+
+    g_point = [jnp.zeros(shape, F32) for _ in range(3)]
+    g_cov = [[jnp.zeros(shape, F32) for _ in range(3)] for _ in range(3)]
+    g_opacity = jnp.zeros(shape, F32)
+    for view in range(views):
+        g = [fetchers[view](f) for f in range(6)] + [shades[channel][view] for channel in range(3)]
+        rotate, _, _ = camera_of(table, view, views, shape)
+        inv, main, at_x, at_y = [held(view, k) for k in range(4)]
+        t_x, t_y, w_x, w_y, conic, direction = [[held(view, 4 + 3 * n + k) for k in range(3)] for n in range(6)]
+        length_back = held(view, 22)
         c_a, c_b, c_c = conic
         half = 0.5 * g[3]
         p00, p01 = g[2] * c_a + half * c_b, g[2] * c_b + half * c_c
@@ -528,16 +589,10 @@
         g_sx, g_sy = dot3(rotate[2], g_tx), dot3(rotate[2], g_ty)
         g_m0 = main * (g[0] - inv * g_sx)
         g_m1 = main * (g[1] - inv * g_sy)
-        g_m2 = -main * (
-            at_x * g[0] + at_y * g[1] + inv * g_main - 2.0 * inv * (at_x * g_sx + at_y * g_sy)
-        )
-        direction, length_back = direction_of(point, center)
-        basis = basis_of(*direction)
+        g_m2 = -main * (at_x * g[0] + at_y * g[1] + inv * g_main - 2.0 * inv * (at_x * g_sx + at_y * g_sy))
         g_basis = [None]
         for k in range(1, 16):
-            g_basis.append(
-                at(11 + 3 * k) * g[6] + at(12 + 3 * k) * g[7] + at(13 + 3 * k) * g[8]
-            )
+            g_basis.append(at(11 + 3 * k) * g[6] + at(12 + 3 * k) * g[7] + at(13 + 3 * k) * g[8])
         g_dir = basis_pull(*direction, g_basis)
         along = dot3(direction, g_dir)
         for j in range(3):
@@ -546,14 +601,6 @@
                 + (g_dir[j] - direction[j] * along) * length_back
             )
         g_opacity = g_opacity + g[5]
-        for k in range(16):
-            for channel in range(3):
-                term = SH_ZERO * g[6 + channel] if k == 0 else basis[k] * g[6 + channel]
-                start = (11 + 3 * k + channel) * rows
-                if view == 0:
-                    total[start : start + rows, :] = term
-                else:
-                    total[start : start + rows, :] += term
     for i in range(3):
         for j in range(i):
             g_cov[i][j] = g_cov[j][i]
@@ -581,25 +628,24 @@
     for k, value in enumerate(g_point + g_scales + g_rots):
         total[k * rows : (k + 1) * rows, :] = value
     base = 0
-    for ref in (pos, scales, rots, cols):
+    for ref in (pos, scales, rots):
         count = ref.shape[0]
-        if ref is cols:
-            base = 11
         for i in range(rows):
             ref[:, i * LANES : (i + 1) * LANES] = total[pl.ds(base * rows + i, count, stride=rows), :]
         base += count
+    copy.wait()
 
 
 def vmem(count):
     return [pl.BlockSpec(memory_space=pltpu.VMEM)] * count
 
 
-def call(kernel, outs, operands, in_specs=None, scratch=(), flops=1_000_000):
+def call(kernel, outs, operands, in_specs=None, scratch=(), flops=1_000_000, out_specs=None):
     return pl.pallas_call(
         kernel,
         out_shape=outs,
         in_specs=in_specs or vmem(len(operands)),
-        out_specs=jax.tree.map(lambda _: pl.BlockSpec(memory_space=pltpu.VMEM), outs),
+        out_specs=out_specs or jax.tree.map(lambda _: pl.BlockSpec(memory_space=pltpu.VMEM), outs),
         scratch_shapes=list(scratch),
         compiler_params=pltpu.CompilerParams(vmem_limit_bytes=32 << 20),
         cost_estimate=pl.CostEstimate(flops=flops, bytes_accessed=1 << 20, transcendentals=0),
@@ -637,16 +683,46 @@
         lines = x.reshape(owners, 1, -1)
         return lax.all_to_all(lines, axes, split_axis=0, concat_axis=0, tiled=True).reshape(x.shape)
 
+    whole, smem, far = [pl.BlockSpec(memory_space=space) for space in (pltpu.VMEM, pltpu.SMEM, pltpu.HBM)]
+    near = [
+        positions,
+        log_scales,
+        rotations,
+        opacities.reshape(rows, LANES),
+        colors,
+        cameras,
+        tile_lists,
+        targets.reshape(passes, 3, 1, pixels),
+        tile_counts.reshape(1, passes),
+        tile_ids.reshape(1, passes),
+    ]
     wanted_ids = call(
         functools.partial(ids_kernel, passes, cams, cap),
         jax.ShapeDtypeStruct((owners, LANES), jnp.int32),
-        [fetch_ids],
+        [pltpu.with_memory_space_constraint(fetch_ids, pltpu.HBM)],
+        in_specs=[far],
+        out_specs=far,
+        scratch=[
+            pltpu.VMEM(fetch_ids.shape, jnp.int32),
+            pltpu.VMEM((owners, LANES), jnp.int32),
+            pltpu.SemaphoreType.DMA,
+        ],
     )
     arrived = exchange(wanted_ids)
-    records, raw, table = call(
-        functools.partial(project_kernel, passes, cams, rows),
-        [shaped(views * FIELDS * rows, LANES), shaped(RAW * rows, LANES), shaped(TERMS * views, LANES)],
-        [positions, log_scales, rotations, opacities.reshape(rows, LANES), colors, cameras],
+    records, raw, table, kept, scene, source, lists = call(
+        functools.partial(project_kernel, passes, cams, rows, owners, cap),
+        [
+            shaped(views * FIELDS * rows, LANES),
+            shaped(RAW * rows, LANES),
+            shaped(TERMS * views, LANES),
+            shaped(views * KEPT * rows, LANES),
+            shaped(passes * SCENE, entries),
+            jax.ShapeDtypeStruct((owners, LANES), jnp.int32),
+            jax.ShapeDtypeStruct((passes, entries), jnp.int32),
+        ],
+        [pltpu.with_memory_space_constraint(x, pltpu.HBM) for x in near],
+        in_specs=[far] * len(near),
+        scratch=[pltpu.VMEM(x.shape, x.dtype) for x in near] + [pltpu.SemaphoreType.DMA((len(near),))],
     )
     packets, inverse = call(
         functools.partial(pick_kernel, passes, cams, tiles, rows, cap, aligned),
@@ -654,30 +730,19 @@
         [arrived, records],
     )
     fetched = exchange(packets)
-    smem = pl.BlockSpec(memory_space=pltpu.SMEM)
-    whole = vmem(1)[0]
     slot_grads = call(
         functools.partial(render_kernel, passes, owners, cap, entries, pixels),
         shaped(owners * SENT, LANES),
-        [
-            fetched,
-            tile_lists,
-            tile_counts.reshape(1, passes),
-            tile_ids.reshape(1, passes),
-            targets.reshape(passes, 3, 1, pixels),
-        ],
-        in_specs=[whole, whole, smem, smem, whole],
-        scratch=[
-            pltpu.VMEM((passes, pixels, entries), F32),
-            pltpu.VMEM((pixels, entries), F32),
-        ],
+        [fetched, lists, scene, source],
+        scratch=[pltpu.VMEM((pixels, entries), kind) for kind in (F32, F32, F32, BF16, BF16) for _ in range(passes)],
     )
     coming = exchange(slot_grads)
     g_pos, g_scales, g_rots, g_opac, g_cols = call(
         functools.partial(pull_kernel, passes, cams, tiles, rows, cap, aligned),
-        [shaped(3, columns), shaped(3, columns), shaped(4, columns), shaped(rows, LANES), shaped(48, columns)],
-        [coming, inverse, raw, table],
-        scratch=[pltpu.VMEM((RAW * rows, LANES), F32)],
+        [shaped(3, columns), shaped(3, columns), shaped(4, columns), shaped(rows, LANES), shaped(*colors.shape)],
+        [coming, inverse, raw, table, kept],
+        out_specs=[whole] * 4 + [far],
+        scratch=[pltpu.VMEM((RAW * rows, LANES), F32), pltpu.VMEM(colors.shape, F32), pltpu.SemaphoreType.DMA],
     )
     return (g_pos, g_scales, g_rots, g_opac.reshape(columns), g_cols)
 

time: 41.3 us -> 38.9 us (0.942)
  local copies, waits for them, and re-layouts: 2.38 us -> 0 us
    unnamed x22 -> x0, local copies, waits for them, and re-layouts: 2.38 us -> none
  transfers between devices with their start and end apart: 1 -> 1, of which waited for: 1 -> 1; matrix products, arithmetic and copies ran while one was open for 0% -> 0% of each run, Pallas kernels for 1% -> 4%
where the time goes in v2:
time: 38.9 us; the launch traced here: 38.6 us
  blocking collectives  18.5 us (48%)
  starting transfers between devices  7.3 us (19%)
  Pallas kernels  6.51 us (17%)
  waiting for transfers between devices  5.6 us (14%)
  between operations  0.66 us (2%)
    all_to_all x2, blocking collectives, exchange(): lax.all_to_all(lines, axes, split_axis=0, concat_axis=0, tiled=True)  18.5 us
    all_to_all x1, starting transfers between devices, exchange(): lax.all_to_all(lines, axes, split_axis=0, concat_axis=0, tiled=True)  7.3 us
    pallas_call x5, Pallas kernels, call(): pl.pallas_call(kernel, out_shape=outs, in_specs=in_specs or vmem(len(oper...  6.51 us
    all_to_all x1, waiting for transfers between devices, exchange(): lax.all_to_all(lines, axes, split_axis=0, concat_axis=0, tiled=True)  5.6 us
  transfers between devices with their start and end apart: 1, of which 1 were waited for; matrix products, arithmetic and copies ran while one was open for 0% of the time, Pallas kernels for 4%

profile of v2, /device:TPU:0, one launch (start us, length us, event | category | flops | bytes accessed | tf_op | source)
XLA Modules:
  0.0 38.6 jit_solution(3120373478364026879)
XLA Ops:
  0.6 1.4 %shard_map.146 = s32[32,128]{1,0:T(8,128)} custom-call(s32[2,1,1,4,8,32]{5,4,3,2,1,0:T(8,128)} %ids.1), custom_call_target="tpu_custom_call" | custom-call | flops 1000000 | bytes 1048576 | tf_op jit(solution)/shard_map/pallas_call | solution.py:644
  2.1 7.3 %all-to-all-start = ((s32[32,1,128]{2,1,0:T(1,128)}), s32[32,1,128]{2,1,0:T(1,128)S(1)}, u32[]{:S(2)}, u32[]{:S(2)}) async-start(s32[32,1,128]{2,1,0:T(1,128)} %bitcast.1), calls=%async_computation | async-start | bytes 32768 | tf_op jit(solution)/shard_map/all_to_all | solution.py:684
  9.4 1.5 %shard_map.147 = (f32[576,128]{1,0:T(8,128)S(1)}, f32[472,128]{1,0:T(8,128)S(1)}, f32[120,128]{1,0:T(8,128)S(1)}, f32[2432,128]{1,0:T(8,128)S(1)}, f32[12,256]{1...) custom-call(f32[3,1024]{1,0:T(4,128)} %far_pos.1, f32[3,1024]{1,0:T(4,128)} %far_scales.1, ...), custom_call_target="tpu_custom_call" | custom-call | flops 1000000 | bytes 1048576 | tf_op jit(solution)/shard_map/pallas_call | solution.py:644
  10.9 5.6 %all-to-all-done = s32[32,1,128]{2,1,0:T(1,128)S(1)} async-done(((s32[32,1,128]{2,1,0:T(1,128)}), s32[32,1,128]{2,1,0:T(1,128)S(1)}, u32[]{:S(2)}, u32[]{:S(2)}) %all-to-all-start) | async-done | bytes 16416 | tf_op jit(solution)/shard_map/all_to_all | solution.py:684
  16.5 0.4 %shard_map.148 = (f32[160,128]{1,0:T(8,128)S(1)}, s32[64,128]{1,0:T(8,128)S(1)}) custom-call(s32[32,128]{1,0:T(8,128)S(1)} %bitcast.17, f32[576,128]{1,0:T(8,128)S(1)} %get-tuple-element.19.rec), custom_call_target="tpu_custom_call" | custom-call | flops 1000000 | bytes 1048576 | tf_op jit(solution)/shard_map/pallas_call | solution.py:644
  16.9 9.3 %all_to_all.15 = f32[32,1,640]{2,1,0:T(1,128)S(1)} all-to-all(f32[32,1,640]{2,1,0:T(1,128)S(1)} %bitcast.16), channel_id=1, replica_groups=mesh['cam'=4,'tile'=8] {'cam','tile'}, dimensions={0} | all-to-all | bytes 163840 | tf_op jit(solution)/shard_map/all_to_all | solution.py:684
  26.1 1.5 %shard_map.149 = f32[160,128]{1,0:T(8,128)S(1)} custom-call(f32[160,128]{1,0:T(8,128)S(1)} %bitcast.14, s32[2,256]{1,0:T(2,128)S(1)} %get-tuple-element.21.lists, f32[12,256]{1,0:T(8,128)S(1)} %get-tuple-element.22.scene, s32[32,128]{1,0:T(8,128)S(1)} %get-tuple-element.23.source), custom_call_target="tpu_custom_call" | custom-call | flops 1000000 | bytes 1048576 | tf_op jit(solution)/shard_map/pallas_call | solution.py:644
  27.6 9.3 %all_to_all.16 = f32[32,1,640]{2,1,0:T(1,128)S(1)} all-to-all(f32[32,1,640]{2,1,0:T(1,128)S(1)} %bitcast.15), channel_id=1, replica_groups=mesh['cam'=4,'tile'=8] {'cam','tile'}, dimensions={0} | all-to-all | bytes 163840 | tf_op jit(solution)/shard_map/all_to_all | solution.py:684
  36.9 1.7 %shard_map.150 = (f32[3,1024]{1,0:T(4,128)}, f32[3,1024]{1,0:T(4,128)}, f32[4,1024]{1,0:T(4,128)}, f32[8,128]{1,0:T(8,128)}, f32[48,1024]{1,0:T(8,128)}) custom-call(f32[160,128]{1,0:T(8,128)S(1)} %bitcast.13, s32[64,128]{1,0:T(8,128)S(1)} %get-tuple-element.24.inverse, f32[472,128]{1,0:T(8,128)S(1)} %get-tuple-element.25.raw, ...), custom_call_target="tpu_custom_call" | custom-call | flops 1000000 | bytes 1048576 | tf_op jit(solution)/shard_map/pallas_call | solution.py:644
Async XLA Ops:
  2.1 14.4 %all-to-all-start = ((s32[32,1,128]{2,1,0:T(1,128)}), s32[32,1,128]{2,1,0:T(1,128)S(1)}, u32[]{:S(2)}, u32[]{:S(2)}) async-start(s32[32,1,128]{2,1,0:T(1,128)} %bitcast.1), calls=%async_computation | async-start | bytes 32768 | tf_op jit(solution)/shard_map/all_to_all | solution.py:684

commit v3 on v2

--- a/solution.py
+++ b/solution.py
@@ -50,6 +50,10 @@
     return high, (x - high.astype(F32)).astype(BF16)
 
 
+def parted(x):
+    return x & (LANES - 1), lax.shift_right_arithmetic(x, LANES.bit_length() - 1)
+
+
 def lane_pick(source, index):
     return jnp.take_along_axis(source, index, axis=1, mode="promise_in_bounds")
 
@@ -236,22 +240,24 @@
         place = jnp.broadcast_to(places[:, p : p + 1], (1, entries))
         for k, value in enumerate((place % 256 * 16 + 8, place // 256 * 16 + 8)):
             scene[p * SCENE + 4 + k : p * SCENE + 5 + k, :] = value.astype(F32)
-        chosen[p : p + 1, :] = lists[p, 0]
+        chosen[p : p + 1, :] = lists[p, 0] // cap
+        chosen[passes + p : passes + p + 1, :] = lists[p, 0] % cap + p * cap
     pair = (LANES, LANES)
     turned = lax.broadcasted_iota(jnp.int32, pair, 0)
     turned_p, turned_j = turned % HALF // cap, turned % cap
     entry = (lax.broadcasted_iota(jnp.int32, pair, 1) + 1).astype(F32)
     owner_row = lax.broadcasted_iota(jnp.int32, (owners, LANES), 0)
-    found = jnp.zeros((owners, LANES), jnp.int32)
-    for p in range(passes):
-        for h in range(entries // LANES):
+    halves = entries // LANES
+    found = jnp.full((owners, LANES), -LANES, jnp.int32)
+    for p in range(passes):
+        for h in range(halves):
             slot = lists[p, 0, :, h * LANES : (h + 1) * LANES]
             mine = jnp.where(jnp.broadcast_to(slot // cap, (owners, LANES)) == owner_row, 1.0, 0.0).astype(BF16)
             here = jnp.where(
                 (jnp.broadcast_to(slot % cap, pair) == turned_j) & (turned_p == p), entry, 0.0
             ).astype(BF16)
             hit = dot(mine, here, ((1,), (1,)))
-            found = jnp.where(hit > 0.5, hit.astype(jnp.int32) + h * LANES, found)
+            found = jnp.where(hit > 0.5, hit.astype(jnp.int32) + ((p * halves + h) * LANES - 1), found)
     source[...] = found
 
     copies[-1].wait()
@@ -294,8 +300,7 @@
     lane_p, _ = lane_pass(shape, cap)
 
     def packets(first, c):
-        asked = ids[pl.ds(first, GROUP), :]
-        low, high = asked % LANES, asked // LANES
+        low, high = parted(ids[pl.ds(first, GROUP), :])
         if aligned:
             blocks = [jnp.broadcast_to(high[:, p * cap : p * cap + 1], shape) for p in range(passes)]
 
@@ -332,8 +337,8 @@
 
     square = (LANES, LANES)
     column = lax.broadcasted_iota(jnp.int32, square, 0)
-    _, lane_j = lane_pass(square, cap)
-    place = (lane_j + 1 + lax.broadcasted_iota(jnp.int32, square, 1) // HALF * cap).astype(F32)
+    turn = lax.broadcasted_iota(jnp.int32, square, 1)
+    place = (turn % HALF + 1 + turn // HALF * LANES).astype(F32)
     wide = (passes * rows, LANES)
     wide_lane = lax.broadcasted_iota(jnp.int32, wide, 1)
     key = lax.broadcasted_iota(jnp.int32, wide, 0)
@@ -341,13 +346,15 @@
     line_lane = lax.broadcasted_iota(jnp.int32, (1, LANES), 1)
 
     def two(c, t, found):
-        asked = jnp.where(line_lane < HALF, ids[pl.ds(c * tiles + t, 1), :], ids[pl.ds(c * tiles + t + 1, 1), :])
-        low = jnp.broadcast_to(asked % LANES, square)
-        high = jnp.broadcast_to(asked // LANES, wide)
+        low, high = parted(
+            jnp.where(line_lane < HALF, ids[pl.ds(c * tiles + t, 1), :], ids[pl.ds(c * tiles + t + 1, 1), :])
+        )
+        low = jnp.broadcast_to(low, square)
+        high = jnp.broadcast_to(high, wide)
         match = jnp.where(low == column, place, 0.0).astype(BF16)
         owner = jnp.where(high + lane_key == key, 1.0, 0.0).astype(BF16)
         hit = dot(owner, match, ((1,), (1,)))
-        return jnp.where(hit > 0.5, hit.astype(jnp.int32) + t * cap, found)
+        return jnp.where(hit > 0.5, hit.astype(jnp.int32) + t * LANES, found)
 
     for c in range(cams):
         found = jnp.zeros(wide, jnp.int32)
@@ -372,9 +379,9 @@
     slot_owner, slot_lane = [], []
     for p in range(passes):
         for h in range(halves):
-            slot = jnp.broadcast_to(lists[p : p + 1, h * LANES : (h + 1) * LANES], shape)
-            slot_owner.append(slot // cap)
-            slot_lane.append(slot % cap + p * cap)
+            part = slice(h * LANES, (h + 1) * LANES)
+            slot_owner.append(jnp.broadcast_to(lists[p : p + 1, part], shape))
+            slot_lane.append(jnp.broadcast_to(lists[passes + p : passes + p + 1, part], shape))
     total = passes * halves
 
     def gather(g, found):
@@ -483,17 +490,14 @@
         )
 
     def packets(first, origin):
-        origin = origin - 1
-        which = jnp.where(origin < 0, -1, origin // LANES)
-        index = jnp.maximum(origin, 0) % LANES
-        own_p, _ = lane_pass(shape, cap)
+        index, which = parted(origin)
 
         def pick(f):
             found = jnp.zeros(shape, F32)
             for p in range(passes):
                 for h in range(halves):
                     line = jnp.broadcast_to(grads[p][f][:, h * LANES : (h + 1) * LANES], shape)
-                    found = jnp.where((which == h) & (own_p == p), lane_pick(line, index), found)
+                    found = jnp.where(which == p * halves + h, lane_pick(line, index), found)
             return found
 
         for r in range(SENT):
@@ -508,7 +512,7 @@
 
 def pull_kernel(
     passes, cams, tiles, rows, cap, aligned, got, inverse, raw, table, kept,
-    pos, scales, rots, opac, cols, total, leaving, done,
+    far_pos, far_scales, far_rots, far_opac, far_cols, total, pos, scales, rots, opac, cols, done,
 ):
     views = passes * cams
     shape = (rows, LANES)
@@ -520,16 +524,17 @@
         p, c = view // cams, view % cams
         slot = inverse[view * rows : (view + 1) * rows, :] - 1
         valid = slot >= 0
-        slot = jnp.maximum(slot, 0)
-        slot_t, slot_lane = slot // cap, slot % cap + p * cap
+        slot_lane, slot_t = parted(jnp.maximum(slot, 0))
         if aligned:
             row_t = jnp.broadcast_to(jnp.max(slot_t, axis=1, keepdims=True), shape)
+        turned = {}
 
         def fetch(f):
             row, shift = f // 2, f % 2 * HALF
             if aligned:
-                lines = got[pl.ds(c * tiles * SENT + row, tiles, stride=SENT), :]
-                return jnp.where(valid, lane_pick(row_pick(lines, row_t), slot_lane + shift), 0.0)
+                if row not in turned:
+                    turned[row] = row_pick(got[pl.ds(c * tiles * SENT + row, tiles, stride=SENT), :], row_t)
+                return jnp.where(valid, lane_pick(turned[row], slot_lane + shift), 0.0)
 
             def one(t, found):
                 line = jnp.broadcast_to(got[pl.ds((c * tiles + t) * SENT + row, 1), :], shape)
@@ -545,6 +550,13 @@
 
     fetchers = [fetcher(view) for view in range(views)]
     shades = [[fetchers[view](6 + channel) for view in range(views)] for channel in range(3)]
+    copies = []
+
+    def send(near, away):
+        copies.append(pltpu.make_async_copy(near, away, done.at[len(copies)]))
+        copies[-1].start()
+
+    sent = 0
     for k in range(16):
         basis = [held(view, KEPT - 16 + k) for view in range(views)] if k else None
         for channel in range(3):
@@ -553,10 +565,12 @@
                 terms = [sum(terms[n : n + 2][1:], terms[n]) for n in range(0, len(terms), 2)]
             start = (11 + 3 * k + channel) * rows
             total[start : start + rows, :] = terms[0] if k else SH_ZERO * terms[0]
-    for i in range(rows):
-        leaving[:, i * LANES : (i + 1) * LANES] = total[pl.ds(11 * rows + i, cols.shape[0], stride=rows), :]
-    copy = pltpu.make_async_copy(leaving, cols, done)
-    copy.start()
+        ready = (3 * k + 3) // 16 * 16
+        if ready > sent:
+            for i in range(rows):
+                cols[sent:ready, i * LANES : (i + 1) * LANES] = total[pl.ds((11 + sent) * rows + i, ready - sent, stride=rows), :]
+            send(cols.at[pl.ds(sent, ready - sent), :], far_cols.at[pl.ds(sent, ready - sent), :])
+            sent = ready
 
     point = [at(k) for k in range(3)]
     squares = [jnp.exp(2.0 * at(3 + k)) for k in range(3)]
@@ -633,7 +647,10 @@
         for i in range(rows):
             ref[:, i * LANES : (i + 1) * LANES] = total[pl.ds(base * rows + i, count, stride=rows), :]
         base += count
-    copy.wait()
+    for near, away in ((pos, far_pos), (scales, far_scales), (rots, far_rots), (opac, far_opac)):
+        send(near, away)
+    for copy in copies:
+        copy.wait()
 
 
 def vmem(count):
@@ -718,7 +735,7 @@
             shaped(views * KEPT * rows, LANES),
             shaped(passes * SCENE, entries),
             jax.ShapeDtypeStruct((owners, LANES), jnp.int32),
-            jax.ShapeDtypeStruct((passes, entries), jnp.int32),
+            jax.ShapeDtypeStruct((2 * passes, entries), jnp.int32),
         ],
         [pltpu.with_memory_space_constraint(x, pltpu.HBM) for x in near],
         in_specs=[far] * len(near),
@@ -741,8 +758,10 @@
         functools.partial(pull_kernel, passes, cams, tiles, rows, cap, aligned),
         [shaped(3, columns), shaped(3, columns), shaped(4, columns), shaped(rows, LANES), shaped(*colors.shape)],
         [coming, inverse, raw, table, kept],
-        out_specs=[whole] * 4 + [far],
-        scratch=[pltpu.VMEM((RAW * rows, LANES), F32), pltpu.VMEM(colors.shape, F32), pltpu.SemaphoreType.DMA],
+        out_specs=[far] * 5,
+        scratch=[pltpu.VMEM((RAW * rows, LANES), F32)]
+        + [pltpu.VMEM(x.shape, F32) for x in near[:5]]
+        + [pltpu.SemaphoreType.DMA((7,))],
     )
     return (g_pos, g_scales, g_rots, g_opac.reshape(columns), g_cols)
 

time: 38.9 us -> 38.7 us (level)
  no operation moved by 1% of the time
where the time goes in v3:
time: 38.7 us; the launch traced here: 38.4 us
  blocking collectives  18.5 us (48%)
  starting transfers between devices  7.3 us (19%)
  Pallas kernels  6.29 us (16%)
  waiting for transfers between devices  5.59 us (14%)
  between operations  0.66 us (2%)
    all_to_all x2, blocking collectives, exchange(): lax.all_to_all(lines, axes, split_axis=0, concat_axis=0, tiled=True)  18.5 us
    all_to_all x1, starting transfers between devices, exchange(): lax.all_to_all(lines, axes, split_axis=0, concat_axis=0, tiled=True)  7.3 us
    pallas_call x5, Pallas kernels, call(): pl.pallas_call(kernel, out_shape=outs, in_specs=in_specs or vmem(len(oper...  6.29 us
    all_to_all x1, waiting for transfers between devices, exchange(): lax.all_to_all(lines, axes, split_axis=0, concat_axis=0, tiled=True)  5.59 us
  transfers between devices with their start and end apart: 1, of which 1 were waited for; matrix products, arithmetic and copies ran while one was open for 0% of the time, Pallas kernels for 4%

profile of v3, /device:TPU:0, one launch (start us, length us, event | category | flops | bytes accessed | tf_op | source)
XLA Modules:
  0.0 38.4 jit_solution(6304055748028110408)
XLA Ops:
  0.6 1.4 %shard_map.146 = s32[32,128]{1,0:T(8,128)} custom-call(s32[2,1,1,4,8,32]{5,4,3,2,1,0:T(8,128)} %ids.1), custom_call_target="tpu_custom_call" | custom-call | flops 1000000 | bytes 1048576 | tf_op jit(solution)/shard_map/pallas_call | solution.py:661
  2.1 7.3 %all-to-all-start = ((s32[32,1,128]{2,1,0:T(1,128)}), s32[32,1,128]{2,1,0:T(1,128)S(1)}, u32[]{:S(2)}, u32[]{:S(2)}) async-start(s32[32,1,128]{2,1,0:T(1,128)} %bitcast.1), calls=%async_computation | async-start | bytes 32768 | tf_op jit(solution)/shard_map/all_to_all | solution.py:701
  9.4 1.5 %shard_map.147 = (f32[576,128]{1,0:T(8,128)S(1)}, f32[472,128]{1,0:T(8,128)S(1)}, f32[120,128]{1,0:T(8,128)S(1)}, f32[2432,128]{1,0:T(8,128)S(1)}, f32[12,256]{1...) custom-call(f32[3,1024]{1,0:T(4,128)} %far_pos.1, f32[3,1024]{1,0:T(4,128)} %far_scales.1, ...), custom_call_target="tpu_custom_call" | custom-call | flops 1000000 | bytes 1048576 | tf_op jit(solution)/shard_map/pallas_call | solution.py:661
  10.9 5.6 %all-to-all-done = s32[32,1,128]{2,1,0:T(1,128)S(1)} async-done(((s32[32,1,128]{2,1,0:T(1,128)}), s32[32,1,128]{2,1,0:T(1,128)S(1)}, u32[]{:S(2)}, u32[]{:S(2)}) %all-to-all-start) | async-done | bytes 16416 | tf_op jit(solution)/shard_map/all_to_all | solution.py:701
  16.5 0.4 shard_map.148
  16.8 9.3 %all_to_all.15 = f32[32,1,640]{2,1,0:T(1,128)S(1)} all-to-all(f32[32,1,640]{2,1,0:T(1,128)S(1)} %bitcast.16), channel_id=1, replica_groups=mesh['cam'=4,'tile'=8] {'cam','tile'}, dimensions={0} | all-to-all | bytes 163840 | tf_op jit(solution)/shard_map/all_to_all | solution.py:701
  26.1 1.5 %shard_map.149 = f32[160,128]{1,0:T(8,128)S(1)} custom-call(f32[160,128]{1,0:T(8,128)S(1)} %bitcast.14, s32[4,256]{1,0:T(4,128)S(1)} %get-tuple-element.21.lists, f32[12,256]{1,0:T(8,128)S(1)} %get-tuple-element.22.scene, s32[32,128]{1,0:T(8,128)S(1)} %get-tuple-element.23.source), custom_call_target="tpu_custom_call" | custom-call | flops 1000000 | bytes 1048576 | tf_op jit(solution)/shard_map/pallas_call | solution.py:661
  27.6 9.3 %all_to_all.16 = f32[32,1,640]{2,1,0:T(1,128)S(1)} all-to-all(f32[32,1,640]{2,1,0:T(1,128)S(1)} %bitcast.15), channel_id=1, replica_groups=mesh['cam'=4,'tile'=8] {'cam','tile'}, dimensions={0} | all-to-all | bytes 163840 | tf_op jit(solution)/shard_map/all_to_all | solution.py:701
  36.9 1.5 %shard_map.150 = (f32[3,1024]{1,0:T(4,128)}, f32[3,1024]{1,0:T(4,128)}, f32[4,1024]{1,0:T(4,128)}, f32[8,128]{1,0:T(8,128)}, f32[48,1024]{1,0:T(8,128)}) custom-call(f32[160,128]{1,0:T(8,128)S(1)} %bitcast.13, s32[64,128]{1,0:T(8,128)S(1)} %get-tuple-element.24.inverse, f32[472,128]{1,0:T(8,128)S(1)} %get-tuple-element.25.raw, ...), custom_call_target="tpu_custom_call" | custom-call | flops 1000000 | bytes 1048576 | tf_op jit(solution)/shard_map/pallas_call | solution.py:661
Async XLA Ops:
  2.1 14.4 %all-to-all-start = ((s32[32,1,128]{2,1,0:T(1,128)}), s32[32,1,128]{2,1,0:T(1,128)S(1)}, u32[]{:S(2)}, u32[]{:S(2)}) async-start(s32[32,1,128]{2,1,0:T(1,128)} %bitcast.1), calls=%async_computation | async-start | bytes 32768 | tf_op jit(solution)/shard_map/all_to_all | solution.py:701

commit v4 on v3

--- a/solution.py
+++ b/solution.py
@@ -34,7 +34,8 @@
 SENT = 5
 GROUP = 8
 RAW = 59
-KEPT = 38
+KEPT = 42
+SHADE = 18
 SCENE = 6
 TERMS = 15
 F32 = jnp.float32
@@ -186,18 +187,19 @@
 
 
 def project_kernel(
-    passes, cams, rows, owners, cap, far_pos, far_scales, far_rots, far_opac, far_cols, far_cam, far_lists, far_wanted,
-    far_counts, far_places, rec, raw, table, kept, scene, source, chosen,
-    pos, scales, rots, opac, cols, cam, lists, wanted, counts, places, done,
+    passes, cams, rows, owners, cap, cols, far_pos, far_scales, far_rots, far_opac, far_cam, far_lists, far_wanted, far_counts, far_places,
+    rec, raw, kept, scene, source, chosen, table, pos, scales, rots, opac, cam, lists, wanted, counts, places, done,
 ):
     views = passes * cams
     shape = (rows, LANES)
-    fars = (far_cam, far_pos, far_scales, far_rots, far_opac, far_lists, far_wanted, far_counts, far_places, far_cols)
-    nears = (cam, pos, scales, rots, opac, lists, wanted, counts, places, cols)
-    copies = [pltpu.make_async_copy(a, b, done.at[k]) for k, (a, b) in enumerate(zip(fars, nears))]
+    fars = (far_cam, far_pos, far_scales, far_rots, far_opac, far_lists, far_wanted, far_counts, far_places)
+    nears = (cam, pos, scales, rots, opac, lists, wanted, counts, places)
+    copies = [pltpu.make_async_copy(away, near, done.at[k]) for k, (away, near) in enumerate(zip(fars, nears))]
     for copy in copies:
         copy.start()
-    for copy in copies[:-1]:
+    for i in range(rows):
+        raw[pl.ds(11 * rows + i, cols.shape[0], stride=rows), :] = cols[:, i * LANES : (i + 1) * LANES]
+    for copy in copies[:5]:
         copy.wait()
     camera_rows(cam, table, passes, cams)
     base = 0
@@ -219,6 +221,7 @@
     spin, _, _ = spin_of([at(6 + k) for k in range(4)])
     cov = world_cov(spin, squares)
     opacity = 1.0 / (1.0 + jnp.exp(-at(10)))
+    sight = []
     for view in range(views):
         rotate, offset, center = camera_of(table, view, views, shape)
         _, inv, main, at_x, at_y, t_x, t_y, w_x, w_y, conic = screen_of(point, cov, rotate, offset)
@@ -227,9 +230,24 @@
         fields = [FOCAL * at_x + CENTER_X, FOCAL * at_y + CENTER_Y, conic[0], conic[1], conic[2], opacity]
         for f, value in enumerate(fields):
             put(rec, view * FIELDS + f, value)
-        for k, value in enumerate([inv, main, at_x, at_y, *t_x, *t_y, *w_x, *w_y, *conic, *direction, back, *basis[1:]]):
+        r_x, r_y = [[dot3(rotate[i], w) for i in range(3)] for w in (w_x, w_y)]
+        moves = []
+        for g_main, g_sx, g_sy in (
+            (2.0 * r_x[0], 2.0 * r_x[2], 0.0),
+            (r_y[0] + r_x[1], r_y[2], r_x[2]),
+            (2.0 * r_y[1], 0.0, 2.0 * r_y[2]),
+        ):
+            g_m = [g_sx, g_sy, g_main - 2.0 * (at_x * g_sx + at_y * g_sy)]
+            size = -main * inv
+            moves += [size * (rotate[0][j] * g_m[0] + rotate[1][j] * g_m[1] + rotate[2][j] * g_m[2]) for j in range(3)]
+        sight.append((direction, back))
+        for k, value in enumerate([*t_x, *t_y, *conic, *moves]):
             put(kept, view * KEPT + k, value)
-
+        for k in range(1, 16):
+            put(kept, view * KEPT + KEPT - 16 + k, basis[k])
+
+    for copy in copies[5:]:
+        copy.wait()
     entries, pixels = lists.shape[-1], wanted.shape[-1]
     entry_row = lax.broadcasted_iota(jnp.int32, (1, entries), 1)
     for p in range(passes):
@@ -260,9 +278,6 @@
             found = jnp.where(hit > 0.5, hit.astype(jnp.int32) + ((p * halves + h) * LANES - 1), found)
     source[...] = found
 
-    copies[-1].wait()
-    for i in range(rows):
-        raw[pl.ds(11 * rows + i, cols.shape[0], stride=rows), :] = cols[:, i * LANES : (i + 1) * LANES]
     for channel in range(3):
         totals = [0.5 + SH_ZERO * at(11 + channel)] * views
         for k in range(1, 16):
@@ -272,6 +287,13 @@
                 totals[view] = totals[view] + kept[start : start + rows, :] * color
         for view in range(views):
             put(rec, view * FIELDS + 6 + channel, totals[view])
+    for view in range(views):
+        direction, back = sight[view]
+        for channel in range(3):
+            slope = basis_pull(*direction, [at(11 + 3 * k + channel) for k in range(16)])
+            along = dot3(direction, slope)
+            for j in range(3):
+                put(kept, view * KEPT + SHADE + 3 * channel + j, (slope[j] - direction[j] * along) * back)
 
 
 def lane_pass(shape, cap):
@@ -279,30 +301,46 @@
     return lane // cap, lane % cap
 
 
-def ids_kernel(passes, cams, cap, ids, out, landed, lines, done):
-    copy = pltpu.make_async_copy(ids, landed, done)
-    copy.start()
-    copy.wait()
+def ids_kernel(passes, cams, cap, ids, *refs):
+    count = (len(refs) - 6) // 2
+    sources, out, results = refs[:count], refs[count], refs[count + 1 : 2 * count + 1]
+    landed, lines, ids_done, out_done, done = refs[2 * count + 1 :]
+    first = pltpu.make_async_copy(ids, landed, ids_done)
+    first.start()
+    copies = [pltpu.make_async_copy(source, result, done.at[k]) for k, (source, result) in enumerate(zip(sources, results))]
+    for copy in copies:
+        copy.start()
+    first.wait()
     for c in range(cams):
         parts = [landed[p, 0, 0, c] for p in range(passes)]
         tiles = parts[0].shape[0]
         if passes * cap < HALF:
             parts.append(jnp.zeros((tiles, HALF - passes * cap), jnp.int32))
         lines[c * tiles : (c + 1) * tiles, :] = jnp.concatenate(parts + parts, axis=1)
-    copy = pltpu.make_async_copy(lines, out, done)
-    copy.start()
-    copy.wait()
-
-
-def pick_kernel(passes, cams, tiles, rows, cap, aligned, ids, rec, out, inverse):
+    last = pltpu.make_async_copy(lines, out, out_done)
+    last.start()
+    for copy in copies:
+        copy.wait()
+    last.wait()
+
+
+def pick_kernel(passes, cams, tiles, rows, cap, aligned, ids, rec, out, inverse, turns):
     shape = (GROUP, LANES)
     lane = lax.broadcasted_iota(jnp.int32, shape, 1)
+    sub = lax.broadcasted_iota(jnp.int32, shape, 0)
     lane_p, _ = lane_pass(shape, cap)
+    if not aligned:
+        turns[...] = jnp.zeros(turns.shape, jnp.int32)
 
     def packets(first, c):
         low, high = parted(ids[pl.ds(first, GROUP), :])
         if aligned:
             blocks = [jnp.broadcast_to(high[:, p * cap : p * cap + 1], shape) for p in range(passes)]
+            for p in range(passes):
+                turn = jnp.zeros(shape, jnp.int32)
+                for t in range(1, tiles):
+                    turn = jnp.where(jnp.broadcast_to(blocks[p][t : t + 1, :], shape) == sub, t, turn)
+                turns[(p * cams + c) * rows : (p * cams + c + 1) * rows, :] = turn
 
         def pick(f):
             found = jnp.zeros(shape, F32)
@@ -401,8 +439,7 @@
         fields = lax.fori_loop(0, owners // GROUP, gather, fields)
     fields = [jnp.sum(x, axis=0, keepdims=True) for x in fields]
 
-    square = (entries, entries)
-    row_at, column_at = lax.broadcasted_iota(jnp.int32, square, 0), lax.broadcasted_iota(jnp.int32, square, 1)
+    row_at, column_at = [lax.broadcasted_iota(jnp.int32, (entries, entries), k) for k in range(2)]
     before = jnp.where(row_at < column_at, 1.0, 0.0).astype(BF16)
     after = jnp.where(row_at > column_at, 1.0, 0.0).astype(BF16)
     column_x = lax.broadcasted_iota(jnp.int32, (wide, entries), 0).astype(F32) - 7.5
@@ -511,7 +548,7 @@
 
 
 def pull_kernel(
-    passes, cams, tiles, rows, cap, aligned, got, inverse, raw, table, kept,
+    passes, cams, tiles, rows, cap, aligned, got, inverse, turns, raw, kept,
     far_pos, far_scales, far_rots, far_opac, far_cols, total, pos, scales, rots, opac, cols, done,
 ):
     views = passes * cams
@@ -525,8 +562,7 @@
         slot = inverse[view * rows : (view + 1) * rows, :] - 1
         valid = slot >= 0
         slot_lane, slot_t = parted(jnp.maximum(slot, 0))
-        if aligned:
-            row_t = jnp.broadcast_to(jnp.max(slot_t, axis=1, keepdims=True), shape)
+        row_t = turns[view * rows : (view + 1) * rows, :]
         turned = {}
 
         def fetch(f):
@@ -572,7 +608,6 @@
             send(cols.at[pl.ds(sent, ready - sent), :], far_cols.at[pl.ds(sent, ready - sent), :])
             sent = ready
 
-    point = [at(k) for k in range(3)]
     squares = [jnp.exp(2.0 * at(3 + k)) for k in range(3)]
     spin, quat, quat_back = spin_of([at(6 + k) for k in range(4)])
 
@@ -581,10 +616,7 @@
     g_opacity = jnp.zeros(shape, F32)
     for view in range(views):
         g = [fetchers[view](f) for f in range(6)] + [shades[channel][view] for channel in range(3)]
-        rotate, _, _ = camera_of(table, view, views, shape)
-        inv, main, at_x, at_y = [held(view, k) for k in range(4)]
-        t_x, t_y, w_x, w_y, conic, direction = [[held(view, 4 + 3 * n + k) for k in range(3)] for n in range(6)]
-        length_back = held(view, 22)
+        t_x, t_y, conic, m_xx, m_xy, m_yy, s_r, s_g, s_b = [[held(view, 3 * n + k) for k in range(3)] for n in range(9)]
         c_a, c_b, c_c = conic
         half = 0.5 * g[3]
         p00, p01 = g[2] * c_a + half * c_b, g[2] * c_b + half * c_c
@@ -597,23 +629,10 @@
         for i in range(3):
             for j in range(i, 3):
                 g_cov[i][j] = g_cov[i][j] + (t_x[i] * left[j] + t_y[i] * right[j])
-        g_tx = [2.0 * (g_xx * w_x[i] + g_xy * w_y[i]) for i in range(3)]
-        g_ty = [2.0 * (g_yy * w_y[i] + g_xy * w_x[i]) for i in range(3)]
-        g_main = dot3(rotate[0], g_tx) + dot3(rotate[1], g_ty)
-        g_sx, g_sy = dot3(rotate[2], g_tx), dot3(rotate[2], g_ty)
-        g_m0 = main * (g[0] - inv * g_sx)
-        g_m1 = main * (g[1] - inv * g_sy)
-        g_m2 = -main * (at_x * g[0] + at_y * g[1] + inv * g_main - 2.0 * inv * (at_x * g_sx + at_y * g_sy))
-        g_basis = [None]
-        for k in range(1, 16):
-            g_basis.append(at(11 + 3 * k) * g[6] + at(12 + 3 * k) * g[7] + at(13 + 3 * k) * g[8])
-        g_dir = basis_pull(*direction, g_basis)
-        along = dot3(direction, g_dir)
+        pulls = ((t_x, g[0]), (t_y, g[1]), (m_xx, g_xx), (m_xy, 2.0 * g_xy), (m_yy, g_yy), (s_r, g[6]), (s_g, g[7]), (s_b, g[8]))
         for j in range(3):
-            g_point[j] = g_point[j] + (
-                rotate[0][j] * g_m0 + rotate[1][j] * g_m1 + rotate[2][j] * g_m2
-                + (g_dir[j] - direction[j] * along) * length_back
-            )
+            for slope, value in pulls:
+                g_point[j] = g_point[j] + slope[j] * value
         g_opacity = g_opacity + g[5]
     for i in range(3):
         for j in range(i):
@@ -701,49 +720,54 @@
         return lax.all_to_all(lines, axes, split_axis=0, concat_axis=0, tiled=True).reshape(x.shape)
 
     whole, smem, far = [pl.BlockSpec(memory_space=space) for space in (pltpu.VMEM, pltpu.SMEM, pltpu.HBM)]
-    near = [
+    near = [colors]
+    wanted_ids, *near = call(
+        functools.partial(ids_kernel, passes, cams, cap),
+        [jax.ShapeDtypeStruct((owners, LANES), jnp.int32)]
+        + [pltpu.VMEM(x.shape, x.dtype) for x in near],
+        [pltpu.with_memory_space_constraint(x, pltpu.HBM) for x in (fetch_ids, *near)],
+        in_specs=[far] * (1 + len(near)),
+        out_specs=[far] + [whole] * len(near),
+        scratch=[
+            pltpu.VMEM(fetch_ids.shape, jnp.int32),
+            pltpu.VMEM((owners, LANES), jnp.int32),
+            pltpu.SemaphoreType.DMA,
+            pltpu.SemaphoreType.DMA,
+            pltpu.SemaphoreType.DMA((len(near),)),
+        ],
+    )
+    arrived = exchange(wanted_ids)
+    small = [
         positions,
         log_scales,
         rotations,
         opacities.reshape(rows, LANES),
-        colors,
         cameras,
         tile_lists,
         targets.reshape(passes, 3, 1, pixels),
         tile_counts.reshape(1, passes),
         tile_ids.reshape(1, passes),
     ]
-    wanted_ids = call(
-        functools.partial(ids_kernel, passes, cams, cap),
-        jax.ShapeDtypeStruct((owners, LANES), jnp.int32),
-        [pltpu.with_memory_space_constraint(fetch_ids, pltpu.HBM)],
-        in_specs=[far],
-        out_specs=far,
-        scratch=[
-            pltpu.VMEM(fetch_ids.shape, jnp.int32),
-            pltpu.VMEM((owners, LANES), jnp.int32),
-            pltpu.SemaphoreType.DMA,
-        ],
-    )
-    arrived = exchange(wanted_ids)
-    records, raw, table, kept, scene, source, lists = call(
+    records, raw, kept, scene, source, lists = call(
         functools.partial(project_kernel, passes, cams, rows, owners, cap),
         [
             shaped(views * FIELDS * rows, LANES),
             shaped(RAW * rows, LANES),
-            shaped(TERMS * views, LANES),
             shaped(views * KEPT * rows, LANES),
             shaped(passes * SCENE, entries),
             jax.ShapeDtypeStruct((owners, LANES), jnp.int32),
             jax.ShapeDtypeStruct((2 * passes, entries), jnp.int32),
         ],
-        [pltpu.with_memory_space_constraint(x, pltpu.HBM) for x in near],
-        in_specs=[far] * len(near),
-        scratch=[pltpu.VMEM(x.shape, x.dtype) for x in near] + [pltpu.SemaphoreType.DMA((len(near),))],
+        [*near, *[pltpu.with_memory_space_constraint(x, pltpu.HBM) for x in small]],
+        in_specs=[whole] * 1 + [far] * len(small),
+        scratch=[pltpu.VMEM((TERMS * views, LANES), F32)]
+        + [pltpu.VMEM(x.shape, x.dtype) for x in small]
+        + [pltpu.SemaphoreType.DMA((len(small),))],
     )
-    packets, inverse = call(
+    codes = jax.ShapeDtypeStruct((views * rows, LANES), jnp.int32)
+    packets, inverse, turns = call(
         functools.partial(pick_kernel, passes, cams, tiles, rows, cap, aligned),
-        [shaped(owners * SENT, LANES), jax.ShapeDtypeStruct((views * rows, LANES), jnp.int32)],
+        [shaped(owners * SENT, LANES), codes, codes],
         [arrived, records],
     )
     fetched = exchange(packets)
@@ -757,10 +781,10 @@
     g_pos, g_scales, g_rots, g_opac, g_cols = call(
         functools.partial(pull_kernel, passes, cams, tiles, rows, cap, aligned),
         [shaped(3, columns), shaped(3, columns), shaped(4, columns), shaped(rows, LANES), shaped(*colors.shape)],
-        [coming, inverse, raw, table, kept],
+        [coming, inverse, turns, raw, kept],
         out_specs=[far] * 5,
         scratch=[pltpu.VMEM((RAW * rows, LANES), F32)]
-        + [pltpu.VMEM(x.shape, F32) for x in near[:5]]
+        + [pltpu.VMEM(shape, F32) for shape in ((3, columns), (3, columns), (4, columns), (rows, LANES), colors.shape)]
         + [pltpu.SemaphoreType.DMA((7,))],
     )
     return (g_pos, g_scales, g_rots, g_opac.reshape(columns), g_cols)

time: 38.7 us -> 38.3 us (0.990)
  waiting for transfers between devices: 5.59 us -> 5.05 us
    all_to_all x1, waiting for transfers between devices: 5.59 us -> 5.05 us  [exchange(): lax.all_to_all(lines, axes, split_axis=0, concat_axis=0, tiled=True)]
  transfers between devices with their start and end apart: 1 -> 1, of which waited for: 1 -> 1; matrix products, arithmetic and copies ran while one was open for 0% -> 0% of each run, Pallas kernels for 4% -> 5%
where the time goes in v4:
time: 38.3 us; the launch traced here: 38 us
  blocking collectives  18.5 us (48%)
  starting transfers between devices  7.3 us (19%)
  Pallas kernels  6.46 us (17%)
  waiting for transfers between devices  5.05 us (13%)
  between operations  0.66 us (2%)
    all_to_all x2, blocking collectives, exchange(): lax.all_to_all(lines, axes, split_axis=0, concat_axis=0, tiled=True)  18.5 us
    all_to_all x1, starting transfers between devices, exchange(): lax.all_to_all(lines, axes, split_axis=0, concat_axis=0, tiled=True)  7.3 us
    pallas_call x5, Pallas kernels, call(): pl.pallas_call(kernel, out_shape=outs, in_specs=in_specs or vmem(len(oper...  6.46 us
    all_to_all x1, waiting for transfers between devices, exchange(): lax.all_to_all(lines, axes, split_axis=0, concat_axis=0, tiled=True)  5.05 us
  transfers between devices with their start and end apart: 1, of which 1 were waited for; matrix products, arithmetic and copies ran while one was open for 0% of the time, Pallas kernels for 5%

profile of v4, /device:TPU:0, one launch (start us, length us, event | category | flops | bytes accessed | tf_op | source)
XLA Modules:
  0.0 38.0 jit_solution(7419866833865272605)
XLA Ops:
  0.6 1.5 %shard_map.146 = (s32[32,128]{1,0:T(8,128)}, f32[48,1024]{1,0:T(8,128)S(1)}) custom-call(s32[2,1,1,4,8,32]{5,4,3,2,1,0:T(8,128)} %ids.1, f32[48,1024]{1,0:T(8,128)} %refs_0_.1), custom_call_target="tpu_custom_call" | custom-call | flops 1000000 | bytes 1048576 | tf_op jit(solution)/shard_map/pallas_call | solution.py:680
  2.1 7.3 %all-to-all-start = ((s32[32,1,128]{2,1,0:T(1,128)}), s32[32,1,128]{2,1,0:T(1,128)S(1)}, u32[]{:S(2)}, u32[]{:S(2)}) async-start(s32[32,1,128]{2,1,0:T(1,128)} %bitcast.1), calls=%async_computation | async-start | bytes 32768 | tf_op jit(solution)/shard_map/all_to_all | solution.py:720
  9.4 2.0 %shard_map.147 = (f32[576,128]{1,0:T(8,128)S(1)}, f32[472,128]{1,0:T(8,128)S(1)}, f32[2688,128]{1,0:T(8,128)S(1)}, f32[12,256]{1,0:T(8,128)S(1)}, s32[32,128]{1,0:T(8,128)S(1)}, /*index=5*/s32[4,256]{1,0:T(4,128)S(1)}) custom-call(f32[48,1024]{1,0:T(8,128)S(1)} %get-tuple-element.22.cols, f32[3,1024]{1,0:T(4,128)} %far_pos.1, f32[3,1024]{1,0:T(4,128)} %far_scales.1, ...), custom_call_target="tpu_custom_call" | custom-call | flops 1000000 | bytes 1048576 | tf_op jit(solution)/shard_map/pallas_call | solution.py:680
  11.4 5.1 %all-to-all-done = s32[32,1,128]{2,1,0:T(1,128)S(1)} async-done(((s32[32,1,128]{2,1,0:T(1,128)}), s32[32,1,128]{2,1,0:T(1,128)S(1)}, u32[]{:S(2)}, u32[]{:S(2)}) %all-to-all-start) | async-done | bytes 16416 | tf_op jit(solution)/shard_map/all_to_all | solution.py:720
  16.5 0.4 %shard_map.148 = (f32[160,128]{1,0:T(8,128)S(1)}, s32[64,128]{1,0:T(8,128)S(1)}, s32[64,128]{1,0:T(8,128)S(1)}) custom-call(s32[32,128]{1,0:T(8,128)S(1)} %bitcast.17, f32[576,128]{1,0:T(8,128)S(1)} %get-tuple-element.23.rec), custom_call_target="tpu_custom_call" | custom-call | flops 1000000 | bytes 1048576 | tf_op jit(solution)/shard_map/pallas_call | solution.py:680
  16.9 9.3 %all_to_all.15 = f32[32,1,640]{2,1,0:T(1,128)S(1)} all-to-all(f32[32,1,640]{2,1,0:T(1,128)S(1)} %bitcast.16), channel_id=1, replica_groups=mesh['cam'=4,'tile'=8] {'cam','tile'}, dimensions={0} | all-to-all | bytes 163840 | tf_op jit(solution)/shard_map/all_to_all | solution.py:720
  26.2 1.5 %shard_map.149 = f32[160,128]{1,0:T(8,128)S(1)} custom-call(f32[160,128]{1,0:T(8,128)S(1)} %bitcast.14, s32[4,256]{1,0:T(4,128)S(1)} %get-tuple-element.25.lists, f32[12,256]{1,0:T(8,128)S(1)} %get-tuple-element.26.scene, s32[32,128]{1,0:T(8,128)S(1)} %get-tuple-element.27.source), custom_call_target="tpu_custom_call" | custom-call | flops 1000000 | bytes 1048576 | tf_op jit(solution)/shard_map/pallas_call | solution.py:680
  27.7 9.3 %all_to_all.16 = f32[32,1,640]{2,1,0:T(1,128)S(1)} all-to-all(f32[32,1,640]{2,1,0:T(1,128)S(1)} %bitcast.15), channel_id=1, replica_groups=mesh['cam'=4,'tile'=8] {'cam','tile'}, dimensions={0} | all-to-all | bytes 163840 | tf_op jit(solution)/shard_map/all_to_all | solution.py:720
  36.9 1.1 %shard_map.150 = (f32[3,1024]{1,0:T(4,128)}, f32[3,1024]{1,0:T(4,128)}, f32[4,1024]{1,0:T(4,128)}, f32[8,128]{1,0:T(8,128)}, f32[48,1024]{1,0:T(8,128)}) custom-call(f32[160,128]{1,0:T(8,128)S(1)} %bitcast.13, s32[64,128]{1,0:T(8,128)S(1)} %get-tuple-element.28.inverse, s32[64,128]{1,0:T(8,128)S(1)} %get-tuple-element.29.turns, ...), custom_call_target="tpu_custom_call" | custom-call | flops 1000000 | bytes 1048576 | tf_op jit(solution)/shard_map/pallas_call | solution.py:680
Async XLA Ops:
  2.1 14.4 %all-to-all-start = ((s32[32,1,128]{2,1,0:T(1,128)}), s32[32,1,128]{2,1,0:T(1,128)S(1)}, u32[]{:S(2)}, u32[]{:S(2)}) async-start(s32[32,1,128]{2,1,0:T(1,128)} %bitcast.1), calls=%async_computation | async-start | bytes 32768 | tf_op jit(solution)/shard_map/all_to_all | solution.py:720

commit v5 on v4

--- a/solution.py
+++ b/solution.py
@@ -138,27 +138,32 @@
     ]
 
 
-def basis_pull(x, y, z, g):
+def slope_terms(c):
+    d = [None] * 4 + [SH_TWO[i] * c[4 + i] for i in range(5)] + [SH_THREE[i] * c[9 + i] for i in range(7)]
+    first = [-SH_ONE * c[3], -SH_ONE * c[1], SH_ONE * c[2]]
+    in_x = (2.0 * (d[8] - d[6]), 6.0 * d[9] - 2.0 * d[11], 2.0 * d[14] - 6.0 * d[12], 3.0 * d[15])
+    in_y = (-2.0 * (d[8] + d[6]), 3.0 * d[9], -2.0 * d[14] - 6.0 * d[12], -2.0 * d[13] - 6.0 * d[15])
+    in_z = (4.0 * d[6], 8.0 * d[11], 8.0 * d[13])
+    return d, first, in_x, in_y, in_z
+
+
+def slope_of(x, y, z, terms):
+    d, first, in_x, in_y, in_z = terms
     xx, yy, zz = x * x, y * y, z * z
     xy, yz, xz = x * y, y * z, x * z
-    less = xx - yy
-    four = 4.0 * zz - xx - yy
-    g4, g5, g6, g7, g8 = [SH_TWO[i] * g[4 + i] for i in range(5)]
-    h = [SH_THREE[i] * g[9 + i] for i in range(7)]
+    less, both = xx - yy, xx + yy
+    four = 4.0 * zz - both
     g_x = (
-        -SH_ONE * g[3] + g4 * y - 2.0 * g6 * x + g7 * z + 2.0 * g8 * x
-        + 6.0 * h[0] * xy + h[1] * yz - 2.0 * h[2] * xy - 6.0 * h[3] * xz
-        + h[4] * (four - 2.0 * xx) + 2.0 * h[5] * xz + 3.0 * h[6] * less
+        first[0] + d[4] * y + in_x[0] * x + d[7] * z + in_x[1] * xy + d[10] * yz + in_x[2] * xz
+        + d[13] * (four - 2.0 * xx) + in_x[3] * less
     )
     g_y = (
-        -SH_ONE * g[1] + g4 * x + g5 * z - 2.0 * g6 * y - 2.0 * g8 * y
-        + 3.0 * h[0] * less + h[1] * xz + h[2] * (four - 2.0 * yy) - 6.0 * h[3] * yz
-        - 2.0 * h[4] * xy - 2.0 * h[5] * yz - 6.0 * h[6] * xy
+        first[1] + d[4] * x + d[5] * z + in_y[0] * y + in_y[1] * less + d[10] * xz + d[11] * (four - 2.0 * yy)
+        + in_y[2] * yz + in_y[3] * xy
     )
     g_z = (
-        SH_ONE * g[2] + g5 * y + 4.0 * g6 * z + g7 * x
-        + h[1] * xy + 8.0 * h[2] * yz + h[3] * (6.0 * zz - 3.0 * xx - 3.0 * yy)
-        + 8.0 * h[4] * xz + h[5] * less
+        first[2] + d[5] * y + in_z[0] * z + d[7] * x + d[10] * xy + in_z[1] * yz + d[12] * (6.0 * zz - 3.0 * both)
+        + in_z[2] * xz + d[14] * less
     )
     return [g_x, g_y, g_z]
 
@@ -187,8 +192,9 @@
 
 
 def project_kernel(
-    passes, cams, rows, owners, cap, cols, far_pos, far_scales, far_rots, far_opac, far_cam, far_lists, far_wanted, far_counts, far_places,
-    rec, raw, kept, scene, source, chosen, table, pos, scales, rots, opac, cam, lists, wanted, counts, places, done,
+    passes, cams, rows, owners, cap, folded, cols, far_pos, far_scales, far_rots, far_opac, far_cam, far_lists, far_wanted,
+    far_counts, far_places, rec, raw, kept, scene, source, chosen,
+    table, pos, scales, rots, opac, cam, lists, wanted, counts, places, done,
 ):
     views = passes * cams
     shape = (rows, LANES)
@@ -250,6 +256,7 @@
         copy.wait()
     entries, pixels = lists.shape[-1], wanted.shape[-1]
     entry_row = lax.broadcasted_iota(jnp.int32, (1, entries), 1)
+    slot_owner, slot_lane = [], []
     for p in range(passes):
         for k in range(3):
             scene[p * SCENE + k : p * SCENE + k + 1, :] = wanted[p, k]
@@ -258,25 +265,36 @@
         place = jnp.broadcast_to(places[:, p : p + 1], (1, entries))
         for k, value in enumerate((place % 256 * 16 + 8, place // 256 * 16 + 8)):
             scene[p * SCENE + 4 + k : p * SCENE + 5 + k, :] = value.astype(F32)
-        chosen[p : p + 1, :] = lists[p, 0] // cap
-        chosen[passes + p : passes + p + 1, :] = lists[p, 0] % cap + p * cap
+        owner, place = lax.div(lists[p, 0], cap), lax.rem(lists[p, 0], cap)
+        if folded:
+            groups = LANES // cap
+            slot_owner.append(lax.div(owner, groups))
+            slot_lane.append(lax.rem(owner + p, groups) * cap + place)
+        else:
+            slot_owner.append(owner)
+            slot_lane.append(place + p * cap)
+        chosen[p : p + 1, :] = slot_owner[p]
+        chosen[passes + p : passes + p + 1, :] = slot_lane[p]
     pair = (LANES, LANES)
-    turned = lax.broadcasted_iota(jnp.int32, pair, 0)
-    turned_p, turned_j = turned % HALF // cap, turned % cap
+    turned = lax.broadcasted_iota(jnp.int32, pair, 0) & (LANES - 1 if folded else HALF - 1)
     entry = (lax.broadcasted_iota(jnp.int32, pair, 1) + 1).astype(F32)
-    owner_row = lax.broadcasted_iota(jnp.int32, (owners, LANES), 0)
+    lines = GROUP if folded else owners
+    line_at = lax.broadcasted_iota(jnp.int32, (lines, LANES), 0)
     halves = entries // LANES
-    found = jnp.full((owners, LANES), -LANES, jnp.int32)
+    found = jnp.full((lines, LANES), -LANES, jnp.int32)
     for p in range(passes):
         for h in range(halves):
-            slot = lists[p, 0, :, h * LANES : (h + 1) * LANES]
-            mine = jnp.where(jnp.broadcast_to(slot // cap, (owners, LANES)) == owner_row, 1.0, 0.0).astype(BF16)
-            here = jnp.where(
-                (jnp.broadcast_to(slot % cap, pair) == turned_j) & (turned_p == p), entry, 0.0
-            ).astype(BF16)
+            part = slice(h * LANES, (h + 1) * LANES)
+            mine = jnp.where(jnp.broadcast_to(slot_owner[p][:, part], (lines, LANES)) == line_at, 1.0, 0.0).astype(BF16)
+            here = jnp.where(jnp.broadcast_to(slot_lane[p][:, part], pair) == turned, entry, 0.0).astype(BF16)
             hit = dot(mine, here, ((1,), (1,)))
             found = jnp.where(hit > 0.5, hit.astype(jnp.int32) + ((p * halves + h) * LANES - 1), found)
-    source[...] = found
+        if folded:
+            source[p * GROUP : (p + 1) * GROUP, :] = found
+            source[(passes + p) * GROUP : (passes + p + 1) * GROUP, :] = pltpu.roll(found, HALF, 1)
+            found = jnp.full((lines, LANES), -LANES, jnp.int32)
+    if not folded:
+        source[...] = found
 
     for channel in range(3):
         totals = [0.5 + SH_ZERO * at(11 + channel)] * views
@@ -287,21 +305,22 @@
                 totals[view] = totals[view] + kept[start : start + rows, :] * color
         for view in range(views):
             put(rec, view * FIELDS + 6 + channel, totals[view])
-    for view in range(views):
-        direction, back = sight[view]
-        for channel in range(3):
-            slope = basis_pull(*direction, [at(11 + 3 * k + channel) for k in range(16)])
+    for channel in range(3):
+        terms = slope_terms([at(11 + 3 * k + channel) for k in range(16)])
+        for view in range(views):
+            direction, back = sight[view]
+            slope = slope_of(*direction, terms)
             along = dot3(direction, slope)
             for j in range(3):
                 put(kept, view * KEPT + SHADE + 3 * channel + j, (slope[j] - direction[j] * along) * back)
 
 
 def lane_pass(shape, cap):
-    lane = lax.broadcasted_iota(jnp.int32, shape, 1) % HALF
-    return lane // cap, lane % cap
-
-
-def ids_kernel(passes, cams, cap, ids, *refs):
+    lane = lax.broadcasted_iota(jnp.int32, shape, 1) & (HALF - 1)
+    return lax.div(lane, cap)
+
+
+def ids_kernel(passes, cams, rows, cap, folded, ids, *refs):
     count = (len(refs) - 6) // 2
     sources, out, results = refs[:count], refs[count], refs[count + 1 : 2 * count + 1]
     landed, lines, ids_done, out_done, done = refs[2 * count + 1 :]
@@ -316,7 +335,14 @@
         tiles = parts[0].shape[0]
         if passes * cap < HALF:
             parts.append(jnp.zeros((tiles, HALF - passes * cap), jnp.int32))
-        lines[c * tiles : (c + 1) * tiles, :] = jnp.concatenate(parts + parts, axis=1)
+        line = jnp.concatenate(parts + parts, axis=1)
+        if folded:
+            at_row, at_lane = [lax.broadcasted_iota(jnp.int32, line.shape, k) for k in range(2)]
+            plain = line
+            for m in range(1, passes):
+                line = jnp.where(lax.rem(at_row, passes) == m, pltpu.roll(plain, m * cap, 1), line)
+            line = line + ((lax.div(at_lane, cap) - at_row) & (LANES // cap - 1)) * (rows * LANES)
+        lines[c * tiles : (c + 1) * tiles, :] = line
     last = pltpu.make_async_copy(lines, out, out_done)
     last.start()
     for copy in copies:
@@ -324,18 +350,26 @@
     last.wait()
 
 
-def pick_kernel(passes, cams, tiles, rows, cap, aligned, ids, rec, out, inverse, turns):
+def pick_kernel(passes, cams, tiles, rows, cap, aligned, folded, ids, rec, out, inverse, turns):
     shape = (GROUP, LANES)
     lane = lax.broadcasted_iota(jnp.int32, shape, 1)
     sub = lax.broadcasted_iota(jnp.int32, shape, 0)
-    lane_p, _ = lane_pass(shape, cap)
     if not aligned:
         turns[...] = jnp.zeros(turns.shape, jnp.int32)
 
     def packets(first, c):
         low, high = parted(ids[pl.ds(first, GROUP), :])
+        if folded:
+            tag, high = lax.div(high, rows), lax.rem(high, rows)
+            lane_p, first_half = lax.rem(tag, passes), tag < passes
+            blocks = [
+                jnp.broadcast_to(jnp.max(jnp.where(lane_p == p, high, 0), axis=1, keepdims=True), shape)
+                for p in range(passes)
+            ]
+        else:
+            lane_p, first_half = lane_pass(shape, cap), lane < HALF
+            blocks = [jnp.broadcast_to(high[:, p * cap : p * cap + 1], shape) for p in range(passes)]
         if aligned:
-            blocks = [jnp.broadcast_to(high[:, p * cap : p * cap + 1], shape) for p in range(passes)]
             for p in range(passes):
                 turn = jnp.zeros(shape, jnp.int32)
                 for t in range(1, tiles):
@@ -359,7 +393,7 @@
         for r in range(SENT):
             value = pick(2 * r)
             if 2 * r + 1 < FIELDS:
-                value = jnp.where(lane < HALF, value, pick(2 * r + 1))
+                value = jnp.where(first_half, value, pick(2 * r + 1))
             out[pl.ds(first * SENT + r, GROUP, stride=SENT), :] = value
 
     for c in range(cams):
@@ -376,21 +410,27 @@
     square = (LANES, LANES)
     column = lax.broadcasted_iota(jnp.int32, square, 0)
     turn = lax.broadcasted_iota(jnp.int32, square, 1)
-    place = (turn % HALF + 1 + turn // HALF * LANES).astype(F32)
+    place = ((turn & (HALF - 1)) + 1 + jnp.where(turn < HALF, 0, LANES)).astype(F32)
+    if folded:
+        tag = lax.div(parted(jnp.broadcast_to(ids[0:1, :], square))[1], rows)
+        place = (jnp.where(tag < passes, turn, ((turn + HALF) & (LANES - 1)) + LANES) + 1).astype(F32)
     wide = (passes * rows, LANES)
     wide_lane = lax.broadcasted_iota(jnp.int32, wide, 1)
     key = lax.broadcasted_iota(jnp.int32, wide, 0)
-    lane_key = jnp.where(wide_lane % HALF < passes * cap, lane_pass(wide, cap)[0] * rows, -(1 << 20))
+    lane_key = jnp.where((wide_lane & (HALF - 1)) < passes * cap, lane_pass(wide, cap) * rows, -(1 << 20))
     line_lane = lax.broadcasted_iota(jnp.int32, (1, LANES), 1)
 
     def two(c, t, found):
-        low, high = parted(
-            jnp.where(line_lane < HALF, ids[pl.ds(c * tiles + t, 1), :], ids[pl.ds(c * tiles + t + 1, 1), :])
-        )
+        these, next_ones = ids[pl.ds(c * tiles + t, 1), :], ids[pl.ds(c * tiles + t + 1, 1), :]
+        if folded:
+            low, high = parted(jnp.where(these < passes * rows * LANES, these, next_ones))
+            high = lax.rem(high, rows * passes)
+        else:
+            low, high = parted(jnp.where(line_lane < HALF, these, next_ones))
         low = jnp.broadcast_to(low, square)
         high = jnp.broadcast_to(high, wide)
         match = jnp.where(low == column, place, 0.0).astype(BF16)
-        owner = jnp.where(high + lane_key == key, 1.0, 0.0).astype(BF16)
+        owner = jnp.where((high if folded else high + lane_key) == key, 1.0, 0.0).astype(BF16)
         hit = dot(owner, match, ((1,), (1,)))
         return jnp.where(hit > 0.5, hit.astype(jnp.int32) + t * LANES, found)
 
@@ -406,7 +446,7 @@
             inverse[start : start + rows, :] = found[p * rows : (p + 1) * rows, :]
 
 
-def render_kernel(passes, owners, cap, entries, pixels, got, lists, scene, source, out, *scratch):
+def render_kernel(passes, owners, cap, folded, entries, pixels, got, lists, scene, source, out, *scratch):
     alphas, ratios, sums, high, low = [scratch[k * passes : (k + 1) * passes] for k in range(5)]
     halves = entries // LANES
     shape = (GROUP, LANES)
@@ -421,6 +461,15 @@
             slot_owner.append(jnp.broadcast_to(lists[p : p + 1, part], shape))
             slot_lane.append(jnp.broadcast_to(lists[passes + p : passes + p + 1, part], shape))
     total = passes * halves
+
+    groups = LANES // cap
+    lane_group = lax.div(lane, cap)
+
+    def merged(choices, back):
+        value = choices[-back % groups]
+        for g in range(1, groups):
+            value = jnp.where(lane_group == g, choices[(g - back) % groups], value)
+        return value
 
     def gather(g, found):
         mine = [slot_owner[i] == g * GROUP + sub for i in range(total)]
@@ -432,7 +481,17 @@
         return tuple(new)
 
     fields = tuple(jnp.zeros(shape, F32) for _ in range(FIELDS * total))
-    if owners <= 32:
+    if folded:
+        mine = [slot_owner[i] == sub for i in range(total)]
+        places = [slot_lane, [(x + HALF) & (LANES - 1) for x in slot_lane]]
+        fields = []
+        for f in range(FIELDS):
+            packets = [got[pl.ds(m * SENT + f // 2, GROUP, stride=groups * SENT), :] for m in range(groups)]
+            for p in range(passes):
+                tile = merged(packets, f % 2 * passes + p)
+                for i in range(p * halves, (p + 1) * halves):
+                    fields.append(jnp.where(mine[i], lane_pick(tile, places[f % 2][i]), 0.0))
+    elif owners <= 32:
         for g in range(owners // GROUP):
             fields = gather(g, fields)
     else:
@@ -526,25 +585,32 @@
             ]
         )
 
-    def packets(first, origin):
-        index, which = parted(origin)
-
-        def pick(f):
-            found = jnp.zeros(shape, F32)
-            for p in range(passes):
-                for h in range(halves):
-                    line = jnp.broadcast_to(grads[p][f][:, h * LANES : (h + 1) * LANES], shape)
-                    found = jnp.where(which == p * halves + h, lane_pick(line, index), found)
-            return found
-
+    def pick(f, which, index, tiles):
+        found = jnp.zeros(shape, F32)
+        for p, h in tiles:
+            line = jnp.broadcast_to(grads[p][f][:, h * LANES : (h + 1) * LANES], shape)
+            found = jnp.where(which == p * halves + h, lane_pick(line, index), found)
+        return found
+
+    if folded:
+        codes = [parted(source[n * GROUP : (n + 1) * GROUP, :]) for n in range(2 * passes)]
         for r in range(SENT):
-            value = pick(2 * r)
+            parts = []
+            for n, (index, which) in enumerate(codes):
+                p, f = n % passes, min(2 * r + n // passes, FIELDS - 1)
+                parts.append(pick(f, which, index, [(p, h) for h in range(halves)]) if 2 * r + n // passes < FIELDS else parts[p])
+            for m in range(groups):
+                out[pl.ds(m * SENT + r, GROUP, stride=groups * SENT), :] = merged(parts, m)
+        return
+
+    every = [(p, h) for p in range(passes) for h in range(halves)]
+    for g in range(owners // GROUP):
+        index, which = parted(source[g * GROUP : (g + 1) * GROUP, :])
+        for r in range(SENT):
+            value = pick(2 * r, which, index, every)
             if 2 * r + 1 < FIELDS:
-                value = jnp.where(lane < HALF, value, pick(2 * r + 1))
-            out[pl.ds(first * SENT + r, GROUP, stride=SENT), :] = value
-
-    for g in range(owners // GROUP):
-        packets(g * GROUP, source[g * GROUP : (g + 1) * GROUP, :])
+                value = jnp.where(lane < HALF, value, pick(2 * r + 1, which, index, every))
+            out[pl.ds(g * GROUP * SENT + r, GROUP, stride=SENT), :] = value
 
 
 def pull_kernel(
@@ -570,11 +636,11 @@
             if aligned:
                 if row not in turned:
                     turned[row] = row_pick(got[pl.ds(c * tiles * SENT + row, tiles, stride=SENT), :], row_t)
-                return jnp.where(valid, lane_pick(turned[row], slot_lane + shift), 0.0)
+                return jnp.where(valid, lane_pick(turned[row], (slot_lane + shift) & (LANES - 1)), 0.0)
 
             def one(t, found):
                 line = jnp.broadcast_to(got[pl.ds((c * tiles + t) * SENT + row, 1), :], shape)
-                return jnp.where(valid & (slot_t == t), lane_pick(line, slot_lane + shift), found)
+                return jnp.where(valid & (slot_t == t), lane_pick(line, (slot_lane + shift) & (LANES - 1)), found)
 
             return lax.fori_loop(0, tiles, one, jnp.zeros(shape, F32))
 
@@ -710,7 +776,8 @@
     rows = columns // LANES
     owners = cams * tiles
     views = passes * cams
-    aligned = tiles == rows == 8
+    aligned = tiles == rows == GROUP
+    folded = 2 * passes * cap == LANES and owners * cap == GROUP * LANES and tiles % (LANES // cap) == 0
 
     def shaped(*shape):
         return jax.ShapeDtypeStruct(shape, F32)
@@ -722,7 +789,7 @@
     whole, smem, far = [pl.BlockSpec(memory_space=space) for space in (pltpu.VMEM, pltpu.SMEM, pltpu.HBM)]
     near = [colors]
     wanted_ids, *near = call(
-        functools.partial(ids_kernel, passes, cams, cap),
+        functools.partial(ids_kernel, passes, cams, rows, cap, folded),
         [jax.ShapeDtypeStruct((owners, LANES), jnp.int32)]
         + [pltpu.VMEM(x.shape, x.dtype) for x in near],
         [pltpu.with_memory_space_constraint(x, pltpu.HBM) for x in (fetch_ids, *near)],
@@ -749,13 +816,13 @@
         tile_ids.reshape(1, passes),
     ]
     records, raw, kept, scene, source, lists = call(
-        functools.partial(project_kernel, passes, cams, rows, owners, cap),
+        functools.partial(project_kernel, passes, cams, rows, owners, cap, folded),
         [
             shaped(views * FIELDS * rows, LANES),
             shaped(RAW * rows, LANES),
             shaped(views * KEPT * rows, LANES),
             shaped(passes * SCENE, entries),
-            jax.ShapeDtypeStruct((owners, LANES), jnp.int32),
+            jax.ShapeDtypeStruct((2 * passes * GROUP if folded else owners, LANES), jnp.int32),
             jax.ShapeDtypeStruct((2 * passes, entries), jnp.int32),
         ],
         [*near, *[pltpu.with_memory_space_constraint(x, pltpu.HBM) for x in small]],
@@ -766,13 +833,13 @@
     )
     codes = jax.ShapeDtypeStruct((views * rows, LANES), jnp.int32)
     packets, inverse, turns = call(
-        functools.partial(pick_kernel, passes, cams, tiles, rows, cap, aligned),
+        functools.partial(pick_kernel, passes, cams, tiles, rows, cap, aligned, folded),
         [shaped(owners * SENT, LANES), codes, codes],
         [arrived, records],
     )
     fetched = exchange(packets)
     slot_grads = call(
-        functools.partial(render_kernel, passes, owners, cap, entries, pixels),
+        functools.partial(render_kernel, passes, owners, cap, folded, entries, pixels),
         shaped(owners * SENT, LANES),
         [fetched, lists, scene, source],
         scratch=[pltpu.VMEM((pixels, entries), kind) for kind in (F32, F32, F32, BF16, BF16) for _ in range(passes)],

time: 38.3 us -> 38.2 us (level)
  no operation moved by 1% of the time
where the time goes in v5:
time: 38.2 us; the launch traced here: 37.9 us
  blocking collectives  18.5 us (48%)
  starting transfers between devices  7.3 us (19%)
  Pallas kernels  6.4 us (17%)
  waiting for transfers between devices  5.05 us (13%)
  between operations  0.66 us (2%)
    all_to_all x2, blocking collectives, exchange(): lax.all_to_all(lines, axes, split_axis=0, concat_axis=0, tiled=True)  18.5 us
    all_to_all x1, starting transfers between devices, exchange(): lax.all_to_all(lines, axes, split_axis=0, concat_axis=0, tiled=True)  7.3 us
    pallas_call x5, Pallas kernels, call(): pl.pallas_call(kernel, out_shape=outs, in_specs=in_specs or vmem(len(oper...  6.4 us
    all_to_all x1, waiting for transfers between devices, exchange(): lax.all_to_all(lines, axes, split_axis=0, concat_axis=0, tiled=True)  5.05 us
  transfers between devices with their start and end apart: 1, of which 1 were waited for; matrix products, arithmetic and copies ran while one was open for 0% of the time, Pallas kernels for 5%

profile of v5, /device:TPU:0, one launch (start us, length us, event | category | flops | bytes accessed | tf_op | source)
XLA Modules:
  0.0 37.9 jit_solution(9464120814239577717)
XLA Ops:
  0.6 1.5 %shard_map.146 = (s32[32,128]{1,0:T(8,128)}, f32[48,1024]{1,0:T(8,128)S(1)}) custom-call(s32[2,1,1,4,8,32]{5,4,3,2,1,0:T(8,128)} %ids.1, f32[48,1024]{1,0:T(8,128)} %refs_0_.1), custom_call_target="tpu_custom_call" | custom-call | flops 1000000 | bytes 1048576 | tf_op jit(solution)/shard_map/pallas_call | solution.py:746
  2.2 7.3 %all-to-all-start = ((s32[32,1,128]{2,1,0:T(1,128)}), s32[32,1,128]{2,1,0:T(1,128)S(1)}, u32[]{:S(2)}, u32[]{:S(2)}) async-start(s32[32,1,128]{2,1,0:T(1,128)} %bitcast.1), calls=%async_computation | async-start | bytes 32768 | tf_op jit(solution)/shard_map/all_to_all | solution.py:787
  9.5 2.0 %shard_map.147 = (f32[576,128]{1,0:T(8,128)S(1)}, f32[472,128]{1,0:T(8,128)S(1)}, f32[2688,128]{1,0:T(8,128)S(1)}, f32[12,256]{1,0:T(8,128)S(1)}, s32[32,128]{1,0:T(8,128)S(1)}, /*index=5*/s32[4,256]{1,0:T(4,128)S(1)}) custom-call(f32[48,1024]{1,0:T(8,128)S(1)} %get-tuple-element.22.cols, f32[3,1024]{1,0:T(4,128)} %far_pos.1, f32[3,1024]{1,0:T(4,128)} %far_scales.1, ...), custom_call_target="tpu_custom_call" | custom-call | flops 1000000 | bytes 1048576 | tf_op jit(solution)/shard_map/pallas_call | solution.py:746
  11.5 5.0 %all-to-all-done = s32[32,1,128]{2,1,0:T(1,128)S(1)} async-done(((s32[32,1,128]{2,1,0:T(1,128)}), s32[32,1,128]{2,1,0:T(1,128)S(1)}, u32[]{:S(2)}, u32[]{:S(2)}) %all-to-all-start) | async-done | bytes 16416 | tf_op jit(solution)/shard_map/all_to_all | solution.py:787
  16.6 0.4 %shard_map.148 = (f32[160,128]{1,0:T(8,128)S(1)}, s32[64,128]{1,0:T(8,128)S(1)}, s32[64,128]{1,0:T(8,128)S(1)}) custom-call(s32[32,128]{1,0:T(8,128)S(1)} %bitcast.17, f32[576,128]{1,0:T(8,128)S(1)} %get-tuple-element.23.rec), custom_call_target="tpu_custom_call" | custom-call | flops 1000000 | bytes 1048576 | tf_op jit(solution)/shard_map/pallas_call | solution.py:746
  17.0 9.3 %all_to_all.15 = f32[32,1,640]{2,1,0:T(1,128)S(1)} all-to-all(f32[32,1,640]{2,1,0:T(1,128)S(1)} %bitcast.16), channel_id=1, replica_groups=mesh['cam'=4,'tile'=8] {'cam','tile'}, dimensions={0} | all-to-all | bytes 163840 | tf_op jit(solution)/shard_map/all_to_all | solution.py:787
  26.2 1.3 %shard_map.149 = f32[160,128]{1,0:T(8,128)S(1)} custom-call(f32[160,128]{1,0:T(8,128)S(1)} %bitcast.14, s32[4,256]{1,0:T(4,128)S(1)} %get-tuple-element.25.lists, f32[12,256]{1,0:T(8,128)S(1)} %get-tuple-element.26.scene, s32[32,128]{1,0:T(8,128)S(1)} %get-tuple-element.27.source), custom_call_target="tpu_custom_call" | custom-call | flops 1000000 | bytes 1048576 | tf_op jit(solution)/shard_map/pallas_call | solution.py:746
  27.6 9.3 %all_to_all.16 = f32[32,1,640]{2,1,0:T(1,128)S(1)} all-to-all(f32[32,1,640]{2,1,0:T(1,128)S(1)} %bitcast.15), channel_id=1, replica_groups=mesh['cam'=4,'tile'=8] {'cam','tile'}, dimensions={0} | all-to-all | bytes 163840 | tf_op jit(solution)/shard_map/all_to_all | solution.py:787
  36.9 1.1 %shard_map.150 = (f32[3,1024]{1,0:T(4,128)}, f32[3,1024]{1,0:T(4,128)}, f32[4,1024]{1,0:T(4,128)}, f32[8,128]{1,0:T(8,128)}, f32[48,1024]{1,0:T(8,128)}) custom-call(f32[160,128]{1,0:T(8,128)S(1)} %bitcast.13, s32[64,128]{1,0:T(8,128)S(1)} %get-tuple-element.28.inverse, s32[64,128]{1,0:T(8,128)S(1)} %get-tuple-element.29.turns, ...), custom_call_target="tpu_custom_call" | custom-call | flops 1000000 | bytes 1048576 | tf_op jit(solution)/shard_map/pallas_call | solution.py:746
Async XLA Ops:
  2.2 14.4 %all-to-all-start = ((s32[32,1,128]{2,1,0:T(1,128)}), s32[32,1,128]{2,1,0:T(1,128)S(1)}, u32[]{:S(2)}, u32[]{:S(2)}) async-start(s32[32,1,128]{2,1,0:T(1,128)} %bitcast.1), calls=%async_computation | async-start | bytes 32768 | tf_op jit(solution)/shard_map/all_to_all | solution.py:787

commit v6 on v5

--- a/solution.py
+++ b/solution.py
@@ -338,9 +338,9 @@
         line = jnp.concatenate(parts + parts, axis=1)
         if folded:
             at_row, at_lane = [lax.broadcasted_iota(jnp.int32, line.shape, k) for k in range(2)]
-            plain = line
             for m in range(1, passes):
-                line = jnp.where(lax.rem(at_row, passes) == m, pltpu.roll(plain, m * cap, 1), line)
+                turned = parts[-m:] + parts[:-m]
+                line = jnp.where(lax.rem(at_row, passes) == m, jnp.concatenate(turned + turned, axis=1), line)
             line = line + ((lax.div(at_lane, cap) - at_row) & (LANES // cap - 1)) * (rows * LANES)
         lines[c * tiles : (c + 1) * tiles, :] = line
     last = pltpu.make_async_copy(lines, out, out_done)

time: 38.2 us -> 38.1 us (level)
  no operation moved by 1% of the time
where the time goes in v6:
time: 38.1 us; the launch traced here: 37.9 us
  blocking collectives  18.5 us (49%)
  starting transfers between devices  7.3 us (19%)
  Pallas kernels  6.34 us (17%)
  waiting for transfers between devices  5.05 us (13%)
  between operations  0.66 us (2%)
    all_to_all x2, blocking collectives, exchange(): lax.all_to_all(lines, axes, split_axis=0, concat_axis=0, tiled=True)  18.5 us
    all_to_all x1, starting transfers between devices, exchange(): lax.all_to_all(lines, axes, split_axis=0, concat_axis=0, tiled=True)  7.3 us
    pallas_call x5, Pallas kernels, call(): pl.pallas_call(kernel, out_shape=outs, in_specs=in_specs or vmem(len(oper...  6.34 us
    all_to_all x1, waiting for transfers between devices, exchange(): lax.all_to_all(lines, axes, split_axis=0, concat_axis=0, tiled=True)  5.05 us
  transfers between devices with their start and end apart: 1, of which 1 were waited for; matrix products, arithmetic and copies ran while one was open for 0% of the time, Pallas kernels for 5%

profile of v6, /device:TPU:0, one launch (start us, length us, event | category | flops | bytes accessed | tf_op | source)
XLA Modules:
  0.0 37.9 jit_solution(9204079082293352674)
XLA Ops:
  0.6 1.5 %shard_map.146 = (s32[32,128]{1,0:T(8,128)}, f32[48,1024]{1,0:T(8,128)S(1)}) custom-call(s32[2,1,1,4,8,32]{5,4,3,2,1,0:T(8,128)} %ids.1, f32[48,1024]{1,0:T(8,128)} %refs_0_.1), custom_call_target="tpu_custom_call" | custom-call | flops 1000000 | bytes 1048576 | tf_op jit(solution)/shard_map/pallas_call | solution.py:746
  2.1 7.3 %all-to-all-start = ((s32[32,1,128]{2,1,0:T(1,128)}), s32[32,1,128]{2,1,0:T(1,128)S(1)}, u32[]{:S(2)}, u32[]{:S(2)}) async-start(s32[32,1,128]{2,1,0:T(1,128)} %bitcast.1), calls=%async_computation | async-start | bytes 32768 | tf_op jit(solution)/shard_map/all_to_all | solution.py:787
  9.4 2.0 %shard_map.147 = (f32[576,128]{1,0:T(8,128)S(1)}, f32[472,128]{1,0:T(8,128)S(1)}, f32[2688,128]{1,0:T(8,128)S(1)}, f32[12,256]{1,0:T(8,128)S(1)}, s32[32,128]{1,0:T(8,128)S(1)}, /*index=5*/s32[4,256]{1,0:T(4,128)S(1)}) custom-call(f32[48,1024]{1,0:T(8,128)S(1)} %get-tuple-element.22.cols, f32[3,1024]{1,0:T(4,128)} %far_pos.1, f32[3,1024]{1,0:T(4,128)} %far_scales.1, ...), custom_call_target="tpu_custom_call" | custom-call | flops 1000000 | bytes 1048576 | tf_op jit(solution)/shard_map/pallas_call | solution.py:746
  11.4 5.0 %all-to-all-done = s32[32,1,128]{2,1,0:T(1,128)S(1)} async-done(((s32[32,1,128]{2,1,0:T(1,128)}), s32[32,1,128]{2,1,0:T(1,128)S(1)}, u32[]{:S(2)}, u32[]{:S(2)}) %all-to-all-start) | async-done | bytes 16416 | tf_op jit(solution)/shard_map/all_to_all | solution.py:787
  16.5 0.4 %shard_map.148 = (f32[160,128]{1,0:T(8,128)S(1)}, s32[64,128]{1,0:T(8,128)S(1)}, s32[64,128]{1,0:T(8,128)S(1)}) custom-call(s32[32,128]{1,0:T(8,128)S(1)} %bitcast.17, f32[576,128]{1,0:T(8,128)S(1)} %get-tuple-element.23.rec), custom_call_target="tpu_custom_call" | custom-call | flops 1000000 | bytes 1048576 | tf_op jit(solution)/shard_map/pallas_call | solution.py:746
  16.9 9.3 %all_to_all.15 = f32[32,1,640]{2,1,0:T(1,128)S(1)} all-to-all(f32[32,1,640]{2,1,0:T(1,128)S(1)} %bitcast.16), channel_id=1, replica_groups=mesh['cam'=4,'tile'=8] {'cam','tile'}, dimensions={0} | all-to-all | bytes 163840 | tf_op jit(solution)/shard_map/all_to_all | solution.py:787
  26.2 1.3 %shard_map.149 = f32[160,128]{1,0:T(8,128)S(1)} custom-call(f32[160,128]{1,0:T(8,128)S(1)} %bitcast.14, s32[4,256]{1,0:T(4,128)S(1)} %get-tuple-element.25.lists, f32[12,256]{1,0:T(8,128)S(1)} %get-tuple-element.26.scene, s32[32,128]{1,0:T(8,128)S(1)} %get-tuple-element.27.source), custom_call_target="tpu_custom_call" | custom-call | flops 1000000 | bytes 1048576 | tf_op jit(solution)/shard_map/pallas_call | solution.py:746
  27.5 9.3 %all_to_all.16 = f32[32,1,640]{2,1,0:T(1,128)S(1)} all-to-all(f32[32,1,640]{2,1,0:T(1,128)S(1)} %bitcast.15), channel_id=1, replica_groups=mesh['cam'=4,'tile'=8] {'cam','tile'}, dimensions={0} | all-to-all | bytes 163840 | tf_op jit(solution)/shard_map/all_to_all | solution.py:787
  36.8 1.1 %shard_map.150 = (f32[3,1024]{1,0:T(4,128)}, f32[3,1024]{1,0:T(4,128)}, f32[4,1024]{1,0:T(4,128)}, f32[8,128]{1,0:T(8,128)}, f32[48,1024]{1,0:T(8,128)}) custom-call(f32[160,128]{1,0:T(8,128)S(1)} %bitcast.13, s32[64,128]{1,0:T(8,128)S(1)} %get-tuple-element.28.inverse, s32[64,128]{1,0:T(8,128)S(1)} %get-tuple-element.29.turns, ...), custom_call_target="tpu_custom_call" | custom-call | flops 1000000 | bytes 1048576 | tf_op jit(solution)/shard_map/pallas_call | solution.py:746
Async XLA Ops:
  2.1 14.4 %all-to-all-start = ((s32[32,1,128]{2,1,0:T(1,128)}), s32[32,1,128]{2,1,0:T(1,128)S(1)}, u32[]{:S(2)}, u32[]{:S(2)}) async-start(s32[32,1,128]{2,1,0:T(1,128)} %bitcast.1), calls=%async_computation | async-start | bytes 32768 | tf_op jit(solution)/shard_map/all_to_all | solution.py:787

commit v7 on v6

--- a/solution.py
+++ b/solution.py
@@ -447,7 +447,10 @@
 
 
 def render_kernel(passes, owners, cap, folded, entries, pixels, got, lists, scene, source, out, *scratch):
-    alphas, ratios, sums, high, low = [scratch[k * passes : (k + 1) * passes] for k in range(5)]
+    alphas, ratios, weights, pulls, before_sums, slopes, after_sums = [scratch[k * passes : (k + 1) * passes] for k in range(7)]
+    clears, shares, pulled_parts = [
+        [scratch[(7 + 2 * k) * passes + p :: passes][:2] for p in range(passes)] for k in range(3)
+    ]
     halves = entries // LANES
     shape = (GROUP, LANES)
     wide = 16
@@ -517,54 +520,92 @@
     def offset_y(p, y):
         return (y - 7.5) - lines[p][1]
 
+    def through(parts, at, matrix):
+        return dot(parts[0][at, :], matrix, ((1,), (0,))) + dot(parts[1][at, :], matrix, ((1,), (0,)))
+
+    consts = []
     for p in range(passes):
         _, _, c_a, c_b, c_c, base = lines[p][:6]
         live = base * scene[p * SCENE + 3 : p * SCENE + 4, :]
-        d_x = spans[p]
-        q_xx = (-0.5 * c_a) * d_x * d_x
-        q_x = -c_b * d_x
+        consts.append((live, (-0.5 * c_a) * spans[p] * spans[p], -c_b * spans[p], 0.5 * c_c))
+
+    def blend(p, y, at):
+        live, q_xx, q_x, c_c = consts[p]
+        d_y = offset_y(p, y)
+        alpha = live * jnp.exp(q_xx + (q_x * d_y - c_c * d_y * d_y))
+        clear = jnp.log(1.0 - alpha)
+        alphas[p][at, :] = alpha
+        ratios[p][at, :] = alpha * jnp.exp(-clear)
+        clears[p][0][at, :], clears[p][1][at, :] = split(clear)
+
+    def weigh(p, y, at):
+        weight = alphas[p][at, :] * jnp.exp(before_sums[p][at, :])
+        weights[p][at, :] = weight
+        shares[p][0][at, :], shares[p][1][at, :] = split(weight)
+
+    def pull(p, y, at):
+        pulled = weights[p][at, :] * slopes[p][at, :]
+        pulls[p][at, :] = pulled
+        pulled_parts[p][0][at, :], pulled_parts[p][1][at, :] = split(pulled)
+
+    totals = [[jnp.zeros((wide, entries), F32)] * 3 for _ in range(passes)]
+
+    def add(p, y, at):
+        m_1, m_y, m_yy = totals[p]
+        grad = pulls[p][at, :] - ratios[p][at, :] * after_sums[p][at, :]
+        d_y = offset_y(p, y)
+        grad_y = grad * d_y
+        totals[p] = [m_1 + grad, m_y + grad_y, m_yy + grad_y * d_y]
+
+    blocks = [slice(n, n + 128) for n in range(0, pixels, 128)]
+    both = range(passes)
+
+    def each(work, p, block):
         for y, at in enumerate(steps):
-            d_y = offset_y(p, y)
-            alpha = live * jnp.exp(q_xx + (q_x * d_y - 0.5 * c_c * d_y * d_y))
-            clear = jnp.log(1.0 - alpha)
-            alphas[p][at, :] = alpha
-            ratios[p][at, :] = alpha * jnp.exp(-clear)
-            high[p][at, :], low[p][at, :] = split(clear)
-    for p in range(passes):
-        sums[p][...] = dot(high[p][...], before, ((1,), (0,))) + dot(low[p][...], before, ((1,), (0,)))
-    for p in range(passes):
-        for at in steps:
-            weight = alphas[p][at, :] * jnp.exp(sums[p][at, :])
-            alphas[p][at, :] = weight
-            high[p][at, :], low[p][at, :] = split(weight)
+            if block.start <= at.start < block.stop:
+                work(p, y, at)
+
+    def sum_before(p, block):
+        before_sums[p][block, :] = through(clears[p], block, before)
+
+    def sum_after(p, block):
+        after_sums[p][block, :] = through(pulled_parts[p], block, after)
+
+    def slope(p, block):
+        r_high, r_low = [r[:, block] for r in residuals[p]]
+        slopes[p][block, :] = dot(jnp.concatenate([r_high, r_high, r_low], axis=0), pair_rows[p], ((0,), (0,)))
+
+    def emit(first, second, third):
+        jobs = [(block, p) for block in blocks for p in both]
+        depth = 2
+        for n in range(len(jobs) + 2 * depth):
+            if n < len(jobs) and first:
+                each(first, jobs[n][1], jobs[n][0])
+            if 0 <= n - depth < len(jobs):
+                second(jobs[n - depth][1], jobs[n - depth][0])
+            if 0 <= n - 2 * depth < len(jobs):
+                each(third, jobs[n - 2 * depth][1], jobs[n - 2 * depth][0])
+
+    emit(blend, sum_before, weigh)
     residuals, pair_rows = [], []
-    for p in range(passes):
+    for p in both:
         c_high, c_low = split(jnp.concatenate(lines[p][6:9], axis=0))
-        both = dot(jnp.concatenate([c_high, c_low], axis=0), high[p][...], ((1,), (1,)))
-        shown = both[0:3, :] + both[3:6, :] + dot(c_high, low[p][...], ((1,), (1,)))
+        pair = dot(jnp.concatenate([c_high, c_low], axis=0), shares[p][0][...], ((1,), (1,)))
+        shown = pair[0:3, :] + pair[3:6, :] + dot(c_high, shares[p][1][...], ((1,), (1,)))
         residuals.append(split(shown - scene[p * SCENE : p * SCENE + 3, :]))
         pair_rows.append(jnp.concatenate([c_high, c_low, c_high], axis=0))
+    for block in blocks:
+        for p in both:
+            slope(p, block)
+    emit(pull, sum_after, add)
     color_grads = []
-    for p in range(passes):
+    for p in both:
         r_high, r_low = residuals[p]
-        sums[p][...] = dot(jnp.concatenate([r_high, r_high, r_low], axis=0), pair_rows[p], ((0,), (0,)))
-        both = dot(jnp.concatenate([r_high, r_low], axis=0), high[p][...], ((1,), (0,)))
-        color_grads.append(both[0:3, :] + both[3:6, :] + dot(r_high, low[p][...], ((1,), (0,))))
-    for p in range(passes):
-        for at in steps:
-            pulled = alphas[p][at, :] * sums[p][at, :]
-            alphas[p][at, :] = pulled
-            high[p][at, :], low[p][at, :] = split(pulled)
-    for p in range(passes):
-        sums[p][...] = dot(high[p][...], after, ((1,), (0,))) + dot(low[p][...], after, ((1,), (0,)))
+        pair = dot(jnp.concatenate([r_high, r_low], axis=0), shares[p][0][...], ((1,), (0,)))
+        color_grads.append(pair[0:3, :] + pair[3:6, :] + dot(r_high, shares[p][1][...], ((1,), (0,))))
     grads = []
-    for p in range(passes):
-        m_1 = m_y = m_yy = jnp.zeros((wide, entries), F32)
-        for y, at in enumerate(steps):
-            grad = alphas[p][at, :] - ratios[p][at, :] * sums[p][at, :]
-            d_y = offset_y(p, y)
-            grad_y = grad * d_y
-            m_1, m_y, m_yy = m_1 + grad, m_y + grad_y, m_yy + grad_y * d_y
+    for p in both:
+        m_1, m_y, m_yy = totals[p]
         d_x = spans[p]
         m_x = m_1 * d_x
         s_1, s_x, s_y, s_xx, s_xy, s_yy = [
@@ -736,6 +777,10 @@
         send(near, away)
     for copy in copies:
         copy.wait()
+
+
+def render_scratch(passes, pixels, entries):
+    return [pltpu.VMEM((pixels, entries), F32)] * (7 * passes) + [pltpu.VMEM((pixels, entries), BF16)] * (6 * passes)
 
 
 def vmem(count):
@@ -842,7 +887,7 @@
         functools.partial(render_kernel, passes, owners, cap, folded, entries, pixels),
         shaped(owners * SENT, LANES),
         [fetched, lists, scene, source],
-        scratch=[pltpu.VMEM((pixels, entries), kind) for kind in (F32, F32, F32, BF16, BF16) for _ in range(passes)],
+        scratch=render_scratch(passes, pixels, entries),
     )
     coming = exchange(slot_grads)
     g_pos, g_scales, g_rots, g_opac, g_cols = call(

time: 38.1 us -> 38.1 us (level)
  no operation moved by 1% of the time
where the time goes in v7:
time: 38.1 us; the launch traced here: 37.9 us
  blocking collectives  18.5 us (49%)
  starting transfers between devices  7.3 us (19%)
  Pallas kernels  6.31 us (17%)
  waiting for transfers between devices  5.05 us (13%)
  between operations  0.66 us (2%)
    all_to_all x2, blocking collectives, exchange(): lax.all_to_all(lines, axes, split_axis=0, concat_axis=0, tiled=True)  18.5 us
    all_to_all x1, starting transfers between devices, exchange(): lax.all_to_all(lines, axes, split_axis=0, concat_axis=0, tiled=True)  7.3 us
    pallas_call x5, Pallas kernels, call(): pl.pallas_call(kernel, out_shape=outs, in_specs=in_specs or vmem(len(oper...  6.31 us
    all_to_all x1, waiting for transfers between devices, exchange(): lax.all_to_all(lines, axes, split_axis=0, concat_axis=0, tiled=True)  5.05 us
  transfers between devices with their start and end apart: 1, of which 1 were waited for; matrix products, arithmetic and copies ran while one was open for 0% of the time, Pallas kernels for 5%

profile of v7, /device:TPU:0, one launch (start us, length us, event | category | flops | bytes accessed | tf_op | source)
XLA Modules:
  0.0 37.9 jit_solution(9338084359465293909)
XLA Ops:
  0.6 1.5 %shard_map.146 = (s32[32,128]{1,0:T(8,128)}, f32[48,1024]{1,0:T(8,128)S(1)}) custom-call(s32[2,1,1,4,8,32]{5,4,3,2,1,0:T(8,128)} %ids.1, f32[48,1024]{1,0:T(8,128)} %refs_0_.1), custom_call_target="tpu_custom_call" | custom-call | flops 1000000 | bytes 1048576 | tf_op jit(solution)/shard_map/pallas_call | solution.py:791
  2.1 7.3 %all-to-all-start = ((s32[32,1,128]{2,1,0:T(1,128)}), s32[32,1,128]{2,1,0:T(1,128)S(1)}, u32[]{:S(2)}, u32[]{:S(2)}) async-start(s32[32,1,128]{2,1,0:T(1,128)} %bitcast.1), calls=%async_computation | async-start | bytes 32768 | tf_op jit(solution)/shard_map/all_to_all | solution.py:832
  9.4 2.0 %shard_map.147 = (f32[576,128]{1,0:T(8,128)S(1)}, f32[472,128]{1,0:T(8,128)S(1)}, f32[2688,128]{1,0:T(8,128)S(1)}, f32[12,256]{1,0:T(8,128)S(1)}, s32[32,128]{1,0:T(8,128)S(1)}, /*index=5*/s32[4,256]{1,0:T(4,128)S(1)}) custom-call(f32[48,1024]{1,0:T(8,128)S(1)} %get-tuple-element.22.cols, f32[3,1024]{1,0:T(4,128)} %far_pos.1, f32[3,1024]{1,0:T(4,128)} %far_scales.1, ...), custom_call_target="tpu_custom_call" | custom-call | flops 1000000 | bytes 1048576 | tf_op jit(solution)/shard_map/pallas_call | solution.py:791
  11.4 5.0 %all-to-all-done = s32[32,1,128]{2,1,0:T(1,128)S(1)} async-done(((s32[32,1,128]{2,1,0:T(1,128)}), s32[32,1,128]{2,1,0:T(1,128)S(1)}, u32[]{:S(2)}, u32[]{:S(2)}) %all-to-all-start) | async-done | bytes 16416 | tf_op jit(solution)/shard_map/all_to_all | solution.py:832
  16.5 0.4 %shard_map.148 = (f32[160,128]{1,0:T(8,128)S(1)}, s32[64,128]{1,0:T(8,128)S(1)}, s32[64,128]{1,0:T(8,128)S(1)}) custom-call(s32[32,128]{1,0:T(8,128)S(1)} %bitcast.17, f32[576,128]{1,0:T(8,128)S(1)} %get-tuple-element.23.rec), custom_call_target="tpu_custom_call" | custom-call | flops 1000000 | bytes 1048576 | tf_op jit(solution)/shard_map/pallas_call | solution.py:791
  16.9 9.3 %all_to_all.15 = f32[32,1,640]{2,1,0:T(1,128)S(1)} all-to-all(f32[32,1,640]{2,1,0:T(1,128)S(1)} %bitcast.16), channel_id=1, replica_groups=mesh['cam'=4,'tile'=8] {'cam','tile'}, dimensions={0} | all-to-all | bytes 163840 | tf_op jit(solution)/shard_map/all_to_all | solution.py:832
  26.2 1.3 %shard_map.149 = f32[160,128]{1,0:T(8,128)S(1)} custom-call(f32[160,128]{1,0:T(8,128)S(1)} %bitcast.14, s32[4,256]{1,0:T(4,128)S(1)} %get-tuple-element.25.lists, f32[12,256]{1,0:T(8,128)S(1)} %get-tuple-element.26.scene, s32[32,128]{1,0:T(8,128)S(1)} %get-tuple-element.27.source), custom_call_target="tpu_custom_call" | custom-call | flops 1000000 | bytes 1048576 | tf_op jit(solution)/shard_map/pallas_call | solution.py:791
  27.5 9.3 %all_to_all.16 = f32[32,1,640]{2,1,0:T(1,128)S(1)} all-to-all(f32[32,1,640]{2,1,0:T(1,128)S(1)} %bitcast.15), channel_id=1, replica_groups=mesh['cam'=4,'tile'=8] {'cam','tile'}, dimensions={0} | all-to-all | bytes 163840 | tf_op jit(solution)/shard_map/all_to_all | solution.py:832
  36.8 1.1 %shard_map.150 = (f32[3,1024]{1,0:T(4,128)}, f32[3,1024]{1,0:T(4,128)}, f32[4,1024]{1,0:T(4,128)}, f32[8,128]{1,0:T(8,128)}, f32[48,1024]{1,0:T(8,128)}) custom-call(f32[160,128]{1,0:T(8,128)S(1)} %bitcast.13, s32[64,128]{1,0:T(8,128)S(1)} %get-tuple-element.28.inverse, s32[64,128]{1,0:T(8,128)S(1)} %get-tuple-element.29.turns, ...), custom_call_target="tpu_custom_call" | custom-call | flops 1000000 | bytes 1048576 | tf_op jit(solution)/shard_map/pallas_call | solution.py:791
Async XLA Ops:
  2.1 14.4 %all-to-all-start = ((s32[32,1,128]{2,1,0:T(1,128)}), s32[32,1,128]{2,1,0:T(1,128)S(1)}, u32[]{:S(2)}, u32[]{:S(2)}) async-start(s32[32,1,128]{2,1,0:T(1,128)} %bitcast.1), calls=%async_computation | async-start | bytes 32768 | tf_op jit(solution)/shard_map/all_to_all | solution.py:832

commit v8 on v7

--- a/solution.py
+++ b/solution.py
@@ -324,12 +324,14 @@
     count = (len(refs) - 6) // 2
     sources, out, results = refs[:count], refs[count], refs[count + 1 : 2 * count + 1]
     landed, lines, ids_done, out_done, done = refs[2 * count + 1 :]
-    first = pltpu.make_async_copy(ids, landed, ids_done)
-    first.start()
+    firsts = [pltpu.make_async_copy(ids.at[p], landed.at[p], ids_done.at[p]) for p in range(passes)]
+    for first in firsts:
+        first.start()
     copies = [pltpu.make_async_copy(source, result, done.at[k]) for k, (source, result) in enumerate(zip(sources, results))]
     for copy in copies:
         copy.start()
-    first.wait()
+    for first in firsts:
+        first.wait()
     for c in range(cams):
         parts = [landed[p, 0, 0, c] for p in range(passes)]
         tiles = parts[0].shape[0]
@@ -843,7 +845,7 @@
         scratch=[
             pltpu.VMEM(fetch_ids.shape, jnp.int32),
             pltpu.VMEM((owners, LANES), jnp.int32),
-            pltpu.SemaphoreType.DMA,
+            pltpu.SemaphoreType.DMA((passes,)),
             pltpu.SemaphoreType.DMA,
             pltpu.SemaphoreType.DMA((len(near),)),
         ],

time: 38.1 us -> 38.1 us (level)
  no operation moved by 1% of the time
where the time goes in v8:
time: 38.1 us; the launch traced here: 37.8 us
  blocking collectives  18.5 us (49%)
  starting transfers between devices  7.3 us (19%)
  Pallas kernels  6.3 us (17%)
  waiting for transfers between devices  5.05 us (13%)
  between operations  0.66 us (2%)
    all_to_all x2, blocking collectives, exchange(): lax.all_to_all(lines, axes, split_axis=0, concat_axis=0, tiled=True)  18.5 us
    all_to_all x1, starting transfers between devices, exchange(): lax.all_to_all(lines, axes, split_axis=0, concat_axis=0, tiled=True)  7.3 us
    pallas_call x5, Pallas kernels, call(): pl.pallas_call(kernel, out_shape=outs, in_specs=in_specs or vmem(len(oper...  6.3 us
    all_to_all x1, waiting for transfers between devices, exchange(): lax.all_to_all(lines, axes, split_axis=0, concat_axis=0, tiled=True)  5.05 us
  transfers between devices with their start and end apart: 1, of which 1 were waited for; matrix products, arithmetic and copies ran while one was open for 0% of the time, Pallas kernels for 5%

profile of v8, /device:TPU:0, one launch (start us, length us, event | category | flops | bytes accessed | tf_op | source)
XLA Modules:
  0.0 37.8 jit_solution(377435803073686384)
XLA Ops:
  0.6 1.5 %shard_map.146 = (s32[32,128]{1,0:T(8,128)}, f32[48,1024]{1,0:T(8,128)S(1)}) custom-call(s32[2,1,1,4,8,32]{5,4,3,2,1,0:T(8,128)} %ids.1, f32[48,1024]{1,0:T(8,128)} %refs_0_.1), custom_call_target="tpu_custom_call" | custom-call | flops 1000000 | bytes 1048576 | tf_op jit(solution)/shard_map/pallas_call | solution.py:793
  2.1 7.3 %all-to-all-start = ((s32[32,1,128]{2,1,0:T(1,128)}), s32[32,1,128]{2,1,0:T(1,128)S(1)}, u32[]{:S(2)}, u32[]{:S(2)}) async-start(s32[32,1,128]{2,1,0:T(1,128)} %bitcast.1), calls=%async_computation | async-start | bytes 32768 | tf_op jit(solution)/shard_map/all_to_all | solution.py:834
  9.4 2.0 %shard_map.147 = (f32[576,128]{1,0:T(8,128)S(1)}, f32[472,128]{1,0:T(8,128)S(1)}, f32[2688,128]{1,0:T(8,128)S(1)}, f32[12,256]{1,0:T(8,128)S(1)}, s32[32,128]{1,0:T(8,128)S(1)}, /*index=5*/s32[4,256]{1,0:T(4,128)S(1)}) custom-call(f32[48,1024]{1,0:T(8,128)S(1)} %get-tuple-element.22.cols, f32[3,1024]{1,0:T(4,128)} %far_pos.1, f32[3,1024]{1,0:T(4,128)} %far_scales.1, ...), custom_call_target="tpu_custom_call" | custom-call | flops 1000000 | bytes 1048576 | tf_op jit(solution)/shard_map/pallas_call | solution.py:793
  11.4 5.0 %all-to-all-done = s32[32,1,128]{2,1,0:T(1,128)S(1)} async-done(((s32[32,1,128]{2,1,0:T(1,128)}), s32[32,1,128]{2,1,0:T(1,128)S(1)}, u32[]{:S(2)}, u32[]{:S(2)}) %all-to-all-start) | async-done | bytes 16416 | tf_op jit(solution)/shard_map/all_to_all | solution.py:834
  16.5 0.4 %shard_map.148 = (f32[160,128]{1,0:T(8,128)S(1)}, s32[64,128]{1,0:T(8,128)S(1)}, s32[64,128]{1,0:T(8,128)S(1)}) custom-call(s32[32,128]{1,0:T(8,128)S(1)} %bitcast.17, f32[576,128]{1,0:T(8,128)S(1)} %get-tuple-element.23.rec), custom_call_target="tpu_custom_call" | custom-call | flops 1000000 | bytes 1048576 | tf_op jit(solution)/shard_map/pallas_call | solution.py:793
  16.9 9.3 %all_to_all.15 = f32[32,1,640]{2,1,0:T(1,128)S(1)} all-to-all(f32[32,1,640]{2,1,0:T(1,128)S(1)} %bitcast.16), channel_id=1, replica_groups=mesh['cam'=4,'tile'=8] {'cam','tile'}, dimensions={0} | all-to-all | bytes 163840 | tf_op jit(solution)/shard_map/all_to_all | solution.py:834
  26.2 1.3 %shard_map.149 = f32[160,128]{1,0:T(8,128)S(1)} custom-call(f32[160,128]{1,0:T(8,128)S(1)} %bitcast.14, s32[4,256]{1,0:T(4,128)S(1)} %get-tuple-element.25.lists, f32[12,256]{1,0:T(8,128)S(1)} %get-tuple-element.26.scene, s32[32,128]{1,0:T(8,128)S(1)} %get-tuple-element.27.source), custom_call_target="tpu_custom_call" | custom-call | flops 1000000 | bytes 1048576 | tf_op jit(solution)/shard_map/pallas_call | solution.py:793
  27.5 9.3 %all_to_all.16 = f32[32,1,640]{2,1,0:T(1,128)S(1)} all-to-all(f32[32,1,640]{2,1,0:T(1,128)S(1)} %bitcast.15), channel_id=1, replica_groups=mesh['cam'=4,'tile'=8] {'cam','tile'}, dimensions={0} | all-to-all | bytes 163840 | tf_op jit(solution)/shard_map/all_to_all | solution.py:834
  36.8 1.1 %shard_map.150 = (f32[3,1024]{1,0:T(4,128)}, f32[3,1024]{1,0:T(4,128)}, f32[4,1024]{1,0:T(4,128)}, f32[8,128]{1,0:T(8,128)}, f32[48,1024]{1,0:T(8,128)}) custom-call(f32[160,128]{1,0:T(8,128)S(1)} %bitcast.13, s32[64,128]{1,0:T(8,128)S(1)} %get-tuple-element.28.inverse, s32[64,128]{1,0:T(8,128)S(1)} %get-tuple-element.29.turns, ...), custom_call_target="tpu_custom_call" | custom-call | flops 1000000 | bytes 1048576 | tf_op jit(solution)/shard_map/pallas_call | solution.py:793
Async XLA Ops:
  2.1 14.4 %all-to-all-start = ((s32[32,1,128]{2,1,0:T(1,128)}), s32[32,1,128]{2,1,0:T(1,128)S(1)}, u32[]{:S(2)}, u32[]{:S(2)}) async-start(s32[32,1,128]{2,1,0:T(1,128)} %bitcast.1), calls=%async_computation | async-start | bytes 32768 | tf_op jit(solution)/shard_map/all_to_all | solution.py:834

commit v9 on v7

--- a/solution.py
+++ b/solution.py
@@ -664,6 +664,10 @@
     def at(k):
         return raw[k * rows : (k + 1) * rows, :]
 
+    squares = [jnp.exp(2.0 * at(3 + k)) for k in range(3)]
+    spin, quat, quat_back = spin_of([at(6 + k) for k in range(4)])
+    opacity = 1.0 / (1.0 + jnp.exp(-at(10)))
+
     def fetcher(view):
         p, c = view // cams, view % cams
         slot = inverse[view * rows : (view + 1) * rows, :] - 1
@@ -715,8 +719,6 @@
             send(cols.at[pl.ds(sent, ready - sent), :], far_cols.at[pl.ds(sent, ready - sent), :])
             sent = ready
 
-    squares = [jnp.exp(2.0 * at(3 + k)) for k in range(3)]
-    spin, quat, quat_back = spin_of([at(6 + k) for k in range(4)])
 
     g_point = [jnp.zeros(shape, F32) for _ in range(3)]
     g_cov = [[jnp.zeros(shape, F32) for _ in range(3)] for _ in range(3)]
@@ -763,7 +765,6 @@
     ]
     along = w * g_quat[0] + x * g_quat[1] + y * g_quat[2] + z * g_quat[3]
     g_rots = [(g_quat[k] - quat[k] * along) * quat_back for k in range(4)]
-    opacity = 1.0 / (1.0 + jnp.exp(-at(10)))
     opac[...] = g_opacity * opacity * (1.0 - opacity)
     for k, value in enumerate(g_point + g_scales + g_rots):
         total[k * rows : (k + 1) * rows, :] = value

time: 38.1 us -> 38.1 us (level)
  no operation moved by 1% of the time
where the time goes in v9:
time: 38.1 us; the launch traced here: 37.9 us
  blocking collectives  18.5 us (49%)
  starting transfers between devices  7.3 us (19%)
  Pallas kernels  6.31 us (17%)
  waiting for transfers between devices  5.05 us (13%)
  between operations  0.66 us (2%)
    all_to_all x2, blocking collectives, exchange(): lax.all_to_all(lines, axes, split_axis=0, concat_axis=0, tiled=True)  18.5 us
    all_to_all x1, starting transfers between devices, exchange(): lax.all_to_all(lines, axes, split_axis=0, concat_axis=0, tiled=True)  7.3 us
    pallas_call x5, Pallas kernels, call(): pl.pallas_call(kernel, out_shape=outs, in_specs=in_specs or vmem(len(oper...  6.31 us
    all_to_all x1, waiting for transfers between devices, exchange(): lax.all_to_all(lines, axes, split_axis=0, concat_axis=0, tiled=True)  5.05 us
  transfers between devices with their start and end apart: 1, of which 1 were waited for; matrix products, arithmetic and copies ran while one was open for 0% of the time, Pallas kernels for 5%

profile of v9, /device:TPU:0, one launch (start us, length us, event | category | flops | bytes accessed | tf_op | source)
XLA Modules:
  0.0 37.9 jit_solution(9338084359465293909)
XLA Ops:
  0.6 1.5 %shard_map.146 = (s32[32,128]{1,0:T(8,128)}, f32[48,1024]{1,0:T(8,128)S(1)}) custom-call(s32[2,1,1,4,8,32]{5,4,3,2,1,0:T(8,128)} %ids.1, f32[48,1024]{1,0:T(8,128)} %refs_0_.1), custom_call_target="tpu_custom_call" | custom-call | flops 1000000 | bytes 1048576 | tf_op jit(solution)/shard_map/pallas_call | solution.py:792
  2.1 7.3 %all-to-all-start = ((s32[32,1,128]{2,1,0:T(1,128)}), s32[32,1,128]{2,1,0:T(1,128)S(1)}, u32[]{:S(2)}, u32[]{:S(2)}) async-start(s32[32,1,128]{2,1,0:T(1,128)} %bitcast.1), calls=%async_computation | async-start | bytes 32768 | tf_op jit(solution)/shard_map/all_to_all | solution.py:833
  9.4 2.0 %shard_map.147 = (f32[576,128]{1,0:T(8,128)S(1)}, f32[472,128]{1,0:T(8,128)S(1)}, f32[2688,128]{1,0:T(8,128)S(1)}, f32[12,256]{1,0:T(8,128)S(1)}, s32[32,128]{1,0:T(8,128)S(1)}, /*index=5*/s32[4,256]{1,0:T(4,128)S(1)}) custom-call(f32[48,1024]{1,0:T(8,128)S(1)} %get-tuple-element.22.cols, f32[3,1024]{1,0:T(4,128)} %far_pos.1, f32[3,1024]{1,0:T(4,128)} %far_scales.1, ...), custom_call_target="tpu_custom_call" | custom-call | flops 1000000 | bytes 1048576 | tf_op jit(solution)/shard_map/pallas_call | solution.py:792
  11.4 5.0 %all-to-all-done = s32[32,1,128]{2,1,0:T(1,128)S(1)} async-done(((s32[32,1,128]{2,1,0:T(1,128)}), s32[32,1,128]{2,1,0:T(1,128)S(1)}, u32[]{:S(2)}, u32[]{:S(2)}) %all-to-all-start) | async-done | bytes 16416 | tf_op jit(solution)/shard_map/all_to_all | solution.py:833
  16.5 0.4 %shard_map.148 = (f32[160,128]{1,0:T(8,128)S(1)}, s32[64,128]{1,0:T(8,128)S(1)}, s32[64,128]{1,0:T(8,128)S(1)}) custom-call(s32[32,128]{1,0:T(8,128)S(1)} %bitcast.17, f32[576,128]{1,0:T(8,128)S(1)} %get-tuple-element.23.rec), custom_call_target="tpu_custom_call" | custom-call | flops 1000000 | bytes 1048576 | tf_op jit(solution)/shard_map/pallas_call | solution.py:792
  16.9 9.3 %all_to_all.15 = f32[32,1,640]{2,1,0:T(1,128)S(1)} all-to-all(f32[32,1,640]{2,1,0:T(1,128)S(1)} %bitcast.16), channel_id=1, replica_groups=mesh['cam'=4,'tile'=8] {'cam','tile'}, dimensions={0} | all-to-all | bytes 163840 | tf_op jit(solution)/shard_map/all_to_all | solution.py:833
  26.2 1.3 %shard_map.149 = f32[160,128]{1,0:T(8,128)S(1)} custom-call(f32[160,128]{1,0:T(8,128)S(1)} %bitcast.14, s32[4,256]{1,0:T(4,128)S(1)} %get-tuple-element.25.lists, f32[12,256]{1,0:T(8,128)S(1)} %get-tuple-element.26.scene, s32[32,128]{1,0:T(8,128)S(1)} %get-tuple-element.27.source), custom_call_target="tpu_custom_call" | custom-call | flops 1000000 | bytes 1048576 | tf_op jit(solution)/shard_map/pallas_call | solution.py:792
  27.5 9.3 %all_to_all.16 = f32[32,1,640]{2,1,0:T(1,128)S(1)} all-to-all(f32[32,1,640]{2,1,0:T(1,128)S(1)} %bitcast.15), channel_id=1, replica_groups=mesh['cam'=4,'tile'=8] {'cam','tile'}, dimensions={0} | all-to-all | bytes 163840 | tf_op jit(solution)/shard_map/all_to_all | solution.py:833
  36.8 1.1 %shard_map.150 = (f32[3,1024]{1,0:T(4,128)}, f32[3,1024]{1,0:T(4,128)}, f32[4,1024]{1,0:T(4,128)}, f32[8,128]{1,0:T(8,128)}, f32[48,1024]{1,0:T(8,128)}) custom-call(f32[160,128]{1,0:T(8,128)S(1)} %bitcast.13, s32[64,128]{1,0:T(8,128)S(1)} %get-tuple-element.28.inverse, s32[64,128]{1,0:T(8,128)S(1)} %get-tuple-element.29.turns, ...), custom_call_target="tpu_custom_call" | custom-call | flops 1000000 | bytes 1048576 | tf_op jit(solution)/shard_map/pallas_call | solution.py:792
Async XLA Ops:
  2.1 14.4 %all-to-all-start = ((s32[32,1,128]{2,1,0:T(1,128)}), s32[32,1,128]{2,1,0:T(1,128)S(1)}, u32[]{:S(2)}, u32[]{:S(2)}) async-start(s32[32,1,128]{2,1,0:T(1,128)} %bitcast.1), calls=%async_computation | async-start | bytes 32768 | tf_op jit(solution)/shard_map/all_to_all | solution.py:833
